TPU v7x, 128 devices: a whole 4x4x4 slice. The times are simulated.
128 devices in a mesh: slab: 16 (over z, x_hi, core), loop: 8 (over y, x_lo).
Axes of the slice: x: 4 (x_hi: 2, x_lo: 2; x = x_hi * 2 + x_lo), y: 4, z: 4, core: 2. Of those that a mesh axis runs over, the one named last changes fastest.
Arguments:
- doc_pool: bfloat16 [16, 8, 256, 4096], P('slab', 'loop'), may hold values from -6 to 6
- cand_owner: int32 [16, 8, 8, 1], P('slab', 'loop'), may hold values from 0 to 15; in each aligned block of 8 rows (0 to 7, 8 to 15, ..., all dimensions but the last counted through in order) at most 2 rows name the same one
- cand_row: int32 [16, 8, 8], P('slab', 'loop'), may hold values from 0 to 255
- elements: bfloat16 [16, 8, 2048, 4096], P('slab', 'loop'), may hold values from -6 to 6
- coverage: float32 [16, 8, 2048], P('slab', 'loop'), may hold values from -0.5 to 1.5
- elem_weight: float32 [16, 8, 2048], P('slab', 'loop'), may hold values from 1 to 10
Outputs:
- gains: float32 [16, 8, 8], P('slab', 'loop')
Inputs may be any that keep to these rules, and one draw needn't show every extreme that they name: `cand_owner`: among the candidates of one device, at most 2 name the same owner; some owner is named exactly 2 times.
All inputs are finite; a program needn't handle non-finite values.
Results may differ from a plain program's by a relative error of at most 0.0003.
Values may be sent and summed in bfloat16 or wider, within the bound.
No kernel may reach another device: no remote copies, remote signals or barrier semaphores. Data moves between devices by JAX's collectives and lax.ppermute only.
A program may use at most 128 MiB of HBM per device.

v0:
```python
import jax
import jax.numpy as jnp
from jax import lax
from jax.sharding import PartitionSpec as P


def body(doc_pool, cand_owner, cand_row, elements, coverage, elem_weight):
    slab_count = lax.axis_size("slab")
    loop_count = lax.axis_size("loop")
    share_len = cand_row.shape[2]
    width = doc_pool.shape[3]
    slot_cap = max(2, 2 * share_len // slab_count)
    pool_local = doc_pool.reshape(doc_pool.shape[2], width)
    owner_ids = cand_owner.reshape(share_len)
    row_ids = cand_row.reshape(share_len)
    docs = elements.reshape(elements.shape[2], width)
    cover_local = coverage.reshape(coverage.shape[2])
    weight_local = elem_weight.reshape(elem_weight.shape[2])
    sim_scale = float(width) ** (-0.5)
    element_total = float(docs.shape[0] * slab_count * loop_count)
    positions = jnp.arange(share_len, dtype=jnp.int32)
    same_owner = owner_ids[:, None] == owner_ids[None, :]
    earlier = positions[None, :] < positions[:, None]
    slot_rank = jnp.sum((same_owner & earlier).astype(jnp.int32), axis=1)
    slot_id = owner_ids * slot_cap + slot_rank
    onehot = (
        slot_id[:, None] == jnp.arange(slab_count * slot_cap, dtype=jnp.int32)[None, :]
    ).astype(jnp.int32)
    requests = jnp.sum(onehot * row_ids[:, None], axis=0).reshape(slab_count, slot_cap)
    doc_rows = jnp.take(
        pool_local,
        lax.all_to_all(requests, "slab", split_axis=0, concat_axis=0, tiled=True),
        axis=0,
    )
    fetched = lax.all_to_all(doc_rows, "slab", split_axis=0, concat_axis=0, tiled=True)
    cand_rows = jnp.take(fetched.reshape(slab_count * slot_cap, width), slot_id, axis=0)
    column_rows = lax.all_gather(cand_rows, "slab", axis=0, tiled=True)
    scores = (
        lax.dot_general(
            docs,
            lax.all_gather(column_rows, "loop", axis=0, tiled=True),
            (((1,), (1,)), ((), ())),
            preferred_element_type=jnp.float32,
        )
        * sim_scale
    )
    running = (
        jnp.sum(weight_local[:, None] * jnp.maximum(scores - cover_local[:, None], 0.0), axis=0)
        / element_total
    )
    terms = (
        running.reshape(loop_count, slab_count, share_len)
        .transpose(1, 0, 2)
        .reshape(slab_count * loop_count, share_len)
    )
    summed = lax.psum_scatter(terms, ("slab", "loop"), scatter_dimension=0, tiled=True)
    return summed.reshape(1, 1, share_len)


def solution(mesh):
    placed = (
        P("slab", "loop", None, None),
        P("slab", "loop", None, None),
        P("slab", "loop", None),
        P("slab", "loop", None, None),
        P("slab", "loop", None),
        P("slab", "loop", None),
    )
    return jax.shard_map(
        body, mesh=mesh, in_specs=placed, out_specs=P("slab", "loop", None), check_vma=False
    )
```

profile of v0, /device:TPU:0, one launch (start us, length us, event | category | flops | bytes accessed | tf_op | source)
XLA Modules:
  0.0 349.3 jit_solution(17800143249456935249)
XLA Ops:
  6.5 1.0 convert_reduce_fusion
  7.5 0.7 compare_and_fusion.1
  8.2 0.7 select_reduce_fusion
  8.9 0.1 all_to_all.13
  9.0 15.3 %all_to_all.20 = s32[16,1,2]{2,1,0:T(1,128)S(1)} all-to-all(s32[16,1,2]{2,1,0:T(1,128)S(1)} %bitcast.36), channel_id=1, replica_groups=mesh['slab'=16,'loop'=8] {'slab'}, dimensions={0} | all-to-all | bytes 256 | tf_op jit(solution)/shard_map/all_to_all | solution.py:32
  24.4 0.1 copy.35
  24.5 0.1 reshape.113
  24.6 0.7 gather_fusion
  25.4 0.2 reshape.112
  25.5 0.1 copy.33
  25.6 1.0 broadcast_select_fusion
  26.6 3.5 %all-to-all-start.1 = ((bf16[16,2,4096]{2,1,0:T(2,128)(2,1)}), bf16[16,2,4096]{2,1,0:T(2,128)(2,1)S(1)}, u32[]{:S(2)}, u32[]{:S(2)}) async-start(bf16[16,2,4096]{2,1,0:T(2,128)(2,1)} %broadcast_select_fusion), calls=%async_computation.1 | async-start | bytes 524288 | tf_op jit(solution)/shard_map/all_to_all | solution.py:35
  30.2 0.7 fusion.5
  30.9 8.8 %all-to-all-done.1 = bf16[16,2,4096]{2,1,0:T(2,128)(2,1)S(1)} async-done(((bf16[16,2,4096]{2,1,0:T(2,128)(2,1)}), bf16[16,2,4096]{2,1,0:T(2,128)(2,1)S(1)}, u32[]{:S(2)}, u32[]{:S(2)}) %all-to-all-start.1) | async-done | bytes 262176 | tf_op jit(solution)/shard_map/all_to_all | solution.py:35
  39.7 0.1 reshape.107
  39.8 0.6 gather_fusion.1
  40.4 0.7 broadcast_select_fusion.1
  41.2 41.9 %all-gather.3.cloned.1.call-done = bf16[128,4096]{1,0:T(8,128)(2,1)} async-done(((bf16[8,4096]{1,0:T(8,128)(2,1)}), bf16[128,4096]{1,0:T(8,128)(2,1)}) %all-gather.3.cloned.1.call-update) | async-done | bytes 1048592 | tf_op jit(solution)/shard_map/all_gather | solution.py:37
  83.1 168.7 %all-gather.5.cloned.1.call-done = bf16[1024,4096]{1,0:T(8,128)(2,1)} async-done(((bf16[128,4096]{1,0:T(8,128)(2,1)}), bf16[1024,4096]{1,0:T(8,128)(2,1)}) %all-gather.5.cloned.1.call-update) | async-done | bytes 8388624 | tf_op jit(solution)/shard_map/all_gather | solution.py:41
  251.8 23.5 %multiply_reduce_fusion = f32[1024]{0:T(1024)S(1)} fusion(bf16[1024,4096]{1,0:T(8,128)(2,1)} %all-gather.5.cloned.1.call-done, bf16[1,1,2048,4096]{3,2,1,0:T(8,128)(2,1)} %param.9, f32[2048]{0:T(1024)} %bitcast.38, f32[2048]{0:T(1024)} %bitcast.39), kind=kOutput, calls=%fused_computation.4 | convolution fusion | flops 17190354944 | bytes 25186304 | tf_op jit(solution)/shard_map/dot_general | solution.py:39
  275.4 0.1 copy.36
  275.5 0.1 reshape.109
  275.6 66.2 %all-reduce = f32[128,8]{0,1:T(8,128)S(1)} all-reduce(f32[128,8]{0,1:T(8,128)S(1)} %reshape.109), channel_id=2, replica_groups=mesh['slab'=16,'loop'=8] {'slab','loop'}, use_global_device_ids=true, to_apply=%region_3.4.clone | all-reduce | flops 1024 | bytes 8192
  341.7 0.7 dynamic-slice_reduce_fusion
  (13 shorter events, 0.3 us)
Async XLA Ops:
  6.5 18.1 %copy-start = (bf16[1,1,256,4096]{3,2,1,0:T(8,128)(2,1)S(1)}, bf16[1,1,256,4096]{3,2,1,0:T(8,128)(2,1)}, u32[]{:S(2)}) copy-start(bf16[1,1,256,4096]{3,2,1,0:T(8,128)(2,1)} %param.6) | copy-start | bytes 6291460
  26.6 13.1 %all-to-all-start.1 = ((bf16[16,2,4096]{2,1,0:T(2,128)(2,1)}), bf16[16,2,4096]{2,1,0:T(2,128)(2,1)S(1)}, u32[]{:S(2)}, u32[]{:S(2)}) async-start(bf16[16,2,4096]{2,1,0:T(2,128)(2,1)} %broadcast_select_fusion), calls=%async_computation.1 | async-start | bytes 524288 | tf_op jit(solution)/shard_map/all_to_all | solution.py:35
  30.2 52.9 %all-gather.3.cloned.1.call-start = ((), (), s32[]{:S(2)}) async-start(), calls=%async_computation.2 | async-start | bytes 1114112 | tf_op jit(solution)/shard_map/all_gather | solution.py:37
  41.1 210.6 %all-gather.5.cloned.1.call-start = ((), (), s32[]{:S(2)}) async-start(), calls=%async_computation.3 | async-start | bytes 9437184 | tf_op jit(solution)/shard_map/all_gather | solution.py:41
Sparse Core Ops, SparseCore 0:
  41.2 41.7 all-gather.2
  84.7 167.0 all-gather.4
where the time goes:
time: 350 us; the launch traced here: 349 us
  waiting for transfers between devices  219 us (63%)
  blocking collectives  81.5 us (23%)
  matrix products  23.5 us (7%)
  between operations  13.5 us (4%)
  other arithmetic  4.8 us (1%)
  starting transfers between devices  3.61 us (1%)
    all_gather x1, waiting for transfers between devices, body(): lax.all_gather(column_rows, 'loop', axis=0, tiled=True)  169 us
    unnamed x1, blocking collectives  66.2 us
    all_gather x1, waiting for transfers between devices, body(): column_rows = lax.all_gather(cand_rows, 'slab', axis=0, tiled=True)  41.9 us
    dot_general x1, matrix products, body(): lax.dot_general(docs, lax.all_gather(column_rows, 'loop', axis=0, tiled=T...  23.5 us
    all_to_all x1, blocking collectives, body(): lax.all_to_all(requests, 'slab', split_axis=0, concat_axis=0, tiled=True)  15.3 us
    all_to_all x1, waiting for transfers between devices, body(): lax.all_to_all(doc_rows, 'slab', split_axis=0, concat_axis=0, tiled=True)  8.8 us
  transfers between devices with their start and end apart: 3, of which 3 were waited for; matrix products, arithmetic and copies ran while one was open for 0% of the time, Pallas kernels for 0%

commit v1 on v0

v1 whole, which is shorter than its diff:
```python
import functools

import jax
import jax.numpy as jnp
from jax import lax
from jax.experimental import pallas as pl
from jax.experimental.pallas import tpu as pltpu
from jax.sharding import PartitionSpec as P

AXES = ("slab", "loop")
RING = 4
TILE = 512


def place(index):
    slab, loop = divmod(index, 8)
    z, rest = divmod(slab, 4)
    hi, core = divmod(rest, 2)
    y, lo = divmod(loop, 2)
    return z, hi * 2 + lo, y, core


def index_of(z, x, y, core):
    return ((z * 2 + x // 2) * 2 + core) * 8 + y * 2 + x % 2


def moves(dz=0, dx=0, dy=0, dc=0):
    pairs = []
    for source in range(128):
        z, x, y, core = place(source)
        pairs.append((source, index_of((z + dz) % RING, (x + dx) % RING, (y + dy) % RING, core ^ dc)))
    return pairs


def send(value, **step):
    return lax.ppermute(value, AXES, moves(**step))


def add_terms(cand, docs, cw, out_ref, start, doc_at):
    scores = lax.dot_general(
        cand[...], docs[pl.ds(start, TILE), :], (((1,), (1,)), ((), ())), preferred_element_type=jnp.float32
    )
    cover = cw[0:1, pl.ds(doc_at, TILE)]
    weight = cw[1:2, pl.ds(doc_at, TILE)]
    term = weight * jnp.maximum(scores - cover, 0.0)
    total = out_ref[...]
    for j in range(TILE // 128):
        total = total + term[:, j * 128 : (j + 1) * 128]
    out_ref[...] = total


def pack(pieces, cand):
    at = 0
    for piece in pieces:
        rows = piece.shape[0]
        cand[at : at + rows, :] = piece[...]
        at += rows


def first_kernel(count, *refs):
    pieces = refs[:count]
    own_hbm, sib_hbm, own_cw, sib_cw, out_ref, own_docs, sib_docs, cand, arrived = refs[count:]
    steps = own_hbm.shape[0] // TILE

    def copy(i, source, target, base):
        rows = pl.ds(pl.multiple_of(i * TILE, TILE), TILE)
        return pltpu.make_async_copy(source.at[rows], target.at[rows], arrived.at[base + i])

    for i in range(steps):
        copy(i, own_hbm, own_docs, 0).start()
    for i in range(steps):
        copy(i, sib_hbm, sib_docs, steps).start()
    pack(pieces, cand)
    out_ref[...] = jnp.zeros_like(out_ref)
    for source, docs, cw, base in ((own_hbm, own_docs, own_cw, 0), (sib_hbm, sib_docs, sib_cw, steps)):

        def step(i, carry, source=source, docs=docs, cw=cw, base=base):
            copy(i, source, docs, base).wait()
            start = pl.multiple_of(i * TILE, TILE)
            add_terms(cand, docs, cw, out_ref, start, start)
            return carry

        lax.fori_loop(0, steps, step, 0)


def later_kernel(count, *refs):
    pieces = refs[:count]
    own_docs, sib_docs, own_cw, sib_cw, out_ref, cand = refs[count:]
    pack(pieces, cand)
    out_ref[...] = jnp.zeros_like(out_ref)
    for docs, cw in ((own_docs, own_cw), (sib_docs, sib_cw)):

        def step(i, carry, docs=docs, cw=cw):
            start = pl.multiple_of(i * TILE, TILE)
            add_terms(cand, docs, cw, out_ref, start, start)
            return carry

        lax.fori_loop(0, docs.shape[0] // TILE, step, 0)


def gains_of(pieces, own_docs, sib_docs, own_cw, sib_cw, name, first=False):
    count = len(pieces)
    rows, width = sum(p.shape[0] for p in pieces), own_docs.shape[1]
    docs = own_docs.shape[0] + sib_docs.shape[0]
    in_vmem = pl.BlockSpec(memory_space=pltpu.VMEM)
    in_hbm = pl.BlockSpec(memory_space=pltpu.HBM)
    out_shape = [jax.ShapeDtypeStruct((rows, 128), jnp.float32)]
    scratch = [pltpu.VMEM((rows, width), jnp.bfloat16)]
    if first:
        out_shape += [pltpu.VMEM(own_docs.shape, own_docs.dtype), pltpu.VMEM(sib_docs.shape, sib_docs.dtype)]
        scratch += [pltpu.SemaphoreType.DMA((docs // TILE,))]
    return pl.pallas_call(
        functools.partial(first_kernel if first else later_kernel, count),
        in_specs=[in_vmem] * count + [in_hbm if first else in_vmem] * 2 + [in_vmem] * 2,
        out_specs=[in_vmem] * len(out_shape),
        out_shape=out_shape,
        scratch_shapes=scratch,
        compiler_params=pltpu.CompilerParams(vmem_limit_bytes=8 * 2**20),
        cost_estimate=pl.CostEstimate(
            flops=2 * docs * rows * width, bytes_accessed=docs * width * 2 if first else 0, transcendentals=0
        ),
        name=name,
    )(*pieces, own_docs, sib_docs, own_cw, sib_cw)


def body(doc_pool, cand_owner, cand_row, elements, coverage, elem_weight):
    share_len = cand_row.shape[2]
    width = doc_pool.shape[3]
    slab_count = 16
    slot_cap = 2
    pool_local = doc_pool.reshape(doc_pool.shape[2], width)
    owner_ids = cand_owner.reshape(share_len)
    row_ids = cand_row.reshape(share_len)
    docs = elements.reshape(elements.shape[2], width)
    scale_up = float(width) ** 0.5
    element_total = float(docs.shape[0] * 128)
    cw = jnp.stack(
        [coverage.reshape(-1) * scale_up, elem_weight.reshape(-1) * (1.0 / (scale_up * element_total))]
    )
    sib_docs = send(docs, dc=1)
    sib_cw = send(cw, dc=1)

    positions = jnp.arange(share_len, dtype=jnp.int32)
    same_owner = owner_ids[:, None] == owner_ids[None, :]
    earlier = positions[None, :] < positions[:, None]
    slot_rank = jnp.sum((same_owner & earlier).astype(jnp.int32), axis=1)
    slot_id = owner_ids * slot_cap + slot_rank
    onehot = (
        slot_id[:, None] == jnp.arange(slab_count * slot_cap, dtype=jnp.int32)[None, :]
    ).astype(jnp.int32)
    requests = jnp.sum(onehot * row_ids[:, None], axis=0).reshape(slab_count, slot_cap)
    asked = lax.all_to_all(requests, "slab", split_axis=0, concat_axis=0, tiled=True)
    doc_rows = pool_local.at[asked.reshape(-1)].get(mode="promise_in_bounds")
    fetched = lax.all_to_all(
        doc_rows.reshape(slab_count, slot_cap, width), "slab", split_axis=0, concat_axis=0, tiled=True
    )
    own = fetched.reshape(slab_count * slot_cap, width).at[slot_id].get(mode="promise_in_bounds")

    z3, z1, z2 = send(own, dz=1), send(own, dz=-1), send(own, dz=2)
    part_a = jnp.concatenate([own, z1], axis=0)
    part_b = jnp.concatenate([z2, z3], axis=0)
    a3, a1, a2 = send(part_a, dx=1), send(part_a, dx=-1), send(part_a, dx=2)
    b3, b1, b2 = send(part_b, dy=1), send(part_b, dy=-1), send(part_b, dy=2)
    block_a = jnp.concatenate([part_a, a1, a2, a3], axis=0)
    block_b = jnp.concatenate([part_b, b1, b2, b3], axis=0)
    aa3, aa1 = send(block_a, dy=1), send(block_a, dy=-1)
    bb3, bb1 = send(block_b, dx=1), send(block_b, dx=-1)
    g0, own_here, sib_here = gains_of(
        [block_a, block_b], docs, sib_docs, cw, sib_cw, "gains_near", first=True
    )
    far_a, far_b, aa1, aa3, bb1, bb3 = lax.optimization_barrier((block_a, block_b, aa1, aa3, bb1, bb3))
    aa2, bb2 = send(far_a, dy=2), send(far_b, dx=2)
    (g1,) = gains_of([aa1, aa3, bb1, bb3], own_here, sib_here, cw, sib_cw, "gains_next")
    cw, g1 = lax.optimization_barrier((cw, g1))
    (g2,) = gains_of([aa2, bb2], own_here, sib_here, cw, sib_cw, "gains_far")
    g0, g1, g2 = jnp.sum(g0, axis=1), jnp.sum(g1, axis=1), jnp.sum(g2, axis=1)
    n = block_a.shape[0]
    gain_a = jnp.stack([g0[:n], g1[:n], g2[:n], g1[n : 2 * n]])
    gain_b = jnp.stack([g0[n:], g1[2 * n : 3 * n], g2[n:], g1[3 * n :]])
    gain_a = gain_a.reshape(RING, RING, 2, share_len)
    gain_b = gain_b.reshape(RING, RING, 2, share_len).transpose(1, 0, 2, 3)
    gains = jnp.concatenate([gain_a, gain_b], axis=2).reshape(64, share_len)

    slab, loop = lax.axis_index("slab"), lax.axis_index("loop")
    my_z, my_x, my_y = slab >> 2, (slab & 2) + (loop & 1), loop >> 1
    to = jnp.arange(64, dtype=jnp.int32)
    to_z, to_x, to_y = to >> 4, ((to >> 2) & 2) + (to & 1), (to >> 1) & 3
    rel = ((to_y - my_y) & 3) * 16 + ((to_x - my_x) & 3) * 4 + ((to_z - my_z) & 3)
    pick = rel[:, None] == jnp.arange(64, dtype=jnp.int32)[None, :]
    terms = jnp.sum(jnp.where(pick[:, :, None], gains[None, :, :], 0.0), axis=1)
    groups = [[i for i in range(128) if place(i)[3] == core] for core in range(2)]
    terms = lax.all_to_all(terms, AXES, split_axis=0, concat_axis=0, tiled=True, axis_index_groups=groups)
    return jnp.sum(terms, axis=0).reshape(1, 1, share_len)


def solution(mesh):
    placed = (
        P("slab", "loop", None, None),
        P("slab", "loop", None, None),
        P("slab", "loop", None),
        P("slab", "loop", None, None),
        P("slab", "loop", None),
        P("slab", "loop", None),
    )
    return jax.shard_map(
        body, mesh=mesh, in_specs=placed, out_specs=P("slab", "loop", None), check_vma=False
    )
```

time: 350 us -> 150 us (0.43)
  waiting for transfers between devices: 219 us -> 44 us
  blocking collectives: 81.5 us -> 17.8 us
  Pallas kernels: 0 us -> 37.2 us
  starting transfers between devices: 3.61 us -> 39.9 us
  matrix products: 23.5 us -> 0 us
  between operations: 13.5 us -> 0.24 us
    all_gather x2 -> x0, waiting for transfers between devices: 211 us -> none  [the longest x1 169 us: body(): lax.all_gather(column_rows, 'loop', axis=0, tiled=True)]
    unnamed x1 -> x0, blocking collectives: 66.2 us -> none
    pallas_call x0 -> x3, Pallas kernels: none -> 37.2 us  [gains_of(): pl.pallas_call(functools.partial(first_kernel if first else later_kernel,...]
    ppermute x0 -> x17, starting transfers between devices: none -> 24.1 us  [send(): return lax.ppermute(value, AXES, moves(**step))]
    dot_general x1 -> x0, matrix products: 23.5 us -> none  [body(): lax.dot_general(docs, lax.all_gather(column_rows, 'loop', axis=0, tiled=T...]
    ppermute x0 -> x17, waiting for transfers between devices: none -> 21.6 us  [send(): return lax.ppermute(value, AXES, moves(**step))]
    all_to_all x1 -> x2, waiting for transfers between devices: 8.8 us -> 22.4 us  [the longest x1 13.5 us: body(): lax.all_to_all(requests, 'slab', split_axis=0, concat_axis=0, tiled=True)]
    all_to_all x1 -> x2, starting transfers between devices: 3.53 us -> 15.8 us  [the longest x1 8 us: body(): lax.all_to_all(requests, 'slab', split_axis=0, concat_axis=0, tiled=True)]
  transfers between devices with their start and end apart: 3 -> 19, of which waited for: 3 -> 13; matrix products, arithmetic and copies ran while one was open for 0% -> 5% of each run, Pallas kernels for 0% -> 17%
where the time goes in v1:
time: 150 us
  waiting for transfers between devices  44 us (29%)
  starting transfers between devices  39.9 us (27%)
  Pallas kernels  37.2 us (25%)
  blocking collectives  17.8 us (12%)
  other arithmetic  5.72 us (4%)
  local copies, waits for them, and re-layouts  4.63 us (3%)
    pallas_call x3, Pallas kernels, gains_of(): pl.pallas_call(functools.partial(first_kernel if first else later_kernel,...  37.2 us
    ppermute x17, starting transfers between devices, send(): return lax.ppermute(value, AXES, moves(**step))  24.1 us
    ppermute x17, waiting for transfers between devices, send(): return lax.ppermute(value, AXES, moves(**step))  21.6 us
    all_to_all x1, blocking collectives, body(): lax.all_to_all(terms, AXES, split_axis=0, concat_axis=0, tiled=True, axis...  17.8 us
    all_to_all x1, waiting for transfers between devices, body(): lax.all_to_all(requests, 'slab', split_axis=0, concat_axis=0, tiled=True)  13.5 us
    all_to_all x1, waiting for transfers between devices, body(): lax.all_to_all(doc_rows.reshape(slab_count, slot_cap, width), 'slab', spl...  8.88 us
    all_to_all x1, starting transfers between devices, body(): lax.all_to_all(requests, 'slab', split_axis=0, concat_axis=0, tiled=True)  8 us
    all_to_all x1, starting transfers between devices, body(): lax.all_to_all(doc_rows.reshape(slab_count, slot_cap, width), 'slab', spl...  7.81 us
  transfers between devices with their start and end apart: 19, of which 13 were waited for; matrix products, arithmetic and copies ran while one was open for 5% of the time, Pallas kernels for 17%

profile of v1, /device:TPU:0, one launch (start us, length us, event | category | flops | bytes accessed | tf_op | source)
XLA Modules:
  0.0 149.5 jit_solution(16630635921131129633)
XLA Ops:
  0.0 1.0 convert_reduce_fusion
  3.1 8.0 %all-to-all-start = ((s32[16,1,2]{2,1,0:T(1,128)}), s32[16,1,2]{2,1,0:T(1,128)S(1)}, u32[]{:S(2)}, u32[]{:S(2)}) async-start(s32[16,1,2]{2,1,0:T(1,128)} %bitcast.3), calls=%async_computation | async-start | bytes 16384 | tf_op jit(solution)/shard_map/all_to_all | solution.py:152
  11.8 13.5 %all-to-all-done = s32[16,1,2]{2,1,0:T(1,128)S(1)} async-done(((s32[16,1,2]{2,1,0:T(1,128)}), s32[16,1,2]{2,1,0:T(1,128)S(1)}, u32[]{:S(2)}, u32[]{:S(2)}) %all-to-all-start) | async-done | bytes 160 | tf_op jit(solution)/shard_map/all_to_all | solution.py:152
  28.2 7.8 %all-to-all-start.1 = ((bf16[16,2,4096]{2,1,0:T(2,128)(2,1)}), bf16[16,2,4096]{2,1,0:T(2,128)(2,1)S(1)}, u32[]{:S(2)}, u32[]{:S(2)}) async-start(bf16[16,2,4096]{2,1,0:T(2,128)(2,1)} %reshape.231), calls=%async_computation.1 | async-start | bytes 524288 | tf_op jit(solution)/shard_map/all_to_all | solution.py:154
  36.7 8.9 %all-to-all-done.1 = bf16[16,2,4096]{2,1,0:T(2,128)(2,1)S(1)} async-done(((bf16[16,2,4096]{2,1,0:T(2,128)(2,1)}), bf16[16,2,4096]{2,1,0:T(2,128)(2,1)S(1)}, u32[]{:S(2)}, u32[]{:S(2)}) %all-to-all-start.1) | async-done | bytes 262176 | tf_op jit(solution)/shard_map/all_to_all | solution.py:154
  46.3 0.9 collective-permute-start.4
  48.1 2.4 %collective-permute-start = (bf16[8,4096]{1,0:T(8,128)(2,1)S(1)}, bf16[8,4096]{1,0:T(8,128)(2,1)S(1)}, u32[]{:S(2)}, u32[]{:S(2)}) collective-permute-start(bf16[8,4096]{1,0:T(8,128)(2,1)S(1)} %gather_fusion.1), channel_id=1, source_target_pairs={{0,96},{1,97},{2,98},{3,99},{4,100},{5,101},{6,102},{7,103},{8,104... | collective-permute-start | bytes 196616 | tf_op jit(solution)/shard_map/ppermute | solution.py:36
  50.6 1.8 %collective-permute-done.4 = bf16[8,4096]{1,0:T(8,128)(2,1)S(1)} collective-permute-done((bf16[8,4096]{1,0:T(8,128)(2,1)S(1)}, bf16[8,4096]{1,0:T(8,128)(2,1)S(1)}, u32[]{:S(2)}, u32[]{:S(2)}) %collective-permute-start.4) | collective-permute-done | bytes 65568 | tf_op jit(solution)/shard_map/ppermute | solution.py:36
  53.0 3.1 %collective-permute-start.6 = (bf16[16,4096]{1,0:T(8,128)(2,1)S(1)}, bf16[16,4096]{1,0:T(8,128)(2,1)S(1)}, u32[]{:S(2)}, u32[]{:S(2)}) collective-permute-start(bf16[16,4096]{1,0:T(8,128)(2,1)S(1)} %get-tuple-element.27), channel_id=1, source_target_pairs={{0,6},{1,7},{2,0},{3,1},{4,2},{5,3},{6,4},{7,5},{8,14},{9,15},{10,... | collective-permute-start | bytes 393224 | tf_op jit(solution)/shard_map/ppermute | solution.py:36
  56.7 1.0 collective-permute-start.8
  58.6 2.2 %collective-permute-done.6 = bf16[16,4096]{1,0:T(8,128)(2,1)S(1)} collective-permute-done((bf16[16,4096]{1,0:T(8,128)(2,1)S(1)}, bf16[16,4096]{1,0:T(8,128)(2,1)S(1)}, u32[]{:S(2)}, u32[]{:S(2)}) %collective-permute-start.6) | collective-permute-done | bytes 131104 | tf_op jit(solution)/shard_map/ppermute | solution.py:36
  60.8 1.9 %collective-permute-start.2 = (bf16[16,4096]{1,0:T(8,128)(2,1)S(1)}, bf16[16,4096]{1,0:T(8,128)(2,1)S(1)}, u32[]{:S(2)}, u32[]{:S(2)}) collective-permute-start(bf16[16,4096]{1,0:T(8,128)(2,1)S(1)} %get-tuple-element.31), channel_id=1, source_target_pairs={{0,16},{1,17},{2,18},{3,19},{4,20},{5,21},{6,22},{7,23},{8,24},{9,... | collective-permute-start | bytes 393224 | tf_op jit(solution)/shard_map/ppermute | solution.py:36
  64.4 2.0 %collective-permute-start.13 = (bf16[64,4096]{1,0:T(8,128)(2,1)S(1)}, bf16[64,4096]{1,0:T(8,128)(2,1)S(1)}, u32[]{:S(2)}, u32[]{:S(2)}) collective-permute-start(bf16[64,4096]{1,0:T(8,128)(2,1)S(1)} %constant_dynamic-update-slice_fusion.9.refs_1_), channel_id=1, source_target_pairs={{0,17},{1,0},{2,19},{3,2},{4,21},{5,4},{6,23},{7,6},{8,25},{9,8},{... | collective-permute-start | bytes 1572872 | tf_op jit(solution)/shard_map/ppermute | solution.py:36
  67.4 2.1 %collective-permute-done.3 = bf16[16,4096]{1,0:T(8,128)(2,1)S(1)} collective-permute-done((bf16[16,4096]{1,0:T(8,128)(2,1)S(1)}, bf16[16,4096]{1,0:T(8,128)(2,1)S(1)}, u32[]{:S(2)}, u32[]{:S(2)}) %collective-permute-start.3) | collective-permute-done | bytes 131104 | tf_op jit(solution)/shard_map/ppermute | solution.py:36
  69.5 4.8 %collective-permute-start.11 = (bf16[64,4096]{1,0:T(8,128)(2,1)S(1)}, bf16[64,4096]{1,0:T(8,128)(2,1)S(1)}, u32[]{:S(2)}, u32[]{:S(2)}) collective-permute-start(bf16[64,4096]{1,0:T(8,128)(2,1)S(1)} %constant_dynamic-update-slice_fusion.2.refs_0_), channel_id=1, source_target_pairs={{0,6},{1,7},{2,0},{3,1},{4,2},{5,3},{6,4},{7,5},{8,14},{9,15},{10,... | collective-permute-start | bytes 1572872 | tf_op jit(solution)/shard_map/ppermute | solution.py:36
  74.3 3.1 %collective-permute-done.13.refs_2_ = bf16[64,4096]{1,0:T(8,128)(2,1)S(1)} collective-permute-done((bf16[64,4096]{1,0:T(8,128)(2,1)S(1)}, bf16[64,4096]{1,0:T(8,128)(2,1)S(1)}, u32[]{:S(2)}, u32[]{:S(2)}) %collective-permute-start.13) | collective-permute-done | bytes 524320 | tf_op jit(solution)/shard_map/ppermute | solution.py:36
  77.5 3.3 %collective-permute-done.14.refs_3_ = bf16[64,4096]{1,0:T(8,128)(2,1)S(1)} collective-permute-done((bf16[64,4096]{1,0:T(8,128)(2,1)S(1)}, bf16[64,4096]{1,0:T(8,128)(2,1)S(1)}, u32[]{:S(2)}, u32[]{:S(2)}) %collective-permute-start.14) | collective-permute-done | bytes 524320 | tf_op jit(solution)/shard_map/ppermute | solution.py:36
  80.8 3.2 %collective-permute-done.11.refs_0_ = bf16[64,4096]{1,0:T(8,128)(2,1)S(1)} collective-permute-done((bf16[64,4096]{1,0:T(8,128)(2,1)S(1)}, bf16[64,4096]{1,0:T(8,128)(2,1)S(1)}, u32[]{:S(2)}, u32[]{:S(2)}) %collective-permute-start.11) | collective-permute-done | bytes 524320 | tf_op jit(solution)/shard_map/ppermute | solution.py:36
  83.9 3.4 %collective-permute-done.12.refs_1_ = bf16[64,4096]{1,0:T(8,128)(2,1)S(1)} collective-permute-done((bf16[64,4096]{1,0:T(8,128)(2,1)S(1)}, bf16[64,4096]{1,0:T(8,128)(2,1)S(1)}, u32[]{:S(2)}, u32[]{:S(2)}) %collective-permute-start.12) | collective-permute-done | bytes 524320 | tf_op jit(solution)/shard_map/ppermute | solution.py:36
  87.4 4.9 %collective-permute-start.16 = (bf16[64,4096]{1,0:T(8,128)(2,1)S(1)}, bf16[64,4096]{1,0:T(8,128)(2,1)S(1)}, u32[]{:S(2)}, u32[]{:S(2)}) collective-permute-start(bf16[64,4096]{1,0:T(8,128)(2,1)S(1)} %constant_dynamic-update-slice_fusion.9.refs_1_), channel_id=1, source_target_pairs={{0,16},{1,17},{2,18},{3,19},{4,20},{5,21},{6,22},{7,23},{8,24},{9,... | collective-permute-start | bytes 1572872 | tf_op jit(solution)/shard_map/ppermute | solution.py:36
  92.3 14.5 %gains_near.1 = (f32[128,128]{1,0:T(8,128)S(1)}, bf16[2048,4096]{1,0:T(8,128)(2,1)S(1)}, bf16[2048,4096]{1,0:T(8,128)(2,1)S(1)}) custom-call(bf16[64,4096]{1,0:T(8,128)(2,1)S(1)} %constant_dynamic-update-slice_fusion.2.refs_0_, bf16[64,4096]{1,0:T(8,128)(2,1)S(1)} %constant_dynamic-update-slice_fusion.9.refs_1_, bf16[2048,4096]{1,0:T(8,128)(2,1)} %bitcast.33, ...), custom_call_target="tpu_custom_call" | custom-call | flops 4294967296 | bytes 33554432 | tf_op jit(solution)/shard_map/gains_near/pallas_call | solution.py:112
  106.8 10.4 %gains_next.1 = f32[256,128]{1,0:T(8,128)S(1)} custom-call(bf16[64,4096]{1,0:T(8,128)(2,1)S(1)} %collective-permute-done.11.refs_0_, bf16[64,4096]{1,0:T(8,128)(2,1)S(1)} %collective-permute-done.12.refs_1_, bf16[64,4096]{1,0:T(8,128)(2,1)S(1)} %collective-permute-done.13.refs_2_, bf16[64,4096]{1,0:T(8,128)(2,1)S(1)} %collective-permute-done.14.refs_3_, ...), custom_call_target="tpu_custom_call" | custom-call | flops 8589934592 | tf_op jit(solution)/shard_map/gains_next/pallas_call | solution.py:112
  117.3 12.3 %gains_far.1 = f32[128,128]{1,0:T(8,128)S(1)} custom-call(bf16[64,4096]{1,0:T(8,128)(2,1)S(1)} %collective-permute-done.15.refs_0_, bf16[64,4096]{1,0:T(8,128)(2,1)S(1)} %collective-permute-done.16.refs_1_, bf16[2048,4096]{1,0:T(8,128)(2,1)S(1)} %get-tuple-element.21.refs_4_.refs_2_, bf16[2048,4096]{1,0:T(8,128)(2,1)S(1)} %get-tuple-element.22.refs_5_.refs_3_, ...), custom_call_target="tpu_custom_call" | custom-call | flops 4294967296 | tf_op jit(solution)/shard_map/gains_far/pallas_call | solution.py:112
  131.1 17.8 %all_to_all.23 = f32[64,1,8]{2,1,0:T(1,128)S(1)} all-to-all(f32[64,1,8]{2,1,0:T(1,128)S(1)} %bitcast.35), channel_id=1, replica_groups={{0,1,2,3,4,5,6,7,16,17,18,19,20,21,22,23,32,33,34,35,36,37,38,39,48,49,..., dimensions={0} | all-to-all | bytes 4096 | tf_op jit(solution)/shard_map/all_to_all | solution.py:192
  (70 shorter events, 15.0 us)
Async XLA Ops:
  0.0 26.6 %copy-start = (bf16[1,1,256,4096]{3,2,1,0:T(8,128)(2,1)S(1)}, bf16[1,1,256,4096]{3,2,1,0:T(8,128)(2,1)}, u32[]{:S(2)}) copy-start(bf16[1,1,256,4096]{3,2,1,0:T(8,128)(2,1)} %param.6) | copy-start | bytes 6291460
  0.0 92.3 %collective-permute-start.9 = (bf16[2048,4096]{1,0:T(8,128)(2,1)}, bf16[2048,4096]{1,0:T(8,128)(2,1)}, u32[]{:S(2)}, u32[]{:S(2)}) collective-permute-start(bf16[2048,4096]{1,0:T(8,128)(2,1)} %bitcast.32), channel_id=1, source_target_pairs={{0,8},{1,9},{2,10},{3,11},{4,12},{5,13},{6,14},{7,15},{8,0},{9,1},... | collective-permute-start | bytes 50331656 | tf_op jit(solution)/shard_map/ppermute | solution.py:36
  3.1 22.2 %all-to-all-start = ((s32[16,1,2]{2,1,0:T(1,128)}), s32[16,1,2]{2,1,0:T(1,128)S(1)}, u32[]{:S(2)}, u32[]{:S(2)}) async-start(s32[16,1,2]{2,1,0:T(1,128)} %bitcast.3), calls=%async_computation | async-start | bytes 16384 | tf_op jit(solution)/shard_map/all_to_all | solution.py:152
  28.2 17.4 %all-to-all-start.1 = ((bf16[16,2,4096]{2,1,0:T(2,128)(2,1)}), bf16[16,2,4096]{2,1,0:T(2,128)(2,1)S(1)}, u32[]{:S(2)}, u32[]{:S(2)}) async-start(bf16[16,2,4096]{2,1,0:T(2,128)(2,1)} %reshape.231), calls=%async_computation.1 | async-start | bytes 524288 | tf_op jit(solution)/shard_map/all_to_all | solution.py:154
  46.3 6.0 %collective-permute-start.4 = (bf16[8,4096]{1,0:T(8,128)(2,1)S(1)}, bf16[8,4096]{1,0:T(8,128)(2,1)S(1)}, u32[]{:S(2)}, u32[]{:S(2)}) collective-permute-start(bf16[8,4096]{1,0:T(8,128)(2,1)S(1)} %gather_fusion.1), channel_id=1, source_target_pairs={{0,64},{1,65},{2,66},{3,67},{4,68},{5,69},{6,70},{7,71},{8,72},{9,... | collective-permute-start | bytes 196616 | tf_op jit(solution)/shard_map/ppermute | solution.py:36
  47.2 5.8 %collective-permute-start.5 = (bf16[8,4096]{1,0:T(8,128)(2,1)S(1)}, bf16[8,4096]{1,0:T(8,128)(2,1)S(1)}, u32[]{:S(2)}, u32[]{:S(2)}) collective-permute-start(bf16[8,4096]{1,0:T(8,128)(2,1)S(1)} %gather_fusion.1), channel_id=1, source_target_pairs={{0,32},{1,33},{2,34},{3,35},{4,36},{5,37},{6,38},{7,39},{8,40},{9,... | collective-permute-start | bytes 196616 | tf_op jit(solution)/shard_map/ppermute | solution.py:36
  48.1 9.6 %collective-permute-start = (bf16[8,4096]{1,0:T(8,128)(2,1)S(1)}, bf16[8,4096]{1,0:T(8,128)(2,1)S(1)}, u32[]{:S(2)}, u32[]{:S(2)}) collective-permute-start(bf16[8,4096]{1,0:T(8,128)(2,1)S(1)} %gather_fusion.1), channel_id=1, source_target_pairs={{0,96},{1,97},{2,98},{3,99},{4,100},{5,101},{6,102},{7,103},{8,104... | collective-permute-start | bytes 196616 | tf_op jit(solution)/shard_map/ppermute | solution.py:36
  53.0 7.7 %collective-permute-start.6 = (bf16[16,4096]{1,0:T(8,128)(2,1)S(1)}, bf16[16,4096]{1,0:T(8,128)(2,1)S(1)}, u32[]{:S(2)}, u32[]{:S(2)}) collective-permute-start(bf16[16,4096]{1,0:T(8,128)(2,1)S(1)} %get-tuple-element.27), channel_id=1, source_target_pairs={{0,6},{1,7},{2,0},{3,1},{4,2},{5,3},{6,4},{7,5},{8,14},{9,15},{10,... | collective-permute-start | bytes 393224 | tf_op jit(solution)/shard_map/ppermute | solution.py:36
  56.1 7.0 %collective-permute-start.7 = (bf16[16,4096]{1,0:T(8,128)(2,1)S(1)}, bf16[16,4096]{1,0:T(8,128)(2,1)S(1)}, u32[]{:S(2)}, u32[]{:S(2)}) collective-permute-start(bf16[16,4096]{1,0:T(8,128)(2,1)S(1)} %get-tuple-element.27), channel_id=1, source_target_pairs={{0,4},{1,5},{2,6},{3,7},{4,0},{5,1},{6,2},{7,3},{8,12},{9,13},{10,... | collective-permute-start | bytes 393224 | tf_op jit(solution)/shard_map/ppermute | solution.py:36
  56.7 7.7 %collective-permute-start.8 = (bf16[16,4096]{1,0:T(8,128)(2,1)S(1)}, bf16[16,4096]{1,0:T(8,128)(2,1)S(1)}, u32[]{:S(2)}, u32[]{:S(2)}) collective-permute-start(bf16[16,4096]{1,0:T(8,128)(2,1)S(1)} %get-tuple-element.27), channel_id=1, source_target_pairs={{0,2},{1,3},{2,4},{3,5},{4,6},{5,7},{6,0},{7,1},{8,10},{9,11},{10,... | collective-permute-start | bytes 393224 | tf_op jit(solution)/shard_map/ppermute | solution.py:36
  57.7 8.7 %collective-permute-start.1 = (bf16[16,4096]{1,0:T(8,128)(2,1)S(1)}, bf16[16,4096]{1,0:T(8,128)(2,1)S(1)}, u32[]{:S(2)}, u32[]{:S(2)}) collective-permute-start(bf16[16,4096]{1,0:T(8,128)(2,1)S(1)} %get-tuple-element.31), channel_id=1, source_target_pairs={{0,17},{1,0},{2,19},{3,2},{4,21},{5,4},{6,23},{7,6},{8,25},{9,8},{... | collective-permute-start | bytes 393224 | tf_op jit(solution)/shard_map/ppermute | solution.py:36
  60.8 6.6 %collective-permute-start.2 = (bf16[16,4096]{1,0:T(8,128)(2,1)S(1)}, bf16[16,4096]{1,0:T(8,128)(2,1)S(1)}, u32[]{:S(2)}, u32[]{:S(2)}) collective-permute-start(bf16[16,4096]{1,0:T(8,128)(2,1)S(1)} %get-tuple-element.31), channel_id=1, source_target_pairs={{0,16},{1,17},{2,18},{3,19},{4,20},{5,21},{6,22},{7,23},{8,24},{9,... | collective-permute-start | bytes 393224 | tf_op jit(solution)/shard_map/ppermute | solution.py:36
  63.1 6.4 %collective-permute-start.3 = (bf16[16,4096]{1,0:T(8,128)(2,1)S(1)}, bf16[16,4096]{1,0:T(8,128)(2,1)S(1)}, u32[]{:S(2)}, u32[]{:S(2)}) collective-permute-start(bf16[16,4096]{1,0:T(8,128)(2,1)S(1)} %get-tuple-element.31), channel_id=1, source_target_pairs={{0,1},{1,16},{2,3},{3,18},{4,5},{5,20},{6,7},{7,22},{8,9},{9,24},{... | collective-permute-start | bytes 393224 | tf_op jit(solution)/shard_map/ppermute | solution.py:36
  64.4 13.0 %collective-permute-start.13 = (bf16[64,4096]{1,0:T(8,128)(2,1)S(1)}, bf16[64,4096]{1,0:T(8,128)(2,1)S(1)}, u32[]{:S(2)}, u32[]{:S(2)}) collective-permute-start(bf16[64,4096]{1,0:T(8,128)(2,1)S(1)} %constant_dynamic-update-slice_fusion.9.refs_1_), channel_id=1, source_target_pairs={{0,17},{1,0},{2,19},{3,2},{4,21},{5,4},{6,23},{7,6},{8,25},{9,8},{... | collective-permute-start | bytes 1572872 | tf_op jit(solution)/shard_map/ppermute | solution.py:36
  66.4 14.4 %collective-permute-start.14 = (bf16[64,4096]{1,0:T(8,128)(2,1)S(1)}, bf16[64,4096]{1,0:T(8,128)(2,1)S(1)}, u32[]{:S(2)}, u32[]{:S(2)}) collective-permute-start(bf16[64,4096]{1,0:T(8,128)(2,1)S(1)} %constant_dynamic-update-slice_fusion.9.refs_1_), channel_id=1, source_target_pairs={{0,1},{1,16},{2,3},{3,18},{4,5},{5,20},{6,7},{7,22},{8,9},{9,24},{... | collective-permute-start | bytes 1572872 | tf_op jit(solution)/shard_map/ppermute | solution.py:36
  69.5 14.5 %collective-permute-start.11 = (bf16[64,4096]{1,0:T(8,128)(2,1)S(1)}, bf16[64,4096]{1,0:T(8,128)(2,1)S(1)}, u32[]{:S(2)}, u32[]{:S(2)}) collective-permute-start(bf16[64,4096]{1,0:T(8,128)(2,1)S(1)} %constant_dynamic-update-slice_fusion.2.refs_0_), channel_id=1, source_target_pairs={{0,6},{1,7},{2,0},{3,1},{4,2},{5,3},{6,4},{7,5},{8,14},{9,15},{10,... | collective-permute-start | bytes 1572872 | tf_op jit(solution)/shard_map/ppermute | solution.py:36
  74.3 13.1 %collective-permute-start.12 = (bf16[64,4096]{1,0:T(8,128)(2,1)S(1)}, bf16[64,4096]{1,0:T(8,128)(2,1)S(1)}, u32[]{:S(2)}, u32[]{:S(2)}) collective-permute-start(bf16[64,4096]{1,0:T(8,128)(2,1)S(1)} %constant_dynamic-update-slice_fusion.2.refs_0_), channel_id=1, source_target_pairs={{0,2},{1,3},{2,4},{3,5},{4,6},{5,7},{6,0},{7,1},{8,10},{9,11},{10,... | collective-permute-start | bytes 1572872 | tf_op jit(solution)/shard_map/ppermute | solution.py:36
  77.4 14.8 %collective-permute-start.10 = (f32[2,2048]{1,0:T(2,128)S(1)}, f32[2,2048]{1,0:T(2,128)S(1)}, u32[]{:S(2)}, u32[]{:S(2)}) collective-permute-start(f32[2,2048]{1,0:T(2,128)S(1)} %pad_maximum_fusion.1.refs_4_.refs_6_), channel_id=1, source_target_pairs={{0,8},{1,9},{2,10},{3,11},{4,12},{5,13},{6,14},{7,15},{8,0},{9,1},... | collective-permute-start | bytes 49160 | tf_op jit(solution)/shard_map/ppermute | solution.py:36
  87.4 29.9 %collective-permute-start.15 = (bf16[64,4096]{1,0:T(8,128)(2,1)S(1)}, bf16[64,4096]{1,0:T(8,128)(2,1)S(1)}, u32[]{:S(2)}, u32[]{:S(2)}) collective-permute-start(bf16[64,4096]{1,0:T(8,128)(2,1)S(1)} %constant_dynamic-update-slice_fusion.2.refs_0_), channel_id=1, source_target_pairs={{0,4},{1,5},{2,6},{3,7},{4,0},{5,1},{6,2},{7,3},{8,12},{9,13},{10,... | collective-permute-start | bytes 1572872 | tf_op jit(solution)/shard_map/ppermute | solution.py:36
  87.4 29.9 %collective-permute-start.16 = (bf16[64,4096]{1,0:T(8,128)(2,1)S(1)}, bf16[64,4096]{1,0:T(8,128)(2,1)S(1)}, u32[]{:S(2)}, u32[]{:S(2)}) collective-permute-start(bf16[64,4096]{1,0:T(8,128)(2,1)S(1)} %constant_dynamic-update-slice_fusion.9.refs_1_), channel_id=1, source_target_pairs={{0,16},{1,17},{2,18},{3,19},{4,20},{5,21},{6,22},{7,23},{8,24},{9,... | collective-permute-start | bytes 1572872 | tf_op jit(solution)/shard_map/ppermute | solution.py:36
  106.8 42.7 %copy-start.1 = (bf16[1,1,256,4096]{3,2,1,0:T(8,128)(2,1)S(1)}, bf16[1,1,256,4096]{3,2,1,0:T(8,128)(2,1)}, u32[]{:S(2)}) copy-start(bf16[1,1,256,4096]{3,2,1,0:T(8,128)(2,1)} %param.6) | copy-start | bytes 6291460

commit v2 on v1

--- a/solution.py
+++ b/solution.py
@@ -36,17 +36,13 @@
     return lax.ppermute(value, AXES, moves(**step))
 
 
-def add_terms(cand, docs, cw, out_ref, start, doc_at):
+def add_terms(cand, docs, cw, out_ref, start):
     scores = lax.dot_general(
-        cand[...], docs[pl.ds(start, TILE), :], (((1,), (1,)), ((), ())), preferred_element_type=jnp.float32
-    )
-    cover = cw[0:1, pl.ds(doc_at, TILE)]
-    weight = cw[1:2, pl.ds(doc_at, TILE)]
-    term = weight * jnp.maximum(scores - cover, 0.0)
-    total = out_ref[...]
-    for j in range(TILE // 128):
-        total = total + term[:, j * 128 : (j + 1) * 128]
-    out_ref[...] = total
+        docs[pl.ds(start, TILE), :], cand[...], (((1,), (1,)), ((), ())), preferred_element_type=jnp.float32
+    )
+    columns = cw[:, pl.ds(start, TILE)].T
+    term = columns[:, 1:2] * jnp.maximum(scores - columns[:, 0:1], 0.0)
+    out_ref[...] += jnp.sum(term.reshape(TILE // 8, 8, term.shape[1]), axis=0)
 
 
 def pack(pieces, cand):
@@ -77,7 +73,7 @@
         def step(i, carry, source=source, docs=docs, cw=cw, base=base):
             copy(i, source, docs, base).wait()
             start = pl.multiple_of(i * TILE, TILE)
-            add_terms(cand, docs, cw, out_ref, start, start)
+            add_terms(cand, docs, cw, out_ref, start)
             return carry
 
         lax.fori_loop(0, steps, step, 0)
@@ -92,7 +88,7 @@
 
         def step(i, carry, docs=docs, cw=cw):
             start = pl.multiple_of(i * TILE, TILE)
-            add_terms(cand, docs, cw, out_ref, start, start)
+            add_terms(cand, docs, cw, out_ref, start)
             return carry
 
         lax.fori_loop(0, docs.shape[0] // TILE, step, 0)
@@ -104,7 +100,7 @@
     docs = own_docs.shape[0] + sib_docs.shape[0]
     in_vmem = pl.BlockSpec(memory_space=pltpu.VMEM)
     in_hbm = pl.BlockSpec(memory_space=pltpu.HBM)
-    out_shape = [jax.ShapeDtypeStruct((rows, 128), jnp.float32)]
+    out_shape = [jax.ShapeDtypeStruct((8, rows), jnp.float32)]
     scratch = [pltpu.VMEM((rows, width), jnp.bfloat16)]
     if first:
         out_shape += [pltpu.VMEM(own_docs.shape, own_docs.dtype), pltpu.VMEM(sib_docs.shape, sib_docs.dtype)]
@@ -117,7 +113,7 @@
         scratch_shapes=scratch,
         compiler_params=pltpu.CompilerParams(vmem_limit_bytes=8 * 2**20),
         cost_estimate=pl.CostEstimate(
-            flops=2 * docs * rows * width, bytes_accessed=docs * width * 2 if first else 0, transcendentals=0
+            flops=5 * docs * rows * width, bytes_accessed=0, transcendentals=0
         ),
         name=name,
     )(*pieces, own_docs, sib_docs, own_cw, sib_cw)
@@ -137,8 +133,7 @@
     cw = jnp.stack(
         [coverage.reshape(-1) * scale_up, elem_weight.reshape(-1) * (1.0 / (scale_up * element_total))]
     )
-    sib_docs = send(docs, dc=1)
-    sib_cw = send(cw, dc=1)
+    cw = jnp.pad(cw, ((0, 6), (0, 0)))
 
     positions = jnp.arange(share_len, dtype=jnp.int32)
     same_owner = owner_ids[:, None] == owner_ids[None, :]
@@ -156,6 +151,8 @@
     )
     own = fetched.reshape(slab_count * slot_cap, width).at[slot_id].get(mode="promise_in_bounds")
 
+    own, outgoing = lax.optimization_barrier((own, docs))
+    sib_docs, sib_cw = send(outgoing, dc=1), send(cw, dc=1)
     z3, z1, z2 = send(own, dz=1), send(own, dz=-1), send(own, dz=2)
     part_a = jnp.concatenate([own, z1], axis=0)
     part_b = jnp.concatenate([z2, z3], axis=0)
@@ -168,12 +165,15 @@
     g0, own_here, sib_here = gains_of(
         [block_a, block_b], docs, sib_docs, cw, sib_cw, "gains_near", first=True
     )
-    far_a, far_b, aa1, aa3, bb1, bb3 = lax.optimization_barrier((block_a, block_b, aa1, aa3, bb1, bb3))
+    far_a, far_b, aa1, aa3, bb1, bb3, g0 = lax.optimization_barrier(
+        (block_a, block_b, aa1, aa3, bb1, bb3, g0)
+    )
     aa2, bb2 = send(far_a, dy=2), send(far_b, dx=2)
     (g1,) = gains_of([aa1, aa3, bb1, bb3], own_here, sib_here, cw, sib_cw, "gains_next")
     cw, g1 = lax.optimization_barrier((cw, g1))
     (g2,) = gains_of([aa2, bb2], own_here, sib_here, cw, sib_cw, "gains_far")
-    g0, g1, g2 = jnp.sum(g0, axis=1), jnp.sum(g1, axis=1), jnp.sum(g2, axis=1)
+    g0, g1, g2 = lax.optimization_barrier((g0, g1, g2))
+    g0, g1, g2 = jnp.sum(g0, axis=0), jnp.sum(g1, axis=0), jnp.sum(g2, axis=0)
     n = block_a.shape[0]
     gain_a = jnp.stack([g0[:n], g1[:n], g2[:n], g1[n : 2 * n]])
     gain_b = jnp.stack([g0[n:], g1[2 * n : 3 * n], g2[n:], g1[3 * n :]])

time: 150 us -> 121 us (0.81)
  waiting for transfers between devices: 44 us -> 21.2 us
  starting transfers between devices: 39.9 us -> 25.8 us
  blocking collectives: 17.8 us -> 30.5 us
  Pallas kernels: 37.2 us -> 33.7 us
    all_to_all x0 -> x1, blocking collectives: none -> 15.3 us  [body(): lax.all_to_all(requests, 'slab', split_axis=0, concat_axis=0, tiled=True)]
    all_to_all x1 -> x0, waiting for transfers between devices: 13.5 us -> none  [body(): lax.all_to_all(requests, 'slab', split_axis=0, concat_axis=0, tiled=True)]
    ppermute x17, waiting for transfers between devices: 21.6 us -> 12.3 us  [send(): return lax.ppermute(value, AXES, moves(**step))]
    all_to_all x1 -> x0, starting transfers between devices: 8 us -> none  [body(): lax.all_to_all(requests, 'slab', split_axis=0, concat_axis=0, tiled=True)]
    all_to_all x1, starting transfers between devices: 7.81 us -> 3.53 us  [body(): lax.all_to_all(doc_rows.reshape(slab_count, slot_cap, width), 'slab', spl...]
    pallas_call x3, Pallas kernels: 37.2 us -> 33.7 us  [gains_of(): pl.pallas_call(functools.partial(first_kernel if first else later_kernel,...]
    all_to_all x1, blocking collectives: 17.8 us -> 15.1 us  [body(): lax.all_to_all(terms, AXES, split_axis=0, concat_axis=0, tiled=True, axis...]
    ppermute x17, starting transfers between devices: 24.1 us -> 22.2 us  [send(): return lax.ppermute(value, AXES, moves(**step))]
  transfers between devices with their start and end apart: 19 -> 18, of which waited for: 13 -> 10; matrix products, arithmetic and copies ran while one was open for 5% -> 1% of each run, Pallas kernels for 17% -> 19%
where the time goes in v2:
time: 121 us
  Pallas kernels  33.7 us (28%)
  blocking collectives  30.5 us (25%)
  starting transfers between devices  25.8 us (21%)
  waiting for transfers between devices  21.2 us (18%)
  other arithmetic  5.44 us (4%)
  local copies, waits for them, and re-layouts  4.04 us (3%)
    pallas_call x3, Pallas kernels, gains_of(): pl.pallas_call(functools.partial(first_kernel if first else later_kernel,...  33.7 us
    ppermute x17, starting transfers between devices, send(): return lax.ppermute(value, AXES, moves(**step))  22.2 us
    all_to_all x1, blocking collectives, body(): lax.all_to_all(requests, 'slab', split_axis=0, concat_axis=0, tiled=True)  15.3 us
    all_to_all x1, blocking collectives, body(): lax.all_to_all(terms, AXES, split_axis=0, concat_axis=0, tiled=True, axis...  15.1 us
    ppermute x17, waiting for transfers between devices, send(): return lax.ppermute(value, AXES, moves(**step))  12.3 us
    all_to_all x1, waiting for transfers between devices, body(): lax.all_to_all(doc_rows.reshape(slab_count, slot_cap, width), 'slab', spl...  8.84 us
    all_to_all x1, starting transfers between devices, body(): lax.all_to_all(doc_rows.reshape(slab_count, slot_cap, width), 'slab', spl...  3.53 us
  transfers between devices with their start and end apart: 18, of which 10 were waited for; matrix products, arithmetic and copies ran while one was open for 1% of the time, Pallas kernels for 19%

profile of v2, /device:TPU:0, one launch (start us, length us, event | category | flops | bytes accessed | tf_op | source)
XLA Modules:
  0.0 120.8 jit_solution(9748820955872907740)
XLA Ops:
  0.0 1.0 convert_reduce_fusion
  2.5 15.3 %all_to_all.23 = s32[16,1,2]{2,1,0:T(1,128)S(1)} all-to-all(s32[16,1,2]{2,1,0:T(1,128)S(1)} %bitcast.34), channel_id=1, replica_groups=mesh['slab'=16,'loop'=8] {'slab'}, dimensions={0} | all-to-all | bytes 256 | tf_op jit(solution)/shard_map/all_to_all | solution.py:147
  19.8 0.9 reshape.231
  20.7 3.5 %all-to-all-start.1 = ((bf16[16,2,4096]{2,1,0:T(2,128)(2,1)}), bf16[16,2,4096]{2,1,0:T(2,128)(2,1)S(1)}, u32[]{:S(2)}, u32[]{:S(2)}) async-start(bf16[16,2,4096]{2,1,0:T(2,128)(2,1)} %reshape.231), calls=%async_computation.1 | async-start | bytes 524288 | tf_op jit(solution)/shard_map/all_to_all | solution.py:149
  24.9 8.8 %all-to-all-done.1 = bf16[16,2,4096]{2,1,0:T(2,128)(2,1)S(1)} async-done(((bf16[16,2,4096]{2,1,0:T(2,128)(2,1)}), bf16[16,2,4096]{2,1,0:T(2,128)(2,1)S(1)}, u32[]{:S(2)}, u32[]{:S(2)}) %all-to-all-start.1) | async-done | bytes 262176 | tf_op jit(solution)/shard_map/all_to_all | solution.py:149
  36.0 0.9 collective-permute-start.4
  36.9 0.9 collective-permute-start.5
  37.8 2.4 %collective-permute-start = (bf16[8,4096]{1,0:T(8,128)(2,1)S(1)}, bf16[8,4096]{1,0:T(8,128)(2,1)S(1)}, u32[]{:S(2)}, u32[]{:S(2)}) collective-permute-start(bf16[8,4096]{1,0:T(8,128)(2,1)S(1)} %gather_fusion.1), channel_id=1, source_target_pairs={{0,96},{1,97},{2,98},{3,99},{4,100},{5,101},{6,102},{7,103},{8,104... | collective-permute-start | bytes 196616 | tf_op jit(solution)/shard_map/ppermute | solution.py:36
  40.2 2.1 %collective-permute-done.4 = bf16[8,4096]{1,0:T(8,128)(2,1)S(1)} collective-permute-done((bf16[8,4096]{1,0:T(8,128)(2,1)S(1)}, bf16[8,4096]{1,0:T(8,128)(2,1)S(1)}, u32[]{:S(2)}, u32[]{:S(2)}) %collective-permute-start.4) | collective-permute-done | bytes 65568 | tf_op jit(solution)/shard_map/ppermute | solution.py:36
  43.0 3.1 %collective-permute-start.6 = (bf16[16,4096]{1,0:T(8,128)(2,1)S(1)}, bf16[16,4096]{1,0:T(8,128)(2,1)S(1)}, u32[]{:S(2)}, u32[]{:S(2)}) collective-permute-start(bf16[16,4096]{1,0:T(8,128)(2,1)S(1)} %get-tuple-element.39), channel_id=1, source_target_pairs={{0,6},{1,7},{2,0},{3,1},{4,2},{5,3},{6,4},{7,5},{8,14},{9,15},{10,... | collective-permute-start | bytes 393224 | tf_op jit(solution)/shard_map/ppermute | solution.py:36
  46.7 1.0 collective-permute-start.8
  47.7 3.7 %collective-permute-done.6 = bf16[16,4096]{1,0:T(8,128)(2,1)S(1)} collective-permute-done((bf16[16,4096]{1,0:T(8,128)(2,1)S(1)}, bf16[16,4096]{1,0:T(8,128)(2,1)S(1)}, u32[]{:S(2)}, u32[]{:S(2)}) %collective-permute-start.6) | collective-permute-done | bytes 131104 | tf_op jit(solution)/shard_map/ppermute | solution.py:36
  52.0 1.7 %collective-permute-done.7 = bf16[16,4096]{1,0:T(8,128)(2,1)S(1)} collective-permute-done((bf16[16,4096]{1,0:T(8,128)(2,1)S(1)}, bf16[16,4096]{1,0:T(8,128)(2,1)S(1)}, u32[]{:S(2)}, u32[]{:S(2)}) %collective-permute-start.7) | collective-permute-done | bytes 131104 | tf_op jit(solution)/shard_map/ppermute | solution.py:36
  55.7 1.4 %collective-permute-done.1 = bf16[16,4096]{1,0:T(8,128)(2,1)S(1)} collective-permute-done((bf16[16,4096]{1,0:T(8,128)(2,1)S(1)}, bf16[16,4096]{1,0:T(8,128)(2,1)S(1)}, u32[]{:S(2)}, u32[]{:S(2)}) %collective-permute-start.1) | collective-permute-done | bytes 131104 | tf_op jit(solution)/shard_map/ppermute | solution.py:36
  57.1 2.5 %collective-permute-start.11 = (bf16[64,4096]{1,0:T(8,128)(2,1)S(1)}, bf16[64,4096]{1,0:T(8,128)(2,1)S(1)}, u32[]{:S(2)}, u32[]{:S(2)}) collective-permute-start(bf16[64,4096]{1,0:T(8,128)(2,1)S(1)} %constant_dynamic-update-slice_fusion.9.refs_1_), channel_id=1, source_target_pairs={{0,17},{1,0},{2,19},{3,2},{4,21},{5,4},{6,23},{7,6},{8,25},{9,8},{... | collective-permute-start | bytes 1572872 | tf_op jit(solution)/shard_map/ppermute | solution.py:36
  59.6 0.9 collective-permute-done.2
  60.5 1.7 %collective-permute-start.12 = (bf16[64,4096]{1,0:T(8,128)(2,1)S(1)}, bf16[64,4096]{1,0:T(8,128)(2,1)S(1)}, u32[]{:S(2)}, u32[]{:S(2)}) collective-permute-start(bf16[64,4096]{1,0:T(8,128)(2,1)S(1)} %constant_dynamic-update-slice_fusion.9.refs_1_), channel_id=1, source_target_pairs={{0,1},{1,16},{2,3},{3,18},{4,5},{5,20},{6,7},{7,22},{8,9},{9,24},{... | collective-permute-start | bytes 1572872 | tf_op jit(solution)/shard_map/ppermute | solution.py:36
  62.2 1.2 collective-permute-done.3
  63.5 3.2 %collective-permute-start.9 = (bf16[64,4096]{1,0:T(8,128)(2,1)S(1)}, bf16[64,4096]{1,0:T(8,128)(2,1)S(1)}, u32[]{:S(2)}, u32[]{:S(2)}) collective-permute-start(bf16[64,4096]{1,0:T(8,128)(2,1)S(1)} %constant_dynamic-update-slice_fusion.2.refs_0_), channel_id=1, source_target_pairs={{0,6},{1,7},{2,0},{3,1},{4,2},{5,3},{6,4},{7,5},{8,14},{9,15},{10,... | collective-permute-start | bytes 1572872 | tf_op jit(solution)/shard_map/ppermute | solution.py:36
  66.7 12.6 %gains_near.1 = (f32[8,128]{1,0:T(8,128)S(1)}, bf16[2048,4096]{1,0:T(8,128)(2,1)S(1)}, bf16[2048,4096]{1,0:T(8,128)(2,1)S(1)}) custom-call(bf16[64,4096]{1,0:T(8,128)(2,1)S(1)} %constant_dynamic-update-slice_fusion.2.refs_0_, bf16[64,4096]{1,0:T(8,128)(2,1)S(1)} %constant_dynamic-update-slice_fusion.9.refs_1_, bf16[2048,4096]{1,0:T(8,128)(2,1)} %bitcast.40, ...), custom_call_target="tpu_custom_call" | custom-call | flops 10737418240 | tf_op jit(solution)/shard_map/gains_near/pallas_call | solution.py:108
  79.7 2.8 %collective-permute-start.16 = (bf16[64,4096]{1,0:T(8,128)(2,1)S(1)}, bf16[64,4096]{1,0:T(8,128)(2,1)S(1)}, u32[]{:S(2)}, u32[]{:S(2)}) collective-permute-start(bf16[64,4096]{1,0:T(8,128)(2,1)S(1)} %constant_dynamic-update-slice_fusion.9.refs_1_), channel_id=1, source_target_pairs={{0,16},{1,17},{2,18},{3,19},{4,20},{5,21},{6,22},{7,23},{8,24},{9,... | collective-permute-start | bytes 1572872 | tf_op jit(solution)/shard_map/ppermute | solution.py:36
  82.5 10.7 %gains_next.1 = f32[8,256]{1,0:T(8,128)S(1)} custom-call(bf16[64,4096]{1,0:T(8,128)(2,1)S(1)} %collective-permute-done.9.refs_0_, bf16[64,4096]{1,0:T(8,128)(2,1)S(1)} %collective-permute-done.10.refs_1_, bf16[64,4096]{1,0:T(8,128)(2,1)S(1)} %collective-permute-done.11.refs_2_, bf16[64,4096]{1,0:T(8,128)(2,1)S(1)} %collective-permute-done.12.refs_3_, ...), custom_call_target="tpu_custom_call" | custom-call | flops 21474836480 | tf_op jit(solution)/shard_map/gains_next/pallas_call | solution.py:108
  93.4 10.4 %gains_far.1 = f32[8,128]{1,0:T(8,128)S(1)} custom-call(bf16[64,4096]{1,0:T(8,128)(2,1)S(1)} %collective-permute-done.15.refs_0_, bf16[64,4096]{1,0:T(8,128)(2,1)S(1)} %collective-permute-done.16.refs_1_, bf16[2048,4096]{1,0:T(8,128)(2,1)S(1)} %get-tuple-element.30.refs_4_.refs_2_, bf16[2048,4096]{1,0:T(8,128)(2,1)S(1)} %get-tuple-element.31.refs_5_.refs_3_, ...), custom_call_target="tpu_custom_call" | custom-call | flops 10737418240 | tf_op jit(solution)/shard_map/gains_far/pallas_call | solution.py:108
  105.1 15.1 %all_to_all.24 = f32[64,1,8]{2,1,0:T(1,128)S(1)} all-to-all(f32[64,1,8]{2,1,0:T(1,128)S(1)} %bitcast.33), channel_id=1, replica_groups={{0,1,2,3,4,5,6,7,16,17,18,19,20,21,22,23,32,33,34,35,36,37,38,39,48,49,..., dimensions={0} | all-to-all | bytes 4096 | tf_op jit(solution)/shard_map/all_to_all | solution.py:192
  (69 shorter events, 12.7 us)
Async XLA Ops:
  0.0 19.1 %copy-start = (bf16[1,1,256,4096]{3,2,1,0:T(8,128)(2,1)S(1)}, bf16[1,1,256,4096]{3,2,1,0:T(8,128)(2,1)}, u32[]{:S(2)}) copy-start(bf16[1,1,256,4096]{3,2,1,0:T(8,128)(2,1)} %param.6) | copy-start | bytes 6291460
  20.7 13.1 %all-to-all-start.1 = ((bf16[16,2,4096]{2,1,0:T(2,128)(2,1)}), bf16[16,2,4096]{2,1,0:T(2,128)(2,1)S(1)}, u32[]{:S(2)}, u32[]{:S(2)}) async-start(bf16[16,2,4096]{2,1,0:T(2,128)(2,1)} %reshape.231), calls=%async_computation.1 | async-start | bytes 524288 | tf_op jit(solution)/shard_map/all_to_all | solution.py:149
  34.5 32.2 %collective-permute-start.13 = (bf16[2048,4096]{1,0:T(8,128)(2,1)}, bf16[2048,4096]{1,0:T(8,128)(2,1)}, u32[]{:S(2)}, u32[]{:S(2)}) collective-permute-start(bf16[2048,4096]{1,0:T(8,128)(2,1)} %bitcast.39), channel_id=1, source_target_pairs={{0,8},{1,9},{2,10},{3,11},{4,12},{5,13},{6,14},{7,15},{8,0},{9,1},... | collective-permute-start | bytes 50331656 | tf_op jit(solution)/shard_map/ppermute | solution.py:36
  35.3 28.1 %collective-permute-start.14 = (f32[8,2048]{1,0:T(8,128)S(1)}, f32[8,2048]{1,0:T(8,128)S(1)}, u32[]{:S(2)}, u32[]{:S(2)}) collective-permute-start(f32[8,2048]{1,0:T(8,128)S(1)} %select_maximum_fusion.refs_4_.refs_6_), channel_id=1, source_target_pairs={{0,8},{1,9},{2,10},{3,11},{4,12},{5,13},{6,14},{7,15},{8,0},{9,1},... | collective-permute-start | bytes 196616 | tf_op jit(solution)/shard_map/ppermute | solution.py:36
  36.0 6.3 %collective-permute-start.4 = (bf16[8,4096]{1,0:T(8,128)(2,1)S(1)}, bf16[8,4096]{1,0:T(8,128)(2,1)S(1)}, u32[]{:S(2)}, u32[]{:S(2)}) collective-permute-start(bf16[8,4096]{1,0:T(8,128)(2,1)S(1)} %gather_fusion.1), channel_id=1, source_target_pairs={{0,64},{1,65},{2,66},{3,67},{4,68},{5,69},{6,70},{7,71},{8,72},{9,... | collective-permute-start | bytes 196616 | tf_op jit(solution)/shard_map/ppermute | solution.py:36
  36.9 6.1 %collective-permute-start.5 = (bf16[8,4096]{1,0:T(8,128)(2,1)S(1)}, bf16[8,4096]{1,0:T(8,128)(2,1)S(1)}, u32[]{:S(2)}, u32[]{:S(2)}) collective-permute-start(bf16[8,4096]{1,0:T(8,128)(2,1)S(1)} %gather_fusion.1), channel_id=1, source_target_pairs={{0,32},{1,33},{2,34},{3,35},{4,36},{5,37},{6,38},{7,39},{8,40},{9,... | collective-permute-start | bytes 196616 | tf_op jit(solution)/shard_map/ppermute | solution.py:36
  37.8 9.0 %collective-permute-start = (bf16[8,4096]{1,0:T(8,128)(2,1)S(1)}, bf16[8,4096]{1,0:T(8,128)(2,1)S(1)}, u32[]{:S(2)}, u32[]{:S(2)}) collective-permute-start(bf16[8,4096]{1,0:T(8,128)(2,1)S(1)} %gather_fusion.1), channel_id=1, source_target_pairs={{0,96},{1,97},{2,98},{3,99},{4,100},{5,101},{6,102},{7,103},{8,104... | collective-permute-start | bytes 196616 | tf_op jit(solution)/shard_map/ppermute | solution.py:36
  43.0 8.4 %collective-permute-start.6 = (bf16[16,4096]{1,0:T(8,128)(2,1)S(1)}, bf16[16,4096]{1,0:T(8,128)(2,1)S(1)}, u32[]{:S(2)}, u32[]{:S(2)}) collective-permute-start(bf16[16,4096]{1,0:T(8,128)(2,1)S(1)} %get-tuple-element.39), channel_id=1, source_target_pairs={{0,6},{1,7},{2,0},{3,1},{4,2},{5,3},{6,4},{7,5},{8,14},{9,15},{10,... | collective-permute-start | bytes 393224 | tf_op jit(solution)/shard_map/ppermute | solution.py:36
  46.1 7.7 %collective-permute-start.7 = (bf16[16,4096]{1,0:T(8,128)(2,1)S(1)}, bf16[16,4096]{1,0:T(8,128)(2,1)S(1)}, u32[]{:S(2)}, u32[]{:S(2)}) collective-permute-start(bf16[16,4096]{1,0:T(8,128)(2,1)S(1)} %get-tuple-element.39), channel_id=1, source_target_pairs={{0,4},{1,5},{2,6},{3,7},{4,0},{5,1},{6,2},{7,3},{8,12},{9,13},{10,... | collective-permute-start | bytes 393224 | tf_op jit(solution)/shard_map/ppermute | solution.py:36
  46.7 8.4 %collective-permute-start.8 = (bf16[16,4096]{1,0:T(8,128)(2,1)S(1)}, bf16[16,4096]{1,0:T(8,128)(2,1)S(1)}, u32[]{:S(2)}, u32[]{:S(2)}) collective-permute-start(bf16[16,4096]{1,0:T(8,128)(2,1)S(1)} %get-tuple-element.39), channel_id=1, source_target_pairs={{0,2},{1,3},{2,4},{3,5},{4,6},{5,7},{6,0},{7,1},{8,10},{9,11},{10,... | collective-permute-start | bytes 393224 | tf_op jit(solution)/shard_map/ppermute | solution.py:36
  51.4 5.7 %collective-permute-start.1 = (bf16[16,4096]{1,0:T(8,128)(2,1)S(1)}, bf16[16,4096]{1,0:T(8,128)(2,1)S(1)}, u32[]{:S(2)}, u32[]{:S(2)}) collective-permute-start(bf16[16,4096]{1,0:T(8,128)(2,1)S(1)} %get-tuple-element.43), channel_id=1, source_target_pairs={{0,17},{1,0},{2,19},{3,2},{4,21},{5,4},{6,23},{7,6},{8,25},{9,8},{... | collective-permute-start | bytes 393224 | tf_op jit(solution)/shard_map/ppermute | solution.py:36
  53.8 6.7 %collective-permute-start.2 = (bf16[16,4096]{1,0:T(8,128)(2,1)S(1)}, bf16[16,4096]{1,0:T(8,128)(2,1)S(1)}, u32[]{:S(2)}, u32[]{:S(2)}) collective-permute-start(bf16[16,4096]{1,0:T(8,128)(2,1)S(1)} %get-tuple-element.43), channel_id=1, source_target_pairs={{0,16},{1,17},{2,18},{3,19},{4,20},{5,21},{6,22},{7,23},{8,24},{9,... | collective-permute-start | bytes 393224 | tf_op jit(solution)/shard_map/ppermute | solution.py:36
  55.1 8.2 %collective-permute-start.3 = (bf16[16,4096]{1,0:T(8,128)(2,1)S(1)}, bf16[16,4096]{1,0:T(8,128)(2,1)S(1)}, u32[]{:S(2)}, u32[]{:S(2)}) collective-permute-start(bf16[16,4096]{1,0:T(8,128)(2,1)S(1)} %get-tuple-element.43), channel_id=1, source_target_pairs={{0,1},{1,16},{2,3},{3,18},{4,5},{5,20},{6,7},{7,22},{8,9},{9,24},{... | collective-permute-start | bytes 393224 | tf_op jit(solution)/shard_map/ppermute | solution.py:36
  57.1 22.2 %collective-permute-start.11 = (bf16[64,4096]{1,0:T(8,128)(2,1)S(1)}, bf16[64,4096]{1,0:T(8,128)(2,1)S(1)}, u32[]{:S(2)}, u32[]{:S(2)}) collective-permute-start(bf16[64,4096]{1,0:T(8,128)(2,1)S(1)} %constant_dynamic-update-slice_fusion.9.refs_1_), channel_id=1, source_target_pairs={{0,17},{1,0},{2,19},{3,2},{4,21},{5,4},{6,23},{7,6},{8,25},{9,8},{... | collective-permute-start | bytes 1572872 | tf_op jit(solution)/shard_map/ppermute | solution.py:36
  60.5 18.8 %collective-permute-start.12 = (bf16[64,4096]{1,0:T(8,128)(2,1)S(1)}, bf16[64,4096]{1,0:T(8,128)(2,1)S(1)}, u32[]{:S(2)}, u32[]{:S(2)}) collective-permute-start(bf16[64,4096]{1,0:T(8,128)(2,1)S(1)} %constant_dynamic-update-slice_fusion.9.refs_1_), channel_id=1, source_target_pairs={{0,1},{1,16},{2,3},{3,18},{4,5},{5,20},{6,7},{7,22},{8,9},{9,24},{... | collective-permute-start | bytes 1572872 | tf_op jit(solution)/shard_map/ppermute | solution.py:36
  63.4 15.9 %collective-permute-start.10 = (bf16[64,4096]{1,0:T(8,128)(2,1)S(1)}, bf16[64,4096]{1,0:T(8,128)(2,1)S(1)}, u32[]{:S(2)}, u32[]{:S(2)}) collective-permute-start(bf16[64,4096]{1,0:T(8,128)(2,1)S(1)} %constant_dynamic-update-slice_fusion.2.refs_0_), channel_id=1, source_target_pairs={{0,2},{1,3},{2,4},{3,5},{4,6},{5,7},{6,0},{7,1},{8,10},{9,11},{10,... | collective-permute-start | bytes 1572872 | tf_op jit(solution)/shard_map/ppermute | solution.py:36
  63.5 15.9 %collective-permute-start.9 = (bf16[64,4096]{1,0:T(8,128)(2,1)S(1)}, bf16[64,4096]{1,0:T(8,128)(2,1)S(1)}, u32[]{:S(2)}, u32[]{:S(2)}) collective-permute-start(bf16[64,4096]{1,0:T(8,128)(2,1)S(1)} %constant_dynamic-update-slice_fusion.2.refs_0_), channel_id=1, source_target_pairs={{0,6},{1,7},{2,0},{3,1},{4,2},{5,3},{6,4},{7,5},{8,14},{9,15},{10,... | collective-permute-start | bytes 1572872 | tf_op jit(solution)/shard_map/ppermute | solution.py:36
  79.3 13.9 %collective-permute-start.15 = (bf16[64,4096]{1,0:T(8,128)(2,1)S(1)}, bf16[64,4096]{1,0:T(8,128)(2,1)S(1)}, u32[]{:S(2)}, u32[]{:S(2)}) collective-permute-start(bf16[64,4096]{1,0:T(8,128)(2,1)S(1)} %constant_dynamic-update-slice_fusion.2.refs_0_), channel_id=1, source_target_pairs={{0,4},{1,5},{2,6},{3,7},{4,0},{5,1},{6,2},{7,3},{8,12},{9,13},{10,... | collective-permute-start | bytes 1572872 | tf_op jit(solution)/shard_map/ppermute | solution.py:36
  79.7 13.7 %collective-permute-start.16 = (bf16[64,4096]{1,0:T(8,128)(2,1)S(1)}, bf16[64,4096]{1,0:T(8,128)(2,1)S(1)}, u32[]{:S(2)}, u32[]{:S(2)}) collective-permute-start(bf16[64,4096]{1,0:T(8,128)(2,1)S(1)} %constant_dynamic-update-slice_fusion.9.refs_1_), channel_id=1, source_target_pairs={{0,16},{1,17},{2,18},{3,19},{4,20},{5,21},{6,22},{7,23},{8,24},{9,... | collective-permute-start | bytes 1572872 | tf_op jit(solution)/shard_map/ppermute | solution.py:36
  82.5 38.3 %copy-start.1 = (bf16[1,1,256,4096]{3,2,1,0:T(8,128)(2,1)S(1)}, bf16[1,1,256,4096]{3,2,1,0:T(8,128)(2,1)}, u32[]{:S(2)}) copy-start(bf16[1,1,256,4096]{3,2,1,0:T(8,128)(2,1)} %param.6) | copy-start | bytes 6291460

commit v3 on v2

v3 whole, which is shorter than its diff:
```python
import functools

import jax
import jax.numpy as jnp
from jax import lax
from jax.experimental import pallas as pl
from jax.experimental.pallas import tpu as pltpu
from jax.sharding import PartitionSpec as P

AXES = ("slab", "loop")
RING = 4
TILE = 512


def place(index):
    slab, loop = divmod(index, 8)
    z, rest = divmod(slab, 4)
    hi, core = divmod(rest, 2)
    y, lo = divmod(loop, 2)
    return z, hi * 2 + lo, y, core


def index_of(z, x, y, core):
    return ((z * 2 + x // 2) * 2 + core) * 8 + y * 2 + x % 2


def moves(*steps):
    pairs = []
    for source in range(128):
        z, x, y, core = place(source)
        step = dict(steps[core % len(steps)])
        z, x, y = z + step.get("z", 0), x + step.get("x", 0), y + step.get("y", 0)
        pairs.append((source, index_of(z % RING, x % RING, y % RING, core ^ step.get("core", 0))))
    return pairs


def send(value, *steps):
    return lax.ppermute(value, AXES, moves(*steps))


def along(value, axes, distance):
    return send(value, *({axis: distance} for axis in axes))


def add_terms(cand, docs, cw, out_ref, start, doc_at):
    scores = lax.dot_general(
        docs[pl.ds(start, TILE), :], cand[...], (((1,), (1,)), ((), ())), preferred_element_type=jnp.float32
    )
    columns = cw[:, pl.ds(doc_at, TILE)].T
    term = columns[:, 1:2] * jnp.maximum(scores - columns[:, 0:1], 0.0)
    out_ref[...] += jnp.sum(term.reshape(TILE // 8, 8, term.shape[1]), axis=0)


def pack(pieces, cand):
    at = 0
    for piece in pieces:
        rows = piece.shape[0]
        cand[at : at + rows, :] = piece[...]
        at += rows


def loading_kernel(spans, held, *refs):
    count = len(spans)
    cand, sources, cws = refs[0], refs[1 : 1 + count], refs[1 + count : 1 + 2 * count]
    outs = refs[1 + 2 * count + held :]
    out_ref, loaded, arrived = outs[0], outs[1 : 1 + count], outs[1 + count :]

    def copy(part, i):
        low = spans[part][0]
        here = pl.ds(pl.multiple_of(i * TILE, TILE), TILE)
        there = pl.ds(pl.multiple_of(low + i * TILE, TILE), TILE)
        return pltpu.make_async_copy(sources[part].at[there], loaded[part].at[here], arrived[part].at[i])

    for part, (low, high) in enumerate(spans):
        for i in range((high - low) // TILE):
            copy(part, i).start()
    out_ref[...] = jnp.zeros_like(out_ref)
    for part, (low, high) in enumerate(spans):

        def step(i, carry, part=part, low=low):
            copy(part, i).wait()
            start = pl.multiple_of(i * TILE, TILE)
            add_terms(cand, loaded[part], cws[part], out_ref, start, pl.multiple_of(low + start, TILE))
            return carry

        lax.fori_loop(0, (high - low) // TILE, step, 0)


def loading_gains(cand, parts, name, held=()):
    rows, width = cand.shape
    spans = tuple((low, high) for _, low, high, _ in parts)
    docs = [pltpu.with_memory_space_constraint(part[0], pltpu.HBM) for part in parts]
    in_vmem = pl.BlockSpec(memory_space=pltpu.VMEM)
    in_hbm = pl.BlockSpec(memory_space=pltpu.HBM)
    sizes = [high - low for low, high in spans]
    return pl.pallas_call(
        functools.partial(loading_kernel, spans, len(held)),
        in_specs=[in_vmem] + [in_hbm] * len(parts) + [in_vmem] * (len(parts) + len(held)),
        out_specs=[in_vmem] * (1 + len(parts)),
        out_shape=[jax.ShapeDtypeStruct((8, rows), jnp.float32)]
        + [pltpu.VMEM((size, width), jnp.bfloat16) for size in sizes],
        scratch_shapes=[pltpu.SemaphoreType.DMA((size // TILE,)) for size in sizes],
        compiler_params=pltpu.CompilerParams(vmem_limit_bytes=8 * 2**20),
        cost_estimate=pl.CostEstimate(
            flops=5 * sum(sizes) * rows * width, bytes_accessed=0, transcendentals=0
        ),
        name=name,
    )(cand, *docs, *[part[3] for part in parts], *held)


def gain_kernel(count, lows, *refs):
    pieces = refs[:count]
    docs, cws = refs[count : count + len(lows)], refs[count + len(lows) : count + 2 * len(lows)]
    out_ref = refs[count + 2 * len(lows)]
    if count > 1:
        cand = refs[-1]
        pack(pieces, cand)
    else:
        (cand,) = pieces
    out_ref[...] = jnp.zeros_like(out_ref)
    for part, low in enumerate(lows):
        for start in range(0, docs[part].shape[0], TILE):
            add_terms(cand, docs[part], cws[part], out_ref, start, low + start)


def gains_of(pieces, parts, name):
    count = len(pieces)
    rows, width = sum(p.shape[0] for p in pieces), pieces[0].shape[1]
    docs = sum(part[0].shape[0] for part in parts)
    in_vmem = pl.BlockSpec(memory_space=pltpu.VMEM)
    return pl.pallas_call(
        functools.partial(gain_kernel, count, tuple(part[1] for part in parts)),
        in_specs=[in_vmem] * (count + 2 * len(parts)),
        out_specs=in_vmem,
        out_shape=jax.ShapeDtypeStruct((8, rows), jnp.float32),
        scratch_shapes=[pltpu.VMEM((rows, width), jnp.bfloat16)] if count > 1 else [],
        compiler_params=pltpu.CompilerParams(vmem_limit_bytes=8 * 2**20),
        cost_estimate=pl.CostEstimate(flops=5 * docs * rows * width, bytes_accessed=0, transcendentals=0),
        name=name,
    )(*pieces, *[part[0] for part in parts], *[part[2] for part in parts])


def answer_kernel(me, asked, pool_hbm, out_ref, picked, pool, arrived):
    chunks = arrived.shape[0]
    size = pool.shape[0] // chunks
    copies = [
        pltpu.make_async_copy(
            pool_hbm.at[i * size : (i + 1) * size], pool.at[i * size : (i + 1) * size], arrived.at[i]
        )
        for i in range(chunks)
    ]
    for copy in copies:
        copy.start()
    askers = asked.shape[0]
    place_of = lax.broadcasted_iota(jnp.int32, asked.shape[1:], 0) * 65536
    for a in range(askers):
        named = asked[a]
        mine = (named >> 16) == me[0]
        key = place_of + (named & 65535)
        first = jnp.min(jnp.where(mine, key, 2**30), axis=0, keepdims=True)
        last = jnp.max(jnp.where(mine, key, 0), axis=0, keepdims=True)
        picked[2 * a : 2 * a + 1, :] = first & 65535
        picked[2 * a + 1 : 2 * a + 2, :] = last & 65535
    lanes = lax.broadcasted_iota(jnp.int32, picked.shape, 1)
    rows = picked[...]
    onehot = jnp.concatenate(
        [(rows == lanes + base).astype(jnp.float32) for base in range(0, pool.shape[0], 128)], axis=1
    ).astype(jnp.bfloat16)
    for copy in copies:
        copy.wait()
    found = jnp.dot(onehot, pool[...], preferred_element_type=jnp.float32)
    for a in range(askers):
        out_ref[a] = found[2 * a : 2 * a + 2, :].astype(out_ref.dtype)


def answer(me, asked, pool):
    in_vmem = pl.BlockSpec(memory_space=pltpu.VMEM)
    askers, width = asked.shape[0], pool.shape[1]
    return pl.pallas_call(
        answer_kernel,
        in_specs=[pl.BlockSpec(memory_space=pltpu.SMEM), in_vmem, pl.BlockSpec(memory_space=pltpu.HBM)],
        out_specs=in_vmem,
        out_shape=jax.ShapeDtypeStruct((askers, 2, width), pool.dtype),
        scratch_shapes=[
            pltpu.VMEM((2 * askers, 128), jnp.int32),
            pltpu.VMEM(pool.shape, pool.dtype),
            pltpu.SemaphoreType.DMA((4,)),
        ],
        compiler_params=pltpu.CompilerParams(vmem_limit_bytes=10 * 2**20),
        name="answer",
    )(me, asked, pltpu.with_memory_space_constraint(pool, pltpu.HBM))


def body(doc_pool, cand_owner, cand_row, elements, coverage, elem_weight):
    share_len = cand_row.shape[2]
    width = doc_pool.shape[3]
    slab_count = 16
    slot_cap = 2
    pool_local = doc_pool.reshape(doc_pool.shape[2], width)
    owner_ids = cand_owner.reshape(share_len)
    row_ids = cand_row.reshape(share_len)
    docs = elements.reshape(elements.shape[2], width)
    scale_up = float(width) ** 0.5
    element_total = float(docs.shape[0] * 128)
    cw = jnp.stack(
        [coverage.reshape(-1) * scale_up, elem_weight.reshape(-1) * (1.0 / (scale_up * element_total))]
    )
    cw = jnp.pad(cw, ((0, 6), (0, 0)))

    slab, loop = lax.axis_index("slab"), lax.axis_index("loop")
    named = jnp.broadcast_to((owner_ids * 65536 + row_ids)[None, :, None], (slab_count, share_len, 128))
    asked = lax.all_to_all(named, "slab", split_axis=0, concat_axis=0, tiled=True)
    rows_out = answer(slab.reshape(1), asked, pool_local)
    rows_out, owner_ids = lax.optimization_barrier((rows_out, owner_ids))
    fetched = lax.all_to_all(rows_out, "slab", split_axis=0, concat_axis=0, tiled=True)
    positions = jnp.arange(share_len, dtype=jnp.int32)
    same_owner = owner_ids[:, None] == owner_ids[None, :]
    earlier = positions[None, :] < positions[:, None]
    slot_rank = jnp.sum((same_owner & earlier).astype(jnp.int32), axis=1)
    slot_id = owner_ids * slot_cap + slot_rank
    sib_cw = send(cw, {"core": 1})
    fetched, slot_id, outgoing, sib_cw = lax.optimization_barrier((fetched, slot_id, docs, sib_cw))
    own = fetched.reshape(slab_count * slot_cap, width).at[slot_id].get(mode="promise_in_bounds")

    sib_docs = send(outgoing, {"core": 1})
    column, first, last = ("z", "z"), ("x", "y"), ("y", "x")
    own = jnp.concatenate([own] + [along(own, column, -d) for d in (1, 2, 3)], axis=0)
    own = jnp.concatenate([own] + [along(own, first, -d) for d in (1, 2, 3)], axis=0)
    after, before = along(own, last, -1), along(own, last, -3)
    size = docs.shape[0]
    half = size // 2
    ga, own_docs, sib_low = loading_gains(
        own, [(docs, 0, size, cw), (sib_docs, 0, half, sib_cw)], "gains_near"
    )
    outgoing, ga = lax.optimization_barrier((own, ga))
    across = along(outgoing, last, -2)
    outgoing, sib_low = lax.optimization_barrier((outgoing, sib_low))
    gb, sib_high = loading_gains(
        outgoing, [(sib_docs, half, size, sib_cw)], "gains_near_rest", held=(own_docs, sib_low)
    )
    after, before, gb = lax.optimization_barrier((after, before, gb))
    parts = [(own_docs, 0, cw), (sib_low, 0, sib_cw), (sib_high, half, sib_cw)]
    g1 = gains_of([after, before], parts, "gains_next")
    across, g1 = lax.optimization_barrier((across, g1))
    g2 = gains_of([across], parts, "gains_far")
    ga, gb, g1, g2 = lax.optimization_barrier((ga, gb, g1, g2))
    g0, g1, g2 = jnp.sum(ga + gb, axis=0), jnp.sum(g1, axis=0), jnp.sum(g2, axis=0)
    n = own.shape[0]
    gains = jnp.concatenate([g0, g1[:n], g2, g1[n:]]).reshape(64, share_len)

    my_z, my_x, my_y = slab >> 2, (slab & 2) + (loop & 1), loop >> 1
    to = jnp.arange(64, dtype=jnp.int32)
    to_z, to_x, to_y = to >> 4, ((to >> 2) & 2) + (to & 1), (to >> 1) & 3
    to_z, to_x, to_y = (to_z - my_z) & 3, (to_x - my_x) & 3, (to_y - my_y) & 3
    rel = jnp.where(slab & 1 == 0, to_y * 16 + to_x * 4, to_x * 16 + to_y * 4) + to_z
    pick = rel[:, None] == jnp.arange(64, dtype=jnp.int32)[None, :]
    terms = jnp.sum(jnp.where(pick[:, :, None], gains[None, :, :], 0.0), axis=1)
    groups = [[i for i in range(128) if place(i)[3] == core] for core in range(2)]
    terms = lax.all_to_all(terms, AXES, split_axis=0, concat_axis=0, tiled=True, axis_index_groups=groups)
    return jnp.sum(terms, axis=0).reshape(1, 1, share_len)


def solution(mesh):
    placed = (
        P("slab", "loop", None, None),
        P("slab", "loop", None, None),
        P("slab", "loop", None),
        P("slab", "loop", None, None),
        P("slab", "loop", None),
        P("slab", "loop", None),
    )
    return jax.shard_map(
        body, mesh=mesh, in_specs=placed, out_specs=P("slab", "loop", None), check_vma=False
    )
```

time: 121 us -> 111 us (0.917)
  blocking collectives: 30.5 us -> 14.1 us
  waiting for transfers between devices: 21.2 us -> 30.5 us
  Pallas kernels: 33.7 us -> 36.6 us
  local copies, waits for them, and re-layouts: 4.04 us -> 1.86 us
  starting transfers between devices: 25.8 us -> 23.7 us
  other arithmetic: 5.44 us -> 3.93 us
    all_to_all x1 -> x0, blocking collectives: 15.3 us -> none  [body(): lax.all_to_all(requests, 'slab', split_axis=0, concat_axis=0, tiled=True)]
    ppermute x17 -> x11, starting transfers between devices: 22.2 us -> 12.2 us  [send(): return lax.ppermute(value, AXES, moves(*steps))]
    all_to_all x1 -> x2, starting transfers between devices: 3.53 us -> 11.5 us  [the longest x1 7.96 us: body(): lax.all_to_all(named, 'slab', split_axis=0, concat_axis=0, tiled=True)]
    all_to_all x1 -> x2, waiting for transfers between devices: 8.84 us -> 14.4 us  [the longest x1 7.94 us: body(): lax.all_to_all(rows_out, 'slab', split_axis=0, concat_axis=0, tiled=True)]
    ppermute x17 -> x11, waiting for transfers between devices: 12.3 us -> 16.2 us  [send(): return lax.ppermute(value, AXES, moves(*steps))]
    pallas_call x3 -> x5, Pallas kernels: 33.7 us -> 36.6 us  [the longest x2 18.1 us: gains_of(): pl.pallas_call(functools.partial(gain_kernel, count, tuple((part[1] for p...]
  transfers between devices with their start and end apart: 18 -> 13, of which waited for: 10 -> 9; matrix products, arithmetic and copies ran while one was open for 1% -> 3% of each run, Pallas kernels for 19% -> 25%
where the time goes in v3:
time: 111 us
  Pallas kernels  36.6 us (33%)
  waiting for transfers between devices  30.5 us (27%)
  starting transfers between devices  23.7 us (21%)
  blocking collectives  14.1 us (13%)
  other arithmetic  3.93 us (4%)
  local copies, waits for them, and re-layouts  1.86 us (2%)
    pallas_call x2, Pallas kernels, gains_of(): pl.pallas_call(functools.partial(gain_kernel, count, tuple((part[1] for p...  18.1 us
    ppermute x11, waiting for transfers between devices, send(): return lax.ppermute(value, AXES, moves(*steps))  16.2 us
    pallas_call x2, Pallas kernels, loading_gains(): pl.pallas_call(functools.partial(loading_kernel, spans, len(held)), in_sp...  15.8 us
    all_to_all x1, blocking collectives, body(): lax.all_to_all(terms, AXES, split_axis=0, concat_axis=0, tiled=True, axis...  14.1 us
    ppermute x11, starting transfers between devices, send(): return lax.ppermute(value, AXES, moves(*steps))  12.2 us
    all_to_all x1, starting transfers between devices, body(): lax.all_to_all(named, 'slab', split_axis=0, concat_axis=0, tiled=True)  7.96 us
    all_to_all x1, waiting for transfers between devices, body(): lax.all_to_all(rows_out, 'slab', split_axis=0, concat_axis=0, tiled=True)  7.94 us
    all_to_all x1, waiting for transfers between devices, body(): lax.all_to_all(named, 'slab', split_axis=0, concat_axis=0, tiled=True)  6.42 us
  transfers between devices with their start and end apart: 13, of which 9 were waited for; matrix products, arithmetic and copies ran while one was open for 3% of the time, Pallas kernels for 25%

profile of v3, /device:TPU:0, one launch (start us, length us, event | category | flops | bytes accessed | tf_op | source)
XLA Modules:
  0.0 110.9 jit_solution(12451768942645064647)
XLA Ops:
  1.4 8.0 %all-to-all-start = ((s32[16,8,128]{2,1,0:T(8,128)}), s32[16,8,128]{2,1,0:T(8,128)S(1)}, u32[]{:S(2)}, u32[]{:S(2)}) async-start(s32[16,8,128]{2,1,0:T(8,128)} %broadcast_in_dim.18), calls=%async_computation | async-start | bytes 131072 | tf_op jit(solution)/shard_map/all_to_all | solution.py:212
  9.3 0.7 multiply_bitcast_fusion
  10.6 6.4 %all-to-all-done.asked = s32[16,8,128]{2,1,0:T(8,128)S(1)} async-done(((s32[16,8,128]{2,1,0:T(8,128)}), s32[16,8,128]{2,1,0:T(8,128)S(1)}, u32[]{:S(2)}, u32[]{:S(2)}) %all-to-all-start) | async-done | bytes 65568 | tf_op jit(solution)/shard_map/all_to_all | solution.py:212
  17.0 2.7 %answer.1 = bf16[16,2,4096]{2,1,0:T(2,128)(2,1)} custom-call(s32[1]{0:T(128)} %bitcast.me, s32[16,8,128]{2,1,0:T(8,128)S(1)} %all-to-all-done.asked, bf16[256,4096]{1,0:T(8,128)(2,1)} %bitcast.17), custom_call_target="tpu_custom_call" | custom-call | tf_op jit(solution)/shard_map/answer/pallas_call | solution.py:179
  19.7 3.5 %all-to-all-start.1 = ((bf16[16,2,4096]{2,1,0:T(2,128)(2,1)}), bf16[16,2,4096]{2,1,0:T(2,128)(2,1)S(1)}, u32[]{:S(2)}, u32[]{:S(2)}) async-start(bf16[16,2,4096]{2,1,0:T(2,128)(2,1)} %answer.1), calls=%async_computation.1 | async-start | bytes 524288 | tf_op jit(solution)/shard_map/all_to_all | solution.py:215
  23.3 0.9 convert_reduce_fusion
  24.9 7.9 %all-to-all-done.1 = bf16[16,2,4096]{2,1,0:T(2,128)(2,1)S(1)} async-done(((bf16[16,2,4096]{2,1,0:T(2,128)(2,1)}), bf16[16,2,4096]{2,1,0:T(2,128)(2,1)S(1)}, u32[]{:S(2)}, u32[]{:S(2)}) %all-to-all-start.1) | async-done | bytes 262176 | tf_op jit(solution)/shard_map/all_to_all | solution.py:215
  33.5 0.9 collective-permute-start.1
  34.4 1.4 %collective-permute-start.2 = (bf16[8,4096]{1,0:T(8,128)(2,1)S(1)}, bf16[8,4096]{1,0:T(8,128)(2,1)S(1)}, u32[]{:S(2)}, u32[]{:S(2)}) collective-permute-start(bf16[8,4096]{1,0:T(8,128)(2,1)S(1)} %gather_fusion), channel_id=1, source_target_pairs={{0,64},{1,65},{2,66},{3,67},{4,68},{5,69},{6,70},{7,71},{8,72},{9,... | collective-permute-start | bytes 196616 | tf_op jit(solution)/shard_map/ppermute | solution.py:38
  36.1 2.4 %collective-permute-done.1 = bf16[8,4096]{1,0:T(8,128)(2,1)S(1)} collective-permute-done((bf16[8,4096]{1,0:T(8,128)(2,1)S(1)}, bf16[8,4096]{1,0:T(8,128)(2,1)S(1)}, u32[]{:S(2)}, u32[]{:S(2)}) %collective-permute-start.1) | collective-permute-done | bytes 65568 | tf_op jit(solution)/shard_map/ppermute | solution.py:38
  38.5 1.9 %collective-permute-done.2 = bf16[8,4096]{1,0:T(8,128)(2,1)S(1)} collective-permute-done((bf16[8,4096]{1,0:T(8,128)(2,1)S(1)}, bf16[8,4096]{1,0:T(8,128)(2,1)S(1)}, u32[]{:S(2)}, u32[]{:S(2)}) %collective-permute-start.2) | collective-permute-done | bytes 65568 | tf_op jit(solution)/shard_map/ppermute | solution.py:38
  40.4 1.3 %collective-permute-done.3 = bf16[8,4096]{1,0:T(8,128)(2,1)S(1)} collective-permute-done((bf16[8,4096]{1,0:T(8,128)(2,1)S(1)}, bf16[8,4096]{1,0:T(8,128)(2,1)S(1)}, u32[]{:S(2)}, u32[]{:S(2)}) %collective-permute-start.3) | collective-permute-done | bytes 65568 | tf_op jit(solution)/shard_map/ppermute | solution.py:38
  42.1 2.4 %collective-permute-start.5 = (bf16[32,4096]{1,0:T(8,128)(2,1)S(1)}, bf16[32,4096]{1,0:T(8,128)(2,1)S(1)}, u32[]{:S(2)}, u32[]{:S(2)}) collective-permute-start(bf16[32,4096]{1,0:T(8,128)(2,1)S(1)} %get-tuple-element.53), channel_id=1, source_target_pairs={{0,16},{1,17},{2,18},{3,19},{4,20},{5,21},{6,22},{7,23},{8,12},{9,... | collective-permute-start | bytes 786440 | tf_op jit(solution)/shard_map/ppermute | solution.py:38
  44.5 3.6 %collective-permute-done.4 = bf16[32,4096]{1,0:T(8,128)(2,1)S(1)} collective-permute-done((bf16[32,4096]{1,0:T(8,128)(2,1)S(1)}, bf16[32,4096]{1,0:T(8,128)(2,1)S(1)}, u32[]{:S(2)}, u32[]{:S(2)}) %collective-permute-start.4) | collective-permute-done | bytes 262176 | tf_op jit(solution)/shard_map/ppermute | solution.py:38
  48.1 2.0 %collective-permute-done.5 = bf16[32,4096]{1,0:T(8,128)(2,1)S(1)} collective-permute-done((bf16[32,4096]{1,0:T(8,128)(2,1)S(1)}, bf16[32,4096]{1,0:T(8,128)(2,1)S(1)}, u32[]{:S(2)}, u32[]{:S(2)}) %collective-permute-start.5) | collective-permute-done | bytes 262176 | tf_op jit(solution)/shard_map/ppermute | solution.py:38
  50.2 2.7 %collective-permute-done.6 = bf16[32,4096]{1,0:T(8,128)(2,1)S(1)} collective-permute-done((bf16[32,4096]{1,0:T(8,128)(2,1)S(1)}, bf16[32,4096]{1,0:T(8,128)(2,1)S(1)}, u32[]{:S(2)}, u32[]{:S(2)}) %collective-permute-start.6) | collective-permute-done | bytes 262176 | tf_op jit(solution)/shard_map/ppermute | solution.py:38
  52.9 3.1 %collective-permute-start.8 = (bf16[128,4096]{1,0:T(8,128)(2,1)S(1)}, bf16[128,4096]{1,0:T(8,128)(2,1)S(1)}, u32[]{:S(2)}, u32[]{:S(2)}) collective-permute-start(bf16[128,4096]{1,0:T(8,128)(2,1)S(1)} %constant_dynamic-update-slice_fusion.4.refs_0_), channel_id=1, source_target_pairs={{0,6},{1,7},{2,0},{3,1},{4,2},{5,3},{6,4},{7,5},{8,25},{9,8},{10,2... | collective-permute-start | bytes 3145736 | tf_op jit(solution)/shard_map/ppermute | solution.py:38
  56.1 2.2 %collective-permute-done.7.refs_2_.refs_1_ = bf16[2048,4096]{1,0:T(8,128)(2,1)} collective-permute-done((bf16[2048,4096]{1,0:T(8,128)(2,1)}, bf16[2048,4096]{1,0:T(8,128)(2,1)}, u32[]{:S(2)}, u32[]{:S(2)}) %collective-permute-start.7) | collective-permute-done | bytes 16777248 | tf_op jit(solution)/shard_map/ppermute | solution.py:38
  58.3 10.9 %gains_near.1 = (f32[8,128]{1,0:T(8,128)S(1)}, bf16[2048,4096]{1,0:T(8,128)(2,1)S(1)}, bf16[1024,4096]{1,0:T(8,128)(2,1)S(1)}) custom-call(bf16[128,4096]{1,0:T(8,128)(2,1)S(1)} %constant_dynamic-update-slice_fusion.4.refs_0_, bf16[2048,4096]{1,0:T(8,128)(2,1)} %bitcast.16, bf16[2048,4096]{1,0:T(8,128)(2,1)} %collective-permute-done.7.refs_2_.refs_1_, ...), custom_call_target="tpu_custom_call" | custom-call | flops 8053063680 | tf_op jit(solution)/shard_map/gains_near/pallas_call | solution.py:96
  69.2 3.3 %collective-permute-start.10 = (bf16[128,4096]{1,0:T(8,128)(2,1)S(1)}, bf16[128,4096]{1,0:T(8,128)(2,1)S(1)}, u32[]{:S(2)}, u32[]{:S(2)}) collective-permute-start(bf16[128,4096]{1,0:T(8,128)(2,1)S(1)} %constant_dynamic-update-slice_fusion.4.refs_0_), channel_id=1, source_target_pairs={{0,4},{1,5},{2,6},{3,7},{4,0},{5,1},{6,2},{7,3},{8,24},{9,25},{10,... | collective-permute-start | bytes 3145736 | tf_op jit(solution)/shard_map/ppermute | solution.py:38
  72.5 4.9 %gains_near_rest.1 = (f32[8,128]{1,0:T(8,128)S(1)}, bf16[1024,4096]{1,0:T(8,128)(2,1)S(1)}) custom-call(bf16[128,4096]{1,0:T(8,128)(2,1)S(1)} %constant_dynamic-update-slice_fusion.4.refs_0_, bf16[2048,4096]{1,0:T(8,128)(2,1)} %collective-permute-done.7.refs_2_.refs_1_, f32[8,2048]{1,0:T(8,128)S(1)} %collective-permute-done.refs_4_.refs_2_.refs_6_.refs_7_.refs_5_, ...), custom_call_target="tpu_custom_call" | custom-call | flops 2684354560 | tf_op jit(solution)/shard_map/gains_near_rest/pallas_call | solution.py:96
  77.4 9.1 %gains_next.1 = f32[8,256]{1,0:T(8,128)S(1)} custom-call(bf16[128,4096]{1,0:T(8,128)(2,1)S(1)} %collective-permute-done.8.refs_0_, bf16[128,4096]{1,0:T(8,128)(2,1)S(1)} %collective-permute-done.9.refs_1_, bf16[2048,4096]{1,0:T(8,128)(2,1)S(1)} %get-tuple-element.40.refs_3_.refs_2_.refs_1_, bf16[1024,4096]{1,0:T(8,128)(2,1)S(1)} %get-tuple-element.41.refs_4_.refs_3_.refs_2_, ...), custom_call_target="tpu_custom_call" | custom-call | flops 21474836480 | tf_op jit(solution)/shard_map/gains_next/pallas_call | solution.py:131
  86.6 8.9 %gains_far.1 = f32[8,128]{1,0:T(8,128)S(1)} custom-call(bf16[128,4096]{1,0:T(8,128)(2,1)S(1)} %collective-permute-done.10.refs_0_, bf16[2048,4096]{1,0:T(8,128)(2,1)S(1)} %get-tuple-element.40.refs_3_.refs_2_.refs_1_, bf16[1024,4096]{1,0:T(8,128)(2,1)S(1)} %get-tuple-element.41.refs_4_.refs_3_.refs_2_, ...), custom_call_target="tpu_custom_call" | custom-call | flops 10737418240 | tf_op jit(solution)/shard_map/gains_far/pallas_call | solution.py:131
  96.2 14.1 %all_to_all.19 = f32[64,1,8]{2,1,0:T(1,128)S(1)} all-to-all(f32[64,1,8]{2,1,0:T(1,128)S(1)} %bitcast.18), channel_id=1, replica_groups={{0,1,2,3,4,5,6,7,16,17,18,19,20,21,22,23,32,33,34,35,36,37,38,39,48,49,..., dimensions={0} | all-to-all | bytes 4096 | tf_op jit(solution)/shard_map/all_to_all | solution.py:259
  (39 shorter events, 5.3 us)
Async XLA Ops:
  1.4 15.6 %all-to-all-start = ((s32[16,8,128]{2,1,0:T(8,128)}), s32[16,8,128]{2,1,0:T(8,128)S(1)}, u32[]{:S(2)}, u32[]{:S(2)}) async-start(s32[16,8,128]{2,1,0:T(8,128)} %broadcast_in_dim.18), calls=%async_computation | async-start | bytes 131072 | tf_op jit(solution)/shard_map/all_to_all | solution.py:212
  10.1 14.8 %collective-permute-start = (f32[8,2048]{1,0:T(8,128)S(1)}, f32[8,2048]{1,0:T(8,128)S(1)}, u32[]{:S(2)}, u32[]{:S(2)}) collective-permute-start(f32[8,2048]{1,0:T(8,128)S(1)} %select_maximum_fusion.refs_3_.refs_5_.refs_4_), channel_id=1, source_target_pairs={{0,8},{1,9},{2,10},{3,11},{4,12},{5,13},{6,14},{7,15},{8,0},{9,1},... | collective-permute-start | bytes 196616 | tf_op jit(solution)/shard_map/ppermute | solution.py:38
  19.7 13.1 %all-to-all-start.1 = ((bf16[16,2,4096]{2,1,0:T(2,128)(2,1)}), bf16[16,2,4096]{2,1,0:T(2,128)(2,1)S(1)}, u32[]{:S(2)}, u32[]{:S(2)}) async-start(bf16[16,2,4096]{2,1,0:T(2,128)(2,1)} %answer.1), calls=%async_computation.1 | async-start | bytes 524288 | tf_op jit(solution)/shard_map/all_to_all | solution.py:215
  32.8 25.5 %collective-permute-start.7 = (bf16[2048,4096]{1,0:T(8,128)(2,1)}, bf16[2048,4096]{1,0:T(8,128)(2,1)}, u32[]{:S(2)}, u32[]{:S(2)}) collective-permute-start(bf16[2048,4096]{1,0:T(8,128)(2,1)} %bitcast.15), channel_id=1, source_target_pairs={{0,8},{1,9},{2,10},{3,11},{4,12},{5,13},{6,14},{7,15},{8,0},{9,1},... | collective-permute-start | bytes 50331656 | tf_op jit(solution)/shard_map/ppermute | solution.py:38
  33.5 5.0 %collective-permute-start.1 = (bf16[8,4096]{1,0:T(8,128)(2,1)S(1)}, bf16[8,4096]{1,0:T(8,128)(2,1)S(1)}, u32[]{:S(2)}, u32[]{:S(2)}) collective-permute-start(bf16[8,4096]{1,0:T(8,128)(2,1)S(1)} %gather_fusion), channel_id=1, source_target_pairs={{0,96},{1,97},{2,98},{3,99},{4,100},{5,101},{6,102},{7,103},{8,104... | collective-permute-start | bytes 196616 | tf_op jit(solution)/shard_map/ppermute | solution.py:38
  34.4 5.9 %collective-permute-start.2 = (bf16[8,4096]{1,0:T(8,128)(2,1)S(1)}, bf16[8,4096]{1,0:T(8,128)(2,1)S(1)}, u32[]{:S(2)}, u32[]{:S(2)}) collective-permute-start(bf16[8,4096]{1,0:T(8,128)(2,1)S(1)} %gather_fusion), channel_id=1, source_target_pairs={{0,64},{1,65},{2,66},{3,67},{4,68},{5,69},{6,70},{7,71},{8,72},{9,... | collective-permute-start | bytes 196616 | tf_op jit(solution)/shard_map/ppermute | solution.py:38
  35.9 5.8 %collective-permute-start.3 = (bf16[8,4096]{1,0:T(8,128)(2,1)S(1)}, bf16[8,4096]{1,0:T(8,128)(2,1)S(1)}, u32[]{:S(2)}, u32[]{:S(2)}) collective-permute-start(bf16[8,4096]{1,0:T(8,128)(2,1)S(1)} %gather_fusion), channel_id=1, source_target_pairs={{0,32},{1,33},{2,34},{3,35},{4,36},{5,37},{6,38},{7,39},{8,40},{9,... | collective-permute-start | bytes 196616 | tf_op jit(solution)/shard_map/ppermute | solution.py:38
  41.7 6.4 %collective-permute-start.4 = (bf16[32,4096]{1,0:T(8,128)(2,1)S(1)}, bf16[32,4096]{1,0:T(8,128)(2,1)S(1)}, u32[]{:S(2)}, u32[]{:S(2)}) collective-permute-start(bf16[32,4096]{1,0:T(8,128)(2,1)S(1)} %get-tuple-element.53), channel_id=1, source_target_pairs={{0,17},{1,0},{2,19},{3,2},{4,21},{5,4},{6,23},{7,6},{8,14},{9,15},... | collective-permute-start | bytes 786440 | tf_op jit(solution)/shard_map/ppermute | solution.py:38
  42.1 8.0 %collective-permute-start.5 = (bf16[32,4096]{1,0:T(8,128)(2,1)S(1)}, bf16[32,4096]{1,0:T(8,128)(2,1)S(1)}, u32[]{:S(2)}, u32[]{:S(2)}) collective-permute-start(bf16[32,4096]{1,0:T(8,128)(2,1)S(1)} %get-tuple-element.53), channel_id=1, source_target_pairs={{0,16},{1,17},{2,18},{3,19},{4,20},{5,21},{6,22},{7,23},{8,12},{9,... | collective-permute-start | bytes 786440 | tf_op jit(solution)/shard_map/ppermute | solution.py:38
  44.5 8.4 %collective-permute-start.6 = (bf16[32,4096]{1,0:T(8,128)(2,1)S(1)}, bf16[32,4096]{1,0:T(8,128)(2,1)S(1)}, u32[]{:S(2)}, u32[]{:S(2)}) collective-permute-start(bf16[32,4096]{1,0:T(8,128)(2,1)S(1)} %get-tuple-element.53), channel_id=1, source_target_pairs={{0,1},{1,16},{2,3},{3,18},{4,5},{5,20},{6,7},{7,22},{8,10},{9,11},... | collective-permute-start | bytes 786440 | tf_op jit(solution)/shard_map/ppermute | solution.py:38
  52.9 24.5 %collective-permute-start.8 = (bf16[128,4096]{1,0:T(8,128)(2,1)S(1)}, bf16[128,4096]{1,0:T(8,128)(2,1)S(1)}, u32[]{:S(2)}, u32[]{:S(2)}) collective-permute-start(bf16[128,4096]{1,0:T(8,128)(2,1)S(1)} %constant_dynamic-update-slice_fusion.4.refs_0_), channel_id=1, source_target_pairs={{0,6},{1,7},{2,0},{3,1},{4,2},{5,3},{6,4},{7,5},{8,25},{9,8},{10,2... | collective-permute-start | bytes 3145736 | tf_op jit(solution)/shard_map/ppermute | solution.py:38
  56.0 21.4 %collective-permute-start.9 = (bf16[128,4096]{1,0:T(8,128)(2,1)S(1)}, bf16[128,4096]{1,0:T(8,128)(2,1)S(1)}, u32[]{:S(2)}, u32[]{:S(2)}) collective-permute-start(bf16[128,4096]{1,0:T(8,128)(2,1)S(1)} %constant_dynamic-update-slice_fusion.4.refs_0_), channel_id=1, source_target_pairs={{0,2},{1,3},{2,4},{3,5},{4,6},{5,7},{6,0},{7,1},{8,9},{9,24},{10,1... | collective-permute-start | bytes 3145736 | tf_op jit(solution)/shard_map/ppermute | solution.py:38
  69.2 17.4 %collective-permute-start.10 = (bf16[128,4096]{1,0:T(8,128)(2,1)S(1)}, bf16[128,4096]{1,0:T(8,128)(2,1)S(1)}, u32[]{:S(2)}, u32[]{:S(2)}) collective-permute-start(bf16[128,4096]{1,0:T(8,128)(2,1)S(1)} %constant_dynamic-update-slice_fusion.4.refs_0_), channel_id=1, source_target_pairs={{0,4},{1,5},{2,6},{3,7},{4,0},{5,1},{6,2},{7,3},{8,24},{9,25},{10,... | collective-permute-start | bytes 3145736 | tf_op jit(solution)/shard_map/ppermute | solution.py:38

commit v4 on v3

--- a/solution.py
+++ b/solution.py
@@ -10,6 +10,8 @@
 AXES = ("slab", "loop")
 RING = 4
 TILE = 512
+LOAD_TILE = 256
+AHEAD = 3
 
 
 def place(index):
@@ -42,13 +44,13 @@
     return send(value, *({axis: distance} for axis in axes))
 
 
-def add_terms(cand, docs, cw, out_ref, start, doc_at):
+def add_terms(cand, docs, cw, out_ref, start, doc_at, tile=TILE):
     scores = lax.dot_general(
-        docs[pl.ds(start, TILE), :], cand[...], (((1,), (1,)), ((), ())), preferred_element_type=jnp.float32
-    )
-    columns = cw[:, pl.ds(doc_at, TILE)].T
+        docs[pl.ds(start, tile), :], cand[...], (((1,), (1,)), ((), ())), preferred_element_type=jnp.float32
+    )
+    columns = cw[:, pl.ds(doc_at, tile)].T
     term = columns[:, 1:2] * jnp.maximum(scores - columns[:, 0:1], 0.0)
-    out_ref[...] += jnp.sum(term.reshape(TILE // 8, 8, term.shape[1]), axis=0)
+    out_ref[...] += jnp.sum(term.reshape(tile // 8, 8, term.shape[1]), axis=0)
 
 
 def pack(pieces, cand):
@@ -59,53 +61,73 @@
         at += rows
 
 
-def loading_kernel(spans, held, *refs):
-    count = len(spans)
-    cand, sources, cws = refs[0], refs[1 : 1 + count], refs[1 + count : 1 + 2 * count]
-    outs = refs[1 + 2 * count + held :]
-    out_ref, loaded, arrived = outs[0], outs[1 : 1 + count], outs[1 + count :]
-
-    def copy(part, i):
-        low = spans[part][0]
-        here = pl.ds(pl.multiple_of(i * TILE, TILE), TILE)
-        there = pl.ds(pl.multiple_of(low + i * TILE, TILE), TILE)
-        return pltpu.make_async_copy(sources[part].at[there], loaded[part].at[here], arrived[part].at[i])
-
-    for part, (low, high) in enumerate(spans):
-        for i in range((high - low) // TILE):
-            copy(part, i).start()
+def load_kernel(docs_hbm, after, docs, arrived):
+    size = docs.shape[0] // arrived.shape[0]
+    copies = [
+        pltpu.make_async_copy(
+            docs_hbm.at[i * size : (i + 1) * size], docs.at[i * size : (i + 1) * size], arrived.at[i]
+        )
+        for i in range(arrived.shape[0])
+    ]
+    for copy in copies:
+        copy.start()
+    for copy in copies:
+        copy.wait()
+
+
+def load(docs, after, name):
+    return pl.pallas_call(
+        load_kernel,
+        in_specs=[pl.BlockSpec(memory_space=pltpu.HBM), pl.BlockSpec(memory_space=pltpu.VMEM)],
+        out_specs=pl.BlockSpec(memory_space=pltpu.VMEM),
+        out_shape=pltpu.VMEM(docs.shape, docs.dtype),
+        scratch_shapes=[pltpu.SemaphoreType.DMA((4,))],
+        compiler_params=pltpu.CompilerParams(vmem_limit_bytes=2 * 2**20),
+        cost_estimate=pl.CostEstimate(flops=0, bytes_accessed=docs.size * 2, transcendentals=0),
+        name=name,
+    )(pltpu.with_memory_space_constraint(docs, pltpu.HBM), after)
+
+
+def loading_kernel(cand, docs_hbm, cw, *refs):
+    out_ref, docs, arrived = refs[-3:]
+    steps = docs_hbm.shape[0] // LOAD_TILE
+
+    def copy(i):
+        rows = pl.ds(pl.multiple_of(i * LOAD_TILE, LOAD_TILE), LOAD_TILE)
+        return pltpu.make_async_copy(docs_hbm.at[rows], docs.at[rows], arrived.at[i])
+
+    for i in range(AHEAD):
+        copy(i).start()
     out_ref[...] = jnp.zeros_like(out_ref)
-    for part, (low, high) in enumerate(spans):
-
-        def step(i, carry, part=part, low=low):
-            copy(part, i).wait()
-            start = pl.multiple_of(i * TILE, TILE)
-            add_terms(cand, loaded[part], cws[part], out_ref, start, pl.multiple_of(low + start, TILE))
-            return carry
-
-        lax.fori_loop(0, (high - low) // TILE, step, 0)
-
-
-def loading_gains(cand, parts, name, held=()):
+
+    def step(i, carry):
+        @pl.when(i + AHEAD < steps)
+        def _():
+            copy(i + AHEAD).start()
+
+        copy(i).wait()
+        start = pl.multiple_of(i * LOAD_TILE, LOAD_TILE)
+        add_terms(cand, docs, cw, out_ref, start, start, LOAD_TILE)
+        return carry
+
+    lax.fori_loop(0, steps, step, 0)
+
+
+def loading_gains(cand, docs, cw, name, held=()):
     rows, width = cand.shape
-    spans = tuple((low, high) for _, low, high, _ in parts)
-    docs = [pltpu.with_memory_space_constraint(part[0], pltpu.HBM) for part in parts]
     in_vmem = pl.BlockSpec(memory_space=pltpu.VMEM)
-    in_hbm = pl.BlockSpec(memory_space=pltpu.HBM)
-    sizes = [high - low for low, high in spans]
-    return pl.pallas_call(
-        functools.partial(loading_kernel, spans, len(held)),
-        in_specs=[in_vmem] + [in_hbm] * len(parts) + [in_vmem] * (len(parts) + len(held)),
-        out_specs=[in_vmem] * (1 + len(parts)),
-        out_shape=[jax.ShapeDtypeStruct((8, rows), jnp.float32)]
-        + [pltpu.VMEM((size, width), jnp.bfloat16) for size in sizes],
-        scratch_shapes=[pltpu.SemaphoreType.DMA((size // TILE,)) for size in sizes],
+    return pl.pallas_call(
+        loading_kernel,
+        in_specs=[in_vmem, pl.BlockSpec(memory_space=pltpu.HBM), in_vmem] + [in_vmem] * len(held),
+        out_specs=[in_vmem] * 2,
+        out_shape=[jax.ShapeDtypeStruct((8, rows), jnp.float32), pltpu.VMEM(docs.shape, docs.dtype)],
+        scratch_shapes=[pltpu.SemaphoreType.DMA((docs.shape[0] // LOAD_TILE,))],
         compiler_params=pltpu.CompilerParams(vmem_limit_bytes=8 * 2**20),
         cost_estimate=pl.CostEstimate(
-            flops=5 * sum(sizes) * rows * width, bytes_accessed=0, transcendentals=0
+            flops=5 * docs.shape[0] * rows * width, bytes_accessed=0, transcendentals=0
         ),
         name=name,
-    )(cand, *docs, *[part[3] for part in parts], *held)
+    )(cand, pltpu.with_memory_space_constraint(docs, pltpu.HBM), cw, *held)
 
 
 def gain_kernel(count, lows, *refs):
@@ -140,17 +162,7 @@
     )(*pieces, *[part[0] for part in parts], *[part[2] for part in parts])
 
 
-def answer_kernel(me, asked, pool_hbm, out_ref, picked, pool, arrived):
-    chunks = arrived.shape[0]
-    size = pool.shape[0] // chunks
-    copies = [
-        pltpu.make_async_copy(
-            pool_hbm.at[i * size : (i + 1) * size], pool.at[i * size : (i + 1) * size], arrived.at[i]
-        )
-        for i in range(chunks)
-    ]
-    for copy in copies:
-        copy.start()
+def answer_kernel(me, asked, pool, out_ref, picked):
     askers = asked.shape[0]
     place_of = lax.broadcasted_iota(jnp.int32, asked.shape[1:], 0) * 65536
     for a in range(askers):
@@ -166,8 +178,6 @@
     onehot = jnp.concatenate(
         [(rows == lanes + base).astype(jnp.float32) for base in range(0, pool.shape[0], 128)], axis=1
     ).astype(jnp.bfloat16)
-    for copy in copies:
-        copy.wait()
     found = jnp.dot(onehot, pool[...], preferred_element_type=jnp.float32)
     for a in range(askers):
         out_ref[a] = found[2 * a : 2 * a + 2, :].astype(out_ref.dtype)
@@ -178,17 +188,13 @@
     askers, width = asked.shape[0], pool.shape[1]
     return pl.pallas_call(
         answer_kernel,
-        in_specs=[pl.BlockSpec(memory_space=pltpu.SMEM), in_vmem, pl.BlockSpec(memory_space=pltpu.HBM)],
+        in_specs=[pl.BlockSpec(memory_space=pltpu.SMEM), in_vmem, in_vmem],
         out_specs=in_vmem,
         out_shape=jax.ShapeDtypeStruct((askers, 2, width), pool.dtype),
-        scratch_shapes=[
-            pltpu.VMEM((2 * askers, 128), jnp.int32),
-            pltpu.VMEM(pool.shape, pool.dtype),
-            pltpu.SemaphoreType.DMA((4,)),
-        ],
+        scratch_shapes=[pltpu.VMEM((2 * askers, 128), jnp.int32)],
         compiler_params=pltpu.CompilerParams(vmem_limit_bytes=10 * 2**20),
         name="answer",
-    )(me, asked, pltpu.with_memory_space_constraint(pool, pltpu.HBM))
+    )(me, asked, pool)
 
 
 def body(doc_pool, cand_owner, cand_row, elements, coverage, elem_weight):
@@ -210,7 +216,7 @@
     slab, loop = lax.axis_index("slab"), lax.axis_index("loop")
     named = jnp.broadcast_to((owner_ids * 65536 + row_ids)[None, :, None], (slab_count, share_len, 128))
     asked = lax.all_to_all(named, "slab", split_axis=0, concat_axis=0, tiled=True)
-    rows_out = answer(slab.reshape(1), asked, pool_local)
+    rows_out = answer(slab.reshape(1), asked, load(pool_local, cw, "load_pool"))
     rows_out, owner_ids = lax.optimization_barrier((rows_out, owner_ids))
     fetched = lax.all_to_all(rows_out, "slab", split_axis=0, concat_axis=0, tiled=True)
     positions = jnp.arange(share_len, dtype=jnp.int32)
@@ -225,24 +231,21 @@
     sib_docs = send(outgoing, {"core": 1})
     column, first, last = ("z", "z"), ("x", "y"), ("y", "x")
     own = jnp.concatenate([own] + [along(own, column, -d) for d in (1, 2, 3)], axis=0)
-    own = jnp.concatenate([own] + [along(own, first, -d) for d in (1, 2, 3)], axis=0)
+    beside = [along(own, first, -d) for d in (1, 2, 3)]
+    own_docs = load(docs, own, "load_own")
+    own, own_docs, *beside = lax.optimization_barrier((own, own_docs, *beside))
+    own = jnp.concatenate([own] + beside, axis=0)
     after, before = along(own, last, -1), along(own, last, -3)
-    size = docs.shape[0]
-    half = size // 2
-    ga, own_docs, sib_low = loading_gains(
-        own, [(docs, 0, size, cw), (sib_docs, 0, half, sib_cw)], "gains_near"
-    )
-    outgoing, ga = lax.optimization_barrier((own, ga))
-    across = along(outgoing, last, -2)
-    outgoing, sib_low = lax.optimization_barrier((outgoing, sib_low))
-    gb, sib_high = loading_gains(
-        outgoing, [(sib_docs, half, size, sib_cw)], "gains_near_rest", held=(own_docs, sib_low)
-    )
+    ga = gains_of([own], [(own_docs, 0, cw)], "gains_near_own")
+    sib_docs, ga = lax.optimization_barrier((sib_docs, ga))
+    gb, sib_docs = loading_gains(own, sib_docs, sib_cw, "gains_near_sib", held=(own_docs,))
     after, before, gb = lax.optimization_barrier((after, before, gb))
-    parts = [(own_docs, 0, cw), (sib_low, 0, sib_cw), (sib_high, half, sib_cw)]
+    half = own.shape[0] // 2
+    across = [along(after[:half], last, -1), along(before[half:], last, -3)]
+    parts = [(own_docs, 0, cw), (sib_docs, 0, sib_cw)]
     g1 = gains_of([after, before], parts, "gains_next")
-    across, g1 = lax.optimization_barrier((across, g1))
-    g2 = gains_of([across], parts, "gains_far")
+    *across, g1 = lax.optimization_barrier((*across, g1))
+    g2 = gains_of(across, parts, "gains_far")
     ga, gb, g1, g2 = lax.optimization_barrier((ga, gb, g1, g2))
     g0, g1, g2 = jnp.sum(ga + gb, axis=0), jnp.sum(g1, axis=0), jnp.sum(g2, axis=0)
     n = own.shape[0]

time: 111 us -> 107 us (0.964)
  waiting for transfers between devices: 30.5 us -> 24.8 us
  Pallas kernels: 36.6 us -> 38.7 us
  starting transfers between devices: 23.7 us -> 22.5 us
    pallas_call x2 -> x3, Pallas kernels: 18.1 us -> 22.7 us  [gains_of(): pl.pallas_call(functools.partial(gain_kernel, count, tuple((part[1] for p...]
    ppermute x11 -> x12, waiting for transfers between devices: 16.2 us -> 12 us  [send(): return lax.ppermute(value, AXES, moves(*steps))]
    all_to_all x1, waiting for transfers between devices: 6.42 us -> 4.86 us  [body(): lax.all_to_all(named, 'slab', split_axis=0, concat_axis=0, tiled=True)]
    pallas_call x1, Pallas kernels: 2.73 us -> 1.2 us  [answer(): pl.pallas_call(answer_kernel, in_specs=[pl.BlockSpec(memory_space=pltpu.S...]
    ppermute x11 -> x12, starting transfers between devices: 12.2 us -> 11 us  [send(): return lax.ppermute(value, AXES, moves(*steps))]
    pallas_call x2 -> x3, Pallas kernels: 15.8 us -> 14.8 us  [the longest x2 7.44 us: load(): pl.pallas_call(load_kernel, in_specs=[pl.BlockSpec(memory_space=pltpu.HBM...]
  transfers between devices with their start and end apart: 13 -> 14, of which waited for: 9 -> 8; matrix products, arithmetic and copies ran while one was open for 3% -> 3% of each run, Pallas kernels for 25% -> 28%
where the time goes in v4:
time: 107 us
  Pallas kernels  38.7 us (36%)
  waiting for transfers between devices  24.8 us (23%)
  starting transfers between devices  22.5 us (21%)
  blocking collectives  14.9 us (14%)
  other arithmetic  3.93 us (4%)
  local copies, waits for them, and re-layouts  1.93 us (2%)
    pallas_call x3, Pallas kernels, gains_of(): pl.pallas_call(functools.partial(gain_kernel, count, tuple((part[1] for p...  22.7 us
    all_to_all x1, blocking collectives, body(): lax.all_to_all(terms, AXES, split_axis=0, concat_axis=0, tiled=True, axis...  14.9 us
    ppermute x12, waiting for transfers between devices, send(): return lax.ppermute(value, AXES, moves(*steps))  12 us
    ppermute x12, starting transfers between devices, send(): return lax.ppermute(value, AXES, moves(*steps))  11 us
    all_to_all x1, starting transfers between devices, body(): lax.all_to_all(named, 'slab', split_axis=0, concat_axis=0, tiled=True)  7.96 us
    all_to_all x1, waiting for transfers between devices, body(): lax.all_to_all(rows_out, 'slab', split_axis=0, concat_axis=0, tiled=True)  7.94 us
    pallas_call x2, Pallas kernels, load(): pl.pallas_call(load_kernel, in_specs=[pl.BlockSpec(memory_space=pltpu.HBM...  7.44 us
    pallas_call x1, Pallas kernels, loading_gains(): pl.pallas_call(loading_kernel, in_specs=[in_vmem, pl.BlockSpec(memory_spa...  7.39 us
  transfers between devices with their start and end apart: 14, of which 8 were waited for; matrix products, arithmetic and copies ran while one was open for 3% of the time, Pallas kernels for 28%

profile of v4, /device:TPU:0, one launch (start us, length us, event | category | flops | bytes accessed | tf_op | source)
XLA Modules:
  0.0 106.9 jit_solution(18064579295561700861)
XLA Ops:
  1.4 8.0 %all-to-all-start = ((s32[16,8,128]{2,1,0:T(8,128)}), s32[16,8,128]{2,1,0:T(8,128)S(1)}, u32[]{:S(2)}, u32[]{:S(2)}) async-start(s32[16,8,128]{2,1,0:T(8,128)} %broadcast_in_dim.18), calls=%async_computation | async-start | bytes 131072 | tf_op jit(solution)/shard_map/all_to_all | solution.py:218
  9.3 0.7 multiply_bitcast_fusion
  10.6 1.5 %load_pool.1.pool = bf16[256,4096]{1,0:T(8,128)(2,1)S(1)} custom-call(bf16[256,4096]{1,0:T(8,128)(2,1)} %bitcast.17, f32[8,2048]{1,0:T(8,128)S(1)} %select_maximum_fusion.after.refs_2_.refs_4_), custom_call_target="tpu_custom_call" | custom-call | bytes 2097152 | tf_op jit(solution)/shard_map/load_pool/pallas_call | solution.py:79
  12.1 4.9 %all-to-all-done.asked = s32[16,8,128]{2,1,0:T(8,128)S(1)} async-done(((s32[16,8,128]{2,1,0:T(8,128)}), s32[16,8,128]{2,1,0:T(8,128)S(1)}, u32[]{:S(2)}, u32[]{:S(2)}) %all-to-all-start) | async-done | bytes 65568 | tf_op jit(solution)/shard_map/all_to_all | solution.py:218
  17.0 1.2 %answer.1 = bf16[16,2,4096]{2,1,0:T(2,128)(2,1)} custom-call(s32[1]{0:T(128)} %bitcast.me, s32[16,8,128]{2,1,0:T(8,128)S(1)} %all-to-all-done.asked, bf16[256,4096]{1,0:T(8,128)(2,1)S(1)} %load_pool.1.pool), custom_call_target="tpu_custom_call" | custom-call | tf_op jit(solution)/shard_map/answer/pallas_call | solution.py:189
  18.2 3.5 %all-to-all-start.1 = ((bf16[16,2,4096]{2,1,0:T(2,128)(2,1)}), bf16[16,2,4096]{2,1,0:T(2,128)(2,1)S(1)}, u32[]{:S(2)}, u32[]{:S(2)}) async-start(bf16[16,2,4096]{2,1,0:T(2,128)(2,1)} %answer.1), calls=%async_computation.1 | async-start | bytes 524288 | tf_op jit(solution)/shard_map/all_to_all | solution.py:221
  21.7 0.9 convert_reduce_fusion
  23.3 7.9 %all-to-all-done.1 = bf16[16,2,4096]{2,1,0:T(2,128)(2,1)S(1)} async-done(((bf16[16,2,4096]{2,1,0:T(2,128)(2,1)}), bf16[16,2,4096]{2,1,0:T(2,128)(2,1)S(1)}, u32[]{:S(2)}, u32[]{:S(2)}) %all-to-all-start.1) | async-done | bytes 262176 | tf_op jit(solution)/shard_map/all_to_all | solution.py:221
  32.0 0.9 collective-permute-start.2
  32.9 1.3 %collective-permute-start.3 = (bf16[8,4096]{1,0:T(8,128)(2,1)S(1)}, bf16[8,4096]{1,0:T(8,128)(2,1)S(1)}, u32[]{:S(2)}, u32[]{:S(2)}) collective-permute-start(bf16[8,4096]{1,0:T(8,128)(2,1)S(1)} %gather_fusion), channel_id=1, source_target_pairs={{0,64},{1,65},{2,66},{3,67},{4,68},{5,69},{6,70},{7,71},{8,72},{9,... | collective-permute-start | bytes 196616 | tf_op jit(solution)/shard_map/ppermute | solution.py:40
  34.4 2.5 %collective-permute-done.2 = bf16[8,4096]{1,0:T(8,128)(2,1)S(1)} collective-permute-done((bf16[8,4096]{1,0:T(8,128)(2,1)S(1)}, bf16[8,4096]{1,0:T(8,128)(2,1)S(1)}, u32[]{:S(2)}, u32[]{:S(2)}) %collective-permute-start.2) | collective-permute-done | bytes 65568 | tf_op jit(solution)/shard_map/ppermute | solution.py:40
  36.9 1.8 %collective-permute-done.3 = bf16[8,4096]{1,0:T(8,128)(2,1)S(1)} collective-permute-done((bf16[8,4096]{1,0:T(8,128)(2,1)S(1)}, bf16[8,4096]{1,0:T(8,128)(2,1)S(1)}, u32[]{:S(2)}, u32[]{:S(2)}) %collective-permute-start.3) | collective-permute-done | bytes 65568 | tf_op jit(solution)/shard_map/ppermute | solution.py:40
  38.7 1.3 %collective-permute-done.4 = bf16[8,4096]{1,0:T(8,128)(2,1)S(1)} collective-permute-done((bf16[8,4096]{1,0:T(8,128)(2,1)S(1)}, bf16[8,4096]{1,0:T(8,128)(2,1)S(1)}, u32[]{:S(2)}, u32[]{:S(2)}) %collective-permute-start.4) | collective-permute-done | bytes 65568 | tf_op jit(solution)/shard_map/ppermute | solution.py:40
  40.4 2.3 %collective-permute-start.6 = (bf16[32,4096]{1,0:T(8,128)(2,1)S(1)}, bf16[32,4096]{1,0:T(8,128)(2,1)S(1)}, u32[]{:S(2)}, u32[]{:S(2)}) collective-permute-start(bf16[32,4096]{1,0:T(8,128)(2,1)S(1)} %constant_dynamic-update-slice_fusion.after), channel_id=1, source_target_pairs={{0,16},{1,17},{2,18},{3,19},{4,20},{5,21},{6,22},{7,23},{8,12},{9,... | collective-permute-start | bytes 786440 | tf_op jit(solution)/shard_map/ppermute | solution.py:40
  42.7 5.9 %load_own.1.refs_1_.refs_0_.refs_2_ = bf16[2048,4096]{1,0:T(8,128)(2,1)S(1)} custom-call(bf16[2048,4096]{1,0:T(8,128)(2,1)} %bitcast.16, bf16[32,4096]{1,0:T(8,128)(2,1)S(1)} %constant_dynamic-update-slice_fusion.after), custom_call_target="tpu_custom_call" | custom-call | bytes 16777216 | tf_op jit(solution)/shard_map/load_own/pallas_call | solution.py:79
  48.6 2.5 %collective-permute-done.7 = bf16[32,4096]{1,0:T(8,128)(2,1)S(1)} collective-permute-done((bf16[32,4096]{1,0:T(8,128)(2,1)S(1)}, bf16[32,4096]{1,0:T(8,128)(2,1)S(1)}, u32[]{:S(2)}, u32[]{:S(2)}) %collective-permute-start.7) | collective-permute-done | bytes 262176 | tf_op jit(solution)/shard_map/ppermute | solution.py:40
  51.2 3.1 %collective-permute-start.8 = (bf16[128,4096]{1,0:T(8,128)(2,1)S(1)}, bf16[128,4096]{1,0:T(8,128)(2,1)S(1)}, u32[]{:S(2)}, u32[]{:S(2)}) collective-permute-start(bf16[128,4096]{1,0:T(8,128)(2,1)S(1)} %constant_dynamic-update-slice_fusion.4.refs_0_.cand), channel_id=1, source_target_pairs={{0,6},{1,7},{2,0},{3,1},{4,2},{5,3},{6,4},{7,5},{8,25},{9,8},{10,2... | collective-permute-start | bytes 3145736 | tf_op jit(solution)/shard_map/ppermute | solution.py:40
  54.4 4.6 %gains_near_own.1 = f32[8,128]{1,0:T(8,128)S(1)} custom-call(bf16[128,4096]{1,0:T(8,128)(2,1)S(1)} %constant_dynamic-update-slice_fusion.4.refs_0_.cand, bf16[2048,4096]{1,0:T(8,128)(2,1)S(1)} %load_own.1.refs_1_.refs_0_.refs_2_, f32[8,2048]{1,0:T(8,128)S(1)} %select_maximum_fusion.after.refs_2_.refs_4_), custom_call_target="tpu_custom_call" | custom-call | flops 5368709120 | tf_op jit(solution)/shard_map/gains_near_own/pallas_call | solution.py:153
  59.0 7.4 %gains_near_sib.1 = (f32[8,128]{1,0:T(8,128)S(1)}, bf16[2048,4096]{1,0:T(8,128)(2,1)S(1)}) custom-call(bf16[128,4096]{1,0:T(8,128)(2,1)S(1)} %constant_dynamic-update-slice_fusion.4.refs_0_.cand, bf16[2048,4096]{1,0:T(8,128)(2,1)} %collective-permute-done.1.docs_hbm, f32[8,2048]{1,0:T(8,128)S(1)} %collective-permute-done.cw.refs_5_, ...), custom_call_target="tpu_custom_call" | custom-call | flops 5368709120 | tf_op jit(solution)/shard_map/gains_near_sib/pallas_call | solution.py:119
  66.6 3.7 %collective-permute-done.9.refs_1_ = bf16[128,4096]{1,0:T(8,128)(2,1)S(1)} collective-permute-done((bf16[128,4096]{1,0:T(8,128)(2,1)S(1)}, bf16[128,4096]{1,0:T(8,128)(2,1)S(1)}, u32[]{:S(2)}, u32[]{:S(2)}) %collective-permute-start.9) | collective-permute-done | bytes 1048608 | tf_op jit(solution)/shard_map/ppermute | solution.py:40
  70.5 2.3 %collective-permute-start.11 = (bf16[64,4096]{1,0:T(8,128)(2,1)S(1)}, bf16[64,4096]{1,0:T(8,128)(2,1)S(1)}, u32[]{:S(2)}, u32[]{:S(2)}) collective-permute-start(bf16[64,4096]{1,0:T(8,128)(2,1)S(1)} %slice.23), channel_id=1, source_target_pairs={{0,2},{1,3},{2,4},{3,5},{4,6},{5,7},{6,0},{7,1},{8,9},{9,24},{10,1... | collective-permute-start | bytes 1572872 | tf_op jit(solution)/shard_map/ppermute | solution.py:40
  72.7 9.1 %gains_next.1 = f32[8,256]{1,0:T(8,128)S(1)} custom-call(bf16[128,4096]{1,0:T(8,128)(2,1)S(1)} %collective-permute-done.8.refs_0_, bf16[128,4096]{1,0:T(8,128)(2,1)S(1)} %collective-permute-done.9.refs_1_, bf16[2048,4096]{1,0:T(8,128)(2,1)S(1)} %load_own.1.refs_1_.refs_0_.refs_2_, bf16[2048,4096]{1,0:T(8,128)(2,1)S(1)} %get-tuple-element.47.refs_3_, ...), custom_call_target="tpu_custom_call" | custom-call | flops 21474836480 | tf_op jit(solution)/shard_map/gains_next/pallas_call | solution.py:153
  81.8 9.0 %gains_far.1 = f32[8,128]{1,0:T(8,128)S(1)} custom-call(bf16[64,4096]{1,0:T(8,128)(2,1)S(1)} %collective-permute-done.10.refs_0_, bf16[64,4096]{1,0:T(8,128)(2,1)S(1)} %collective-permute-done.11.refs_1_, bf16[2048,4096]{1,0:T(8,128)(2,1)S(1)} %load_own.1.refs_1_.refs_0_.refs_2_, bf16[2048,4096]{1,0:T(8,128)(2,1)S(1)} %get-tuple-element.47.refs_3_, ...), custom_call_target="tpu_custom_call" | custom-call | flops 10737418240 | tf_op jit(solution)/shard_map/gains_far/pallas_call | solution.py:153
  91.5 14.9 %all_to_all.19 = f32[64,1,8]{2,1,0:T(1,128)S(1)} all-to-all(f32[64,1,8]{2,1,0:T(1,128)S(1)} %bitcast.18), channel_id=1, replica_groups={{0,1,2,3,4,5,6,7,16,17,18,19,20,21,22,23,32,33,34,35,36,37,38,39,48,49,..., dimensions={0} | all-to-all | bytes 4096 | tf_op jit(solution)/shard_map/all_to_all | solution.py:262
  (46 shorter events, 5.6 us)
Async XLA Ops:
  1.4 15.6 %all-to-all-start = ((s32[16,8,128]{2,1,0:T(8,128)}), s32[16,8,128]{2,1,0:T(8,128)S(1)}, u32[]{:S(2)}, u32[]{:S(2)}) async-start(s32[16,8,128]{2,1,0:T(8,128)} %broadcast_in_dim.18), calls=%async_computation | async-start | bytes 131072 | tf_op jit(solution)/shard_map/all_to_all | solution.py:218
  10.1 13.2 %collective-permute-start = (f32[8,2048]{1,0:T(8,128)S(1)}, f32[8,2048]{1,0:T(8,128)S(1)}, u32[]{:S(2)}, u32[]{:S(2)}) collective-permute-start(f32[8,2048]{1,0:T(8,128)S(1)} %select_maximum_fusion.after.refs_2_.refs_4_), channel_id=1, source_target_pairs={{0,8},{1,9},{2,10},{3,11},{4,12},{5,13},{6,14},{7,15},{8,0},{9,1},... | collective-permute-start | bytes 196616 | tf_op jit(solution)/shard_map/ppermute | solution.py:40
  18.2 13.1 %all-to-all-start.1 = ((bf16[16,2,4096]{2,1,0:T(2,128)(2,1)}), bf16[16,2,4096]{2,1,0:T(2,128)(2,1)S(1)}, u32[]{:S(2)}, u32[]{:S(2)}) async-start(bf16[16,2,4096]{2,1,0:T(2,128)(2,1)} %answer.1), calls=%async_computation.1 | async-start | bytes 524288 | tf_op jit(solution)/shard_map/all_to_all | solution.py:221
  31.3 27.7 %collective-permute-start.1 = (bf16[2048,4096]{1,0:T(8,128)(2,1)}, bf16[2048,4096]{1,0:T(8,128)(2,1)}, u32[]{:S(2)}, u32[]{:S(2)}) collective-permute-start(bf16[2048,4096]{1,0:T(8,128)(2,1)} %bitcast.15), channel_id=1, source_target_pairs={{0,8},{1,9},{2,10},{3,11},{4,12},{5,13},{6,14},{7,15},{8,0},{9,1},... | collective-permute-start | bytes 50331656 | tf_op jit(solution)/shard_map/ppermute | solution.py:40
  32.0 5.0 %collective-permute-start.2 = (bf16[8,4096]{1,0:T(8,128)(2,1)S(1)}, bf16[8,4096]{1,0:T(8,128)(2,1)S(1)}, u32[]{:S(2)}, u32[]{:S(2)}) collective-permute-start(bf16[8,4096]{1,0:T(8,128)(2,1)S(1)} %gather_fusion), channel_id=1, source_target_pairs={{0,96},{1,97},{2,98},{3,99},{4,100},{5,101},{6,102},{7,103},{8,104... | collective-permute-start | bytes 196616 | tf_op jit(solution)/shard_map/ppermute | solution.py:40
  32.9 5.8 %collective-permute-start.3 = (bf16[8,4096]{1,0:T(8,128)(2,1)S(1)}, bf16[8,4096]{1,0:T(8,128)(2,1)S(1)}, u32[]{:S(2)}, u32[]{:S(2)}) collective-permute-start(bf16[8,4096]{1,0:T(8,128)(2,1)S(1)} %gather_fusion), channel_id=1, source_target_pairs={{0,64},{1,65},{2,66},{3,67},{4,68},{5,69},{6,70},{7,71},{8,72},{9,... | collective-permute-start | bytes 196616 | tf_op jit(solution)/shard_map/ppermute | solution.py:40
  34.2 5.8 %collective-permute-start.4 = (bf16[8,4096]{1,0:T(8,128)(2,1)S(1)}, bf16[8,4096]{1,0:T(8,128)(2,1)S(1)}, u32[]{:S(2)}, u32[]{:S(2)}) collective-permute-start(bf16[8,4096]{1,0:T(8,128)(2,1)S(1)} %gather_fusion), channel_id=1, source_target_pairs={{0,32},{1,33},{2,34},{3,35},{4,36},{5,37},{6,38},{7,39},{8,40},{9,... | collective-permute-start | bytes 196616 | tf_op jit(solution)/shard_map/ppermute | solution.py:40
  40.0 8.6 %collective-permute-start.5 = (bf16[32,4096]{1,0:T(8,128)(2,1)S(1)}, bf16[32,4096]{1,0:T(8,128)(2,1)S(1)}, u32[]{:S(2)}, u32[]{:S(2)}) collective-permute-start(bf16[32,4096]{1,0:T(8,128)(2,1)S(1)} %constant_dynamic-update-slice_fusion.after), channel_id=1, source_target_pairs={{0,17},{1,0},{2,19},{3,2},{4,21},{5,4},{6,23},{7,6},{8,14},{9,15},... | collective-permute-start | bytes 786440 | tf_op jit(solution)/shard_map/ppermute | solution.py:40
  40.4 8.2 %collective-permute-start.6 = (bf16[32,4096]{1,0:T(8,128)(2,1)S(1)}, bf16[32,4096]{1,0:T(8,128)(2,1)S(1)}, u32[]{:S(2)}, u32[]{:S(2)}) collective-permute-start(bf16[32,4096]{1,0:T(8,128)(2,1)S(1)} %constant_dynamic-update-slice_fusion.after), channel_id=1, source_target_pairs={{0,16},{1,17},{2,18},{3,19},{4,20},{5,21},{6,22},{7,23},{8,12},{9,... | collective-permute-start | bytes 786440 | tf_op jit(solution)/shard_map/ppermute | solution.py:40
  42.7 8.4 %collective-permute-start.7 = (bf16[32,4096]{1,0:T(8,128)(2,1)S(1)}, bf16[32,4096]{1,0:T(8,128)(2,1)S(1)}, u32[]{:S(2)}, u32[]{:S(2)}) collective-permute-start(bf16[32,4096]{1,0:T(8,128)(2,1)S(1)} %constant_dynamic-update-slice_fusion.after), channel_id=1, source_target_pairs={{0,1},{1,16},{2,3},{3,18},{4,5},{5,20},{6,7},{7,22},{8,10},{9,11},... | collective-permute-start | bytes 786440 | tf_op jit(solution)/shard_map/ppermute | solution.py:40
  51.2 15.4 %collective-permute-start.8 = (bf16[128,4096]{1,0:T(8,128)(2,1)S(1)}, bf16[128,4096]{1,0:T(8,128)(2,1)S(1)}, u32[]{:S(2)}, u32[]{:S(2)}) collective-permute-start(bf16[128,4096]{1,0:T(8,128)(2,1)S(1)} %constant_dynamic-update-slice_fusion.4.refs_0_.cand), channel_id=1, source_target_pairs={{0,6},{1,7},{2,0},{3,1},{4,2},{5,3},{6,4},{7,5},{8,25},{9,8},{10,2... | collective-permute-start | bytes 3145736 | tf_op jit(solution)/shard_map/ppermute | solution.py:40
  54.3 16.0 %collective-permute-start.9 = (bf16[128,4096]{1,0:T(8,128)(2,1)S(1)}, bf16[128,4096]{1,0:T(8,128)(2,1)S(1)}, u32[]{:S(2)}, u32[]{:S(2)}) collective-permute-start(bf16[128,4096]{1,0:T(8,128)(2,1)S(1)} %constant_dynamic-update-slice_fusion.4.refs_0_.cand), channel_id=1, source_target_pairs={{0,2},{1,3},{2,4},{3,5},{4,6},{5,7},{6,0},{7,1},{8,9},{9,24},{10,1... | collective-permute-start | bytes 3145736 | tf_op jit(solution)/shard_map/ppermute | solution.py:40
  70.3 11.5 %collective-permute-start.10 = (bf16[64,4096]{1,0:T(8,128)(2,1)S(1)}, bf16[64,4096]{1,0:T(8,128)(2,1)S(1)}, u32[]{:S(2)}, u32[]{:S(2)}) collective-permute-start(bf16[64,4096]{1,0:T(8,128)(2,1)S(1)} %slice.22), channel_id=1, source_target_pairs={{0,6},{1,7},{2,0},{3,1},{4,2},{5,3},{6,4},{7,5},{8,25},{9,8},{10,2... | collective-permute-start | bytes 1572872 | tf_op jit(solution)/shard_map/ppermute | solution.py:40
  70.5 11.4 %collective-permute-start.11 = (bf16[64,4096]{1,0:T(8,128)(2,1)S(1)}, bf16[64,4096]{1,0:T(8,128)(2,1)S(1)}, u32[]{:S(2)}, u32[]{:S(2)}) collective-permute-start(bf16[64,4096]{1,0:T(8,128)(2,1)S(1)} %slice.23), channel_id=1, source_target_pairs={{0,2},{1,3},{2,4},{3,5},{4,6},{5,7},{6,0},{7,1},{8,9},{9,24},{10,1... | collective-permute-start | bytes 1572872 | tf_op jit(solution)/shard_map/ppermute | solution.py:40

commit v5 on v4

--- a/solution.py
+++ b/solution.py
@@ -10,8 +10,6 @@
 AXES = ("slab", "loop")
 RING = 4
 TILE = 512
-LOAD_TILE = 256
-AHEAD = 3
 
 
 def place(index):
@@ -88,46 +86,50 @@
     )(pltpu.with_memory_space_constraint(docs, pltpu.HBM), after)
 
 
-def loading_kernel(cand, docs_hbm, cw, *refs):
-    out_ref, docs, arrived = refs[-3:]
-    steps = docs_hbm.shape[0] // LOAD_TILE
-
-    def copy(i):
-        rows = pl.ds(pl.multiple_of(i * LOAD_TILE, LOAD_TILE), LOAD_TILE)
-        return pltpu.make_async_copy(docs_hbm.at[rows], docs.at[rows], arrived.at[i])
-
-    for i in range(AHEAD):
-        copy(i).start()
+def loading_kernel(count, *refs):
+    pieces = refs[:count]
+    own_docs, sib_hbm, own_cw, sib_cw, out_ref, sib_docs, cand, arrived = refs[count:]
+    copies = [
+        pltpu.make_async_copy(
+            sib_hbm.at[start : start + TILE], sib_docs.at[start : start + TILE], arrived.at[start // TILE]
+        )
+        for start in range(0, sib_docs.shape[0], TILE)
+    ]
+    for copy in copies:
+        copy.start()
+    pack(pieces, cand)
     out_ref[...] = jnp.zeros_like(out_ref)
-
-    def step(i, carry):
-        @pl.when(i + AHEAD < steps)
-        def _():
-            copy(i + AHEAD).start()
-
-        copy(i).wait()
-        start = pl.multiple_of(i * LOAD_TILE, LOAD_TILE)
-        add_terms(cand, docs, cw, out_ref, start, start, LOAD_TILE)
-        return carry
-
-    lax.fori_loop(0, steps, step, 0)
-
-
-def loading_gains(cand, docs, cw, name, held=()):
-    rows, width = cand.shape
+    for start in range(0, own_docs.shape[0], TILE):
+        add_terms(cand, own_docs, own_cw, out_ref, start, start)
+    for copy in copies:
+        copy.wait()
+    for start in range(0, sib_docs.shape[0], TILE):
+        add_terms(cand, sib_docs, sib_cw, out_ref, start, start)
+
+
+def loading_gains(pieces, own_docs, sib_docs, own_cw, sib_cw, name):
+    count = len(pieces)
+    rows, width = sum(p.shape[0] for p in pieces), pieces[0].shape[1]
     in_vmem = pl.BlockSpec(memory_space=pltpu.VMEM)
-    return pl.pallas_call(
-        loading_kernel,
-        in_specs=[in_vmem, pl.BlockSpec(memory_space=pltpu.HBM), in_vmem] + [in_vmem] * len(held),
+    in_hbm = pl.BlockSpec(memory_space=pltpu.HBM)
+    return pl.pallas_call(
+        functools.partial(loading_kernel, count),
+        in_specs=[in_vmem] * (count + 1) + [in_hbm] + [in_vmem] * 2,
         out_specs=[in_vmem] * 2,
-        out_shape=[jax.ShapeDtypeStruct((8, rows), jnp.float32), pltpu.VMEM(docs.shape, docs.dtype)],
-        scratch_shapes=[pltpu.SemaphoreType.DMA((docs.shape[0] // LOAD_TILE,))],
+        out_shape=[
+            jax.ShapeDtypeStruct((8, rows), jnp.float32),
+            pltpu.VMEM(sib_docs.shape, sib_docs.dtype),
+        ],
+        scratch_shapes=[
+            pltpu.VMEM((rows, width), jnp.bfloat16),
+            pltpu.SemaphoreType.DMA((sib_docs.shape[0] // TILE,)),
+        ],
         compiler_params=pltpu.CompilerParams(vmem_limit_bytes=8 * 2**20),
         cost_estimate=pl.CostEstimate(
-            flops=5 * docs.shape[0] * rows * width, bytes_accessed=0, transcendentals=0
+            flops=5 * sib_docs.shape[0] * rows * width, bytes_accessed=0, transcendentals=0
         ),
         name=name,
-    )(cand, pltpu.with_memory_space_constraint(docs, pltpu.HBM), cw, *held)
+    )(*pieces, own_docs, pltpu.with_memory_space_constraint(sib_docs, pltpu.HBM), own_cw, sib_cw)
 
 
 def gain_kernel(count, lows, *refs):
@@ -232,24 +234,25 @@
     column, first, last = ("z", "z"), ("x", "y"), ("y", "x")
     own = jnp.concatenate([own] + [along(own, column, -d) for d in (1, 2, 3)], axis=0)
     beside = [along(own, first, -d) for d in (1, 2, 3)]
-    own_docs = load(docs, own, "load_own")
-    own, own_docs, *beside = lax.optimization_barrier((own, own_docs, *beside))
-    own = jnp.concatenate([own] + beside, axis=0)
-    after, before = along(own, last, -1), along(own, last, -3)
-    ga = gains_of([own], [(own_docs, 0, cw)], "gains_near_own")
-    sib_docs, ga = lax.optimization_barrier((sib_docs, ga))
-    gb, sib_docs = loading_gains(own, sib_docs, sib_cw, "gains_near_sib", held=(own_docs,))
-    after, before, gb = lax.optimization_barrier((after, before, gb))
-    half = own.shape[0] // 2
-    across = [along(after[:half], last, -1), along(before[half:], last, -3)]
+    low = jnp.concatenate([own, beside[0]], axis=0)
+    high = jnp.concatenate(beside[1:], axis=0)
+    after_low, before_high = along(low, last, -1), along(high, last, -3)
+    own_docs = load(docs, low, "load_own")
+    low_again, high_again, own_docs = lax.optimization_barrier((low, high, own_docs))
+    after_high, before_low = along(high_again, last, -1), along(low_again, last, -3)
+    far_low, far_high = along(after_low, last, -1), along(before_high, last, -3)
+    g1, sib_docs = loading_gains(
+        [low_again, high_again, after_low, before_high], own_docs, sib_docs, cw, sib_cw, "gains_near"
+    )
+    after_high, before_low, far_low, far_high, g1 = lax.optimization_barrier(
+        (after_high, before_low, far_low, far_high, g1)
+    )
     parts = [(own_docs, 0, cw), (sib_docs, 0, sib_cw)]
-    g1 = gains_of([after, before], parts, "gains_next")
-    *across, g1 = lax.optimization_barrier((*across, g1))
-    g2 = gains_of(across, parts, "gains_far")
-    ga, gb, g1, g2 = lax.optimization_barrier((ga, gb, g1, g2))
-    g0, g1, g2 = jnp.sum(ga + gb, axis=0), jnp.sum(g1, axis=0), jnp.sum(g2, axis=0)
-    n = own.shape[0]
-    gains = jnp.concatenate([g0, g1[:n], g2, g1[n:]]).reshape(64, share_len)
+    g2 = gains_of([after_high, before_low, far_low, far_high], parts, "gains_far")
+    g1, g2 = lax.optimization_barrier((g1, g2))
+    n = low.shape[0]
+    g1, g2 = jnp.sum(g1, axis=0).reshape(4, n), jnp.sum(g2, axis=0).reshape(4, n)
+    gains = jnp.stack([g1[0], g1[1], g1[2], g2[0], g2[2], g2[3], g2[1], g1[3]]).reshape(64, share_len)
 
     my_z, my_x, my_y = slab >> 2, (slab & 2) + (loop & 1), loop >> 1
     to = jnp.arange(64, dtype=jnp.int32)

time: 107 us -> 103 us (0.963)
  Pallas kernels: 38.7 us -> 28.2 us
  starting transfers between devices: 22.5 us -> 26.6 us
  waiting for transfers between devices: 24.8 us -> 27.9 us
    pallas_call x3 -> x1, Pallas kernels: 22.7 us -> 8.98 us  [gains_of(): pl.pallas_call(functools.partial(gain_kernel, count, tuple((part[1] for p...]
    ppermute x12 -> x14, starting transfers between devices: 11 us -> 15.1 us  [send(): return lax.ppermute(value, AXES, moves(*steps))]
    pallas_call x1, Pallas kernels: 7.39 us -> 10.6 us  [loading_gains(): pl.pallas_call(functools.partial(loading_kernel, count), in_specs=[in_vme...]
    ppermute x12 -> x14, waiting for transfers between devices: 12 us -> 15.1 us  [send(): return lax.ppermute(value, AXES, moves(*steps))]
  transfers between devices with their start and end apart: 14 -> 16, of which waited for: 8 -> 8; matrix products, arithmetic and copies ran while one was open for 3% -> 3% of each run, Pallas kernels for 28% -> 19%
where the time goes in v5:
time: 103 us
  Pallas kernels  28.2 us (27%)
  waiting for transfers between devices  27.9 us (27%)
  starting transfers between devices  26.6 us (26%)
  blocking collectives  14.3 us (14%)
  other arithmetic  3.89 us (4%)
  local copies, waits for them, and re-layouts  1.78 us (2%)
    ppermute x14, starting transfers between devices, send(): return lax.ppermute(value, AXES, moves(*steps))  15.1 us
    ppermute x14, waiting for transfers between devices, send(): return lax.ppermute(value, AXES, moves(*steps))  15.1 us
    all_to_all x1, blocking collectives, body(): lax.all_to_all(terms, AXES, split_axis=0, concat_axis=0, tiled=True, axis...  14.3 us
    pallas_call x1, Pallas kernels, loading_gains(): pl.pallas_call(functools.partial(loading_kernel, count), in_specs=[in_vme...  10.6 us
    pallas_call x1, Pallas kernels, gains_of(): pl.pallas_call(functools.partial(gain_kernel, count, tuple((part[1] for p...  8.98 us
    all_to_all x1, starting transfers between devices, body(): lax.all_to_all(named, 'slab', split_axis=0, concat_axis=0, tiled=True)  7.96 us
    all_to_all x1, waiting for transfers between devices, body(): lax.all_to_all(rows_out, 'slab', split_axis=0, concat_axis=0, tiled=True)  7.94 us
    pallas_call x2, Pallas kernels, load(): pl.pallas_call(load_kernel, in_specs=[pl.BlockSpec(memory_space=pltpu.HBM...  7.44 us
  transfers between devices with their start and end apart: 16, of which 8 were waited for; matrix products, arithmetic and copies ran while one was open for 3% of the time, Pallas kernels for 19%

profile of v5, /device:TPU:0, one launch (start us, length us, event | category | flops | bytes accessed | tf_op | source)
XLA Modules:
  0.0 102.7 jit_solution(11457058825372642669)
XLA Ops:
  1.4 8.0 %all-to-all-start = ((s32[16,8,128]{2,1,0:T(8,128)}), s32[16,8,128]{2,1,0:T(8,128)S(1)}, u32[]{:S(2)}, u32[]{:S(2)}) async-start(s32[16,8,128]{2,1,0:T(8,128)} %broadcast_in_dim.39), calls=%async_computation | async-start | bytes 131072 | tf_op jit(solution)/shard_map/all_to_all | solution.py:220
  10.6 1.5 %load_pool.1.pool = bf16[256,4096]{1,0:T(8,128)(2,1)S(1)} custom-call(bf16[256,4096]{1,0:T(8,128)(2,1)} %bitcast.33, f32[8,2048]{1,0:T(8,128)S(1)} %select_maximum_fusion.after.refs_6_), custom_call_target="tpu_custom_call" | custom-call | bytes 2097152 | tf_op jit(solution)/shard_map/load_pool/pallas_call | solution.py:77
  12.1 4.9 %all-to-all-done.asked = s32[16,8,128]{2,1,0:T(8,128)S(1)} async-done(((s32[16,8,128]{2,1,0:T(8,128)}), s32[16,8,128]{2,1,0:T(8,128)S(1)}, u32[]{:S(2)}, u32[]{:S(2)}) %all-to-all-start) | async-done | bytes 65568 | tf_op jit(solution)/shard_map/all_to_all | solution.py:220
  17.0 1.2 %answer.1 = bf16[16,2,4096]{2,1,0:T(2,128)(2,1)} custom-call(s32[1]{0:T(128)} %bitcast.me, s32[16,8,128]{2,1,0:T(8,128)S(1)} %all-to-all-done.asked, bf16[256,4096]{1,0:T(8,128)(2,1)S(1)} %load_pool.1.pool), custom_call_target="tpu_custom_call" | custom-call | tf_op jit(solution)/shard_map/answer/pallas_call | solution.py:191
  18.2 3.5 %all-to-all-start.1 = ((bf16[16,2,4096]{2,1,0:T(2,128)(2,1)}), bf16[16,2,4096]{2,1,0:T(2,128)(2,1)S(1)}, u32[]{:S(2)}, u32[]{:S(2)}) async-start(bf16[16,2,4096]{2,1,0:T(2,128)(2,1)} %answer.1), calls=%async_computation.1 | async-start | bytes 524288 | tf_op jit(solution)/shard_map/all_to_all | solution.py:223
  21.8 0.9 convert_reduce_fusion
  23.3 7.9 %all-to-all-done.1 = bf16[16,2,4096]{2,1,0:T(2,128)(2,1)S(1)} async-done(((bf16[16,2,4096]{2,1,0:T(2,128)(2,1)}), bf16[16,2,4096]{2,1,0:T(2,128)(2,1)S(1)}, u32[]{:S(2)}, u32[]{:S(2)}) %all-to-all-start.1) | async-done | bytes 262176 | tf_op jit(solution)/shard_map/all_to_all | solution.py:223
  32.0 0.9 collective-permute-start.1
  32.9 1.4 %collective-permute-start.2 = (bf16[8,4096]{1,0:T(8,128)(2,1)S(1)}, bf16[8,4096]{1,0:T(8,128)(2,1)S(1)}, u32[]{:S(2)}, u32[]{:S(2)}) collective-permute-start(bf16[8,4096]{1,0:T(8,128)(2,1)S(1)} %gather_fusion), channel_id=1, source_target_pairs={{0,64},{1,65},{2,66},{3,67},{4,68},{5,69},{6,70},{7,71},{8,72},{9,... | collective-permute-start | bytes 196616 | tf_op jit(solution)/shard_map/ppermute | solution.py:38
  34.5 2.4 %collective-permute-done.1 = bf16[8,4096]{1,0:T(8,128)(2,1)S(1)} collective-permute-done((bf16[8,4096]{1,0:T(8,128)(2,1)S(1)}, bf16[8,4096]{1,0:T(8,128)(2,1)S(1)}, u32[]{:S(2)}, u32[]{:S(2)}) %collective-permute-start.1) | collective-permute-done | bytes 65568 | tf_op jit(solution)/shard_map/ppermute | solution.py:38
  37.0 1.9 %collective-permute-done.2 = bf16[8,4096]{1,0:T(8,128)(2,1)S(1)} collective-permute-done((bf16[8,4096]{1,0:T(8,128)(2,1)S(1)}, bf16[8,4096]{1,0:T(8,128)(2,1)S(1)}, u32[]{:S(2)}, u32[]{:S(2)}) %collective-permute-start.2) | collective-permute-done | bytes 65568 | tf_op jit(solution)/shard_map/ppermute | solution.py:38
  38.8 1.3 %collective-permute-done.3 = bf16[8,4096]{1,0:T(8,128)(2,1)S(1)} collective-permute-done((bf16[8,4096]{1,0:T(8,128)(2,1)S(1)}, bf16[8,4096]{1,0:T(8,128)(2,1)S(1)}, u32[]{:S(2)}, u32[]{:S(2)}) %collective-permute-start.3) | collective-permute-done | bytes 65568 | tf_op jit(solution)/shard_map/ppermute | solution.py:38
  40.9 2.6 %collective-permute-start.4 = (bf16[32,4096]{1,0:T(8,128)(2,1)S(1)}, bf16[32,4096]{1,0:T(8,128)(2,1)S(1)}, u32[]{:S(2)}, u32[]{:S(2)}) collective-permute-start(bf16[32,4096]{1,0:T(8,128)(2,1)S(1)} %get-tuple-element.41), channel_id=1, source_target_pairs={{0,17},{1,0},{2,19},{3,2},{4,21},{5,4},{6,23},{7,6},{8,14},{9,15},... | collective-permute-start | bytes 786440 | tf_op jit(solution)/shard_map/ppermute | solution.py:38
  43.5 4.6 %collective-permute-done.5 = bf16[32,4096]{1,0:T(8,128)(2,1)S(1)} collective-permute-done((bf16[32,4096]{1,0:T(8,128)(2,1)S(1)}, bf16[32,4096]{1,0:T(8,128)(2,1)S(1)}, u32[]{:S(2)}, u32[]{:S(2)}) %collective-permute-start.5) | collective-permute-done | bytes 262176 | tf_op jit(solution)/shard_map/ppermute | solution.py:38
  48.1 3.0 %collective-permute-done.6 = bf16[32,4096]{1,0:T(8,128)(2,1)S(1)} collective-permute-done((bf16[32,4096]{1,0:T(8,128)(2,1)S(1)}, bf16[32,4096]{1,0:T(8,128)(2,1)S(1)}, u32[]{:S(2)}, u32[]{:S(2)}) %collective-permute-start.6) | collective-permute-done | bytes 262176 | tf_op jit(solution)/shard_map/ppermute | solution.py:38
  51.1 1.6 %collective-permute-start.11 = (bf16[64,4096]{1,0:T(8,128)(2,1)S(1)}, bf16[64,4096]{1,0:T(8,128)(2,1)S(1)}, u32[]{:S(2)}, u32[]{:S(2)}) collective-permute-start(bf16[64,4096]{1,0:T(8,128)(2,1)S(1)} %constant_dynamic-update-slice_fusion.9.refs_1_), channel_id=1, source_target_pairs={{0,2},{1,3},{2,4},{3,5},{4,6},{5,7},{6,0},{7,1},{8,9},{9,24},{10,1... | collective-permute-start | bytes 1572872 | tf_op jit(solution)/shard_map/ppermute | solution.py:38
  52.8 1.7 %collective-permute-start.9 = (bf16[64,4096]{1,0:T(8,128)(2,1)S(1)}, bf16[64,4096]{1,0:T(8,128)(2,1)S(1)}, u32[]{:S(2)}, u32[]{:S(2)}) collective-permute-start(bf16[64,4096]{1,0:T(8,128)(2,1)S(1)} %constant_dynamic-update-slice_fusion.4.after.refs_0_), channel_id=1, source_target_pairs={{0,6},{1,7},{2,0},{3,1},{4,2},{5,3},{6,4},{7,5},{8,25},{9,8},{10,2... | collective-permute-start | bytes 1572872 | tf_op jit(solution)/shard_map/ppermute | solution.py:38
  54.6 5.9 %load_own.1.refs_4_ = bf16[2048,4096]{1,0:T(8,128)(2,1)S(1)} custom-call(bf16[2048,4096]{1,0:T(8,128)(2,1)} %bitcast.32, bf16[64,4096]{1,0:T(8,128)(2,1)S(1)} %constant_dynamic-update-slice_fusion.4.after.refs_0_), custom_call_target="tpu_custom_call" | custom-call | bytes 16777216 | tf_op jit(solution)/shard_map/load_own/pallas_call | solution.py:77
  60.5 1.9 %collective-permute-start.7 = (bf16[64,4096]{1,0:T(8,128)(2,1)S(1)}, bf16[64,4096]{1,0:T(8,128)(2,1)S(1)}, u32[]{:S(2)}, u32[]{:S(2)}) collective-permute-start(bf16[64,4096]{1,0:T(8,128)(2,1)S(1)} %constant_dynamic-update-slice_fusion.9.refs_1_), channel_id=1, source_target_pairs={{0,6},{1,7},{2,0},{3,1},{4,2},{5,3},{6,4},{7,5},{8,25},{9,8},{10,2... | collective-permute-start | bytes 1572872 | tf_op jit(solution)/shard_map/ppermute | solution.py:38
  62.9 2.9 %collective-permute-start.10 = (bf16[64,4096]{1,0:T(8,128)(2,1)S(1)}, bf16[64,4096]{1,0:T(8,128)(2,1)S(1)}, u32[]{:S(2)}, u32[]{:S(2)}) collective-permute-start(bf16[64,4096]{1,0:T(8,128)(2,1)S(1)} %collective-permute-done.9.refs_2_), channel_id=1, source_target_pairs={{0,6},{1,7},{2,0},{3,1},{4,2},{5,3},{6,4},{7,5},{8,25},{9,8},{10,2... | collective-permute-start | bytes 1572872 | tf_op jit(solution)/shard_map/ppermute | solution.py:38
  65.9 10.6 %gains_near.1 = (f32[8,256]{1,0:T(8,128)S(1)}, bf16[2048,4096]{1,0:T(8,128)(2,1)S(1)}) custom-call(bf16[64,4096]{1,0:T(8,128)(2,1)S(1)} %constant_dynamic-update-slice_fusion.4.after.refs_0_, bf16[64,4096]{1,0:T(8,128)(2,1)S(1)} %constant_dynamic-update-slice_fusion.9.refs_1_, bf16[64,4096]{1,0:T(8,128)(2,1)S(1)} %collective-permute-done.9.refs_2_, ...), custom_call_target="tpu_custom_call" | custom-call | flops 10737418240 | tf_op jit(solution)/shard_map/gains_near/pallas_call | solution.py:115
  76.4 1.9 %collective-permute-done.12.refs_3_ = bf16[64,4096]{1,0:T(8,128)(2,1)S(1)} collective-permute-done((bf16[64,4096]{1,0:T(8,128)(2,1)S(1)}, bf16[64,4096]{1,0:T(8,128)(2,1)S(1)}, u32[]{:S(2)}, u32[]{:S(2)}) %collective-permute-start.12) | collective-permute-done | bytes 524320 | tf_op jit(solution)/shard_map/ppermute | solution.py:38
  78.4 9.0 %gains_far.1 = f32[8,256]{1,0:T(8,128)S(1)} custom-call(bf16[64,4096]{1,0:T(8,128)(2,1)S(1)} %collective-permute-done.7.refs_0_, bf16[64,4096]{1,0:T(8,128)(2,1)S(1)} %collective-permute-done.8.refs_1_, bf16[64,4096]{1,0:T(8,128)(2,1)S(1)} %collective-permute-done.10.refs_2_, bf16[64,4096]{1,0:T(8,128)(2,1)S(1)} %collective-permute-done.12.refs_3_, ...), custom_call_target="tpu_custom_call" | custom-call | flops 21474836480 | tf_op jit(solution)/shard_map/gains_far/pallas_call | solution.py:155
  87.9 14.3 %all_to_all.19 = f32[64,1,8]{2,1,0:T(1,128)S(1)} all-to-all(f32[64,1,8]{2,1,0:T(1,128)S(1)} %bitcast.34), channel_id=1, replica_groups={{0,1,2,3,4,5,6,7,16,17,18,19,20,21,22,23,32,33,34,35,36,37,38,39,48,49,..., dimensions={0} | all-to-all | bytes 4096 | tf_op jit(solution)/shard_map/all_to_all | solution.py:265
  (42 shorter events, 6.8 us)
Async XLA Ops:
  1.4 15.6 %all-to-all-start = ((s32[16,8,128]{2,1,0:T(8,128)}), s32[16,8,128]{2,1,0:T(8,128)S(1)}, u32[]{:S(2)}, u32[]{:S(2)}) async-start(s32[16,8,128]{2,1,0:T(8,128)} %broadcast_in_dim.39), calls=%async_computation | async-start | bytes 131072 | tf_op jit(solution)/shard_map/all_to_all | solution.py:220
  10.1 13.2 %collective-permute-start = (f32[8,2048]{1,0:T(8,128)S(1)}, f32[8,2048]{1,0:T(8,128)S(1)}, u32[]{:S(2)}, u32[]{:S(2)}) collective-permute-start(f32[8,2048]{1,0:T(8,128)S(1)} %select_maximum_fusion.after.refs_6_), channel_id=1, source_target_pairs={{0,8},{1,9},{2,10},{3,11},{4,12},{5,13},{6,14},{7,15},{8,0},{9,1},... | collective-permute-start | bytes 196616 | tf_op jit(solution)/shard_map/ppermute | solution.py:38
  18.2 13.1 %all-to-all-start.1 = ((bf16[16,2,4096]{2,1,0:T(2,128)(2,1)}), bf16[16,2,4096]{2,1,0:T(2,128)(2,1)S(1)}, u32[]{:S(2)}, u32[]{:S(2)}) async-start(bf16[16,2,4096]{2,1,0:T(2,128)(2,1)} %answer.1), calls=%async_computation.1 | async-start | bytes 524288 | tf_op jit(solution)/shard_map/all_to_all | solution.py:223
  31.3 34.6 %collective-permute-start.13 = (bf16[2048,4096]{1,0:T(8,128)(2,1)}, bf16[2048,4096]{1,0:T(8,128)(2,1)}, u32[]{:S(2)}, u32[]{:S(2)}) collective-permute-start(bf16[2048,4096]{1,0:T(8,128)(2,1)} %bitcast.31), channel_id=1, source_target_pairs={{0,8},{1,9},{2,10},{3,11},{4,12},{5,13},{6,14},{7,15},{8,0},{9,1},... | collective-permute-start | bytes 50331656 | tf_op jit(solution)/shard_map/ppermute | solution.py:38
  32.0 5.0 %collective-permute-start.1 = (bf16[8,4096]{1,0:T(8,128)(2,1)S(1)}, bf16[8,4096]{1,0:T(8,128)(2,1)S(1)}, u32[]{:S(2)}, u32[]{:S(2)}) collective-permute-start(bf16[8,4096]{1,0:T(8,128)(2,1)S(1)} %gather_fusion), channel_id=1, source_target_pairs={{0,96},{1,97},{2,98},{3,99},{4,100},{5,101},{6,102},{7,103},{8,104... | collective-permute-start | bytes 196616 | tf_op jit(solution)/shard_map/ppermute | solution.py:38
  32.9 5.9 %collective-permute-start.2 = (bf16[8,4096]{1,0:T(8,128)(2,1)S(1)}, bf16[8,4096]{1,0:T(8,128)(2,1)S(1)}, u32[]{:S(2)}, u32[]{:S(2)}) collective-permute-start(bf16[8,4096]{1,0:T(8,128)(2,1)S(1)} %gather_fusion), channel_id=1, source_target_pairs={{0,64},{1,65},{2,66},{3,67},{4,68},{5,69},{6,70},{7,71},{8,72},{9,... | collective-permute-start | bytes 196616 | tf_op jit(solution)/shard_map/ppermute | solution.py:38
  34.3 5.8 %collective-permute-start.3 = (bf16[8,4096]{1,0:T(8,128)(2,1)S(1)}, bf16[8,4096]{1,0:T(8,128)(2,1)S(1)}, u32[]{:S(2)}, u32[]{:S(2)}) collective-permute-start(bf16[8,4096]{1,0:T(8,128)(2,1)S(1)} %gather_fusion), channel_id=1, source_target_pairs={{0,32},{1,33},{2,34},{3,35},{4,36},{5,37},{6,38},{7,39},{8,40},{9,... | collective-permute-start | bytes 196616 | tf_op jit(solution)/shard_map/ppermute | solution.py:38
  40.1 8.0 %collective-permute-start.5 = (bf16[32,4096]{1,0:T(8,128)(2,1)S(1)}, bf16[32,4096]{1,0:T(8,128)(2,1)S(1)}, u32[]{:S(2)}, u32[]{:S(2)}) collective-permute-start(bf16[32,4096]{1,0:T(8,128)(2,1)S(1)} %get-tuple-element.41), channel_id=1, source_target_pairs={{0,16},{1,17},{2,18},{3,19},{4,20},{5,21},{6,22},{7,23},{8,12},{9,... | collective-permute-start | bytes 786440 | tf_op jit(solution)/shard_map/ppermute | solution.py:38
  40.9 11.9 %collective-permute-start.4 = (bf16[32,4096]{1,0:T(8,128)(2,1)S(1)}, bf16[32,4096]{1,0:T(8,128)(2,1)S(1)}, u32[]{:S(2)}, u32[]{:S(2)}) collective-permute-start(bf16[32,4096]{1,0:T(8,128)(2,1)S(1)} %get-tuple-element.41), channel_id=1, source_target_pairs={{0,17},{1,0},{2,19},{3,2},{4,21},{5,4},{6,23},{7,6},{8,14},{9,15},... | collective-permute-start | bytes 786440 | tf_op jit(solution)/shard_map/ppermute | solution.py:38
  43.5 7.6 %collective-permute-start.6 = (bf16[32,4096]{1,0:T(8,128)(2,1)S(1)}, bf16[32,4096]{1,0:T(8,128)(2,1)S(1)}, u32[]{:S(2)}, u32[]{:S(2)}) collective-permute-start(bf16[32,4096]{1,0:T(8,128)(2,1)S(1)} %get-tuple-element.41), channel_id=1, source_target_pairs={{0,1},{1,16},{2,3},{3,18},{4,5},{5,20},{6,7},{7,22},{8,10},{9,11},... | collective-permute-start | bytes 786440 | tf_op jit(solution)/shard_map/ppermute | solution.py:38
  51.1 11.5 %collective-permute-start.11 = (bf16[64,4096]{1,0:T(8,128)(2,1)S(1)}, bf16[64,4096]{1,0:T(8,128)(2,1)S(1)}, u32[]{:S(2)}, u32[]{:S(2)}) collective-permute-start(bf16[64,4096]{1,0:T(8,128)(2,1)S(1)} %constant_dynamic-update-slice_fusion.9.refs_1_), channel_id=1, source_target_pairs={{0,2},{1,3},{2,4},{3,5},{4,6},{5,7},{6,0},{7,1},{8,9},{9,24},{10,1... | collective-permute-start | bytes 1572872 | tf_op jit(solution)/shard_map/ppermute | solution.py:38
  52.8 10.2 %collective-permute-start.9 = (bf16[64,4096]{1,0:T(8,128)(2,1)S(1)}, bf16[64,4096]{1,0:T(8,128)(2,1)S(1)}, u32[]{:S(2)}, u32[]{:S(2)}) collective-permute-start(bf16[64,4096]{1,0:T(8,128)(2,1)S(1)} %constant_dynamic-update-slice_fusion.4.after.refs_0_), channel_id=1, source_target_pairs={{0,6},{1,7},{2,0},{3,1},{4,2},{5,3},{6,4},{7,5},{8,25},{9,8},{10,2... | collective-permute-start | bytes 1572872 | tf_op jit(solution)/shard_map/ppermute | solution.py:38
  60.5 15.9 %collective-permute-start.7 = (bf16[64,4096]{1,0:T(8,128)(2,1)S(1)}, bf16[64,4096]{1,0:T(8,128)(2,1)S(1)}, u32[]{:S(2)}, u32[]{:S(2)}) collective-permute-start(bf16[64,4096]{1,0:T(8,128)(2,1)S(1)} %constant_dynamic-update-slice_fusion.9.refs_1_), channel_id=1, source_target_pairs={{0,6},{1,7},{2,0},{3,1},{4,2},{5,3},{6,4},{7,5},{8,25},{9,8},{10,2... | collective-permute-start | bytes 1572872 | tf_op jit(solution)/shard_map/ppermute | solution.py:38
  62.4 14.1 %collective-permute-start.8 = (bf16[64,4096]{1,0:T(8,128)(2,1)S(1)}, bf16[64,4096]{1,0:T(8,128)(2,1)S(1)}, u32[]{:S(2)}, u32[]{:S(2)}) collective-permute-start(bf16[64,4096]{1,0:T(8,128)(2,1)S(1)} %constant_dynamic-update-slice_fusion.4.after.refs_0_), channel_id=1, source_target_pairs={{0,2},{1,3},{2,4},{3,5},{4,6},{5,7},{6,0},{7,1},{8,9},{9,24},{10,1... | collective-permute-start | bytes 1572872 | tf_op jit(solution)/shard_map/ppermute | solution.py:38
  62.6 15.8 %collective-permute-start.12 = (bf16[64,4096]{1,0:T(8,128)(2,1)S(1)}, bf16[64,4096]{1,0:T(8,128)(2,1)S(1)}, u32[]{:S(2)}, u32[]{:S(2)}) collective-permute-start(bf16[64,4096]{1,0:T(8,128)(2,1)S(1)} %collective-permute-done.11.refs_3_), channel_id=1, source_target_pairs={{0,2},{1,3},{2,4},{3,5},{4,6},{5,7},{6,0},{7,1},{8,9},{9,24},{10,1... | collective-permute-start | bytes 1572872 | tf_op jit(solution)/shard_map/ppermute | solution.py:38
  62.9 15.4 %collective-permute-start.10 = (bf16[64,4096]{1,0:T(8,128)(2,1)S(1)}, bf16[64,4096]{1,0:T(8,128)(2,1)S(1)}, u32[]{:S(2)}, u32[]{:S(2)}) collective-permute-start(bf16[64,4096]{1,0:T(8,128)(2,1)S(1)} %collective-permute-done.9.refs_2_), channel_id=1, source_target_pairs={{0,6},{1,7},{2,0},{3,1},{4,2},{5,3},{6,4},{7,5},{8,25},{9,8},{10,2... | collective-permute-start | bytes 1572872 | tf_op jit(solution)/shard_map/ppermute | solution.py:38

commit v6 on v5

--- a/solution.py
+++ b/solution.py
@@ -99,8 +99,10 @@
         copy.start()
     pack(pieces, cand)
     out_ref[...] = jnp.zeros_like(out_ref)
+    rows = cand.shape[0]
+    new = pl.ds(rows // 2, rows // 2)
     for start in range(0, own_docs.shape[0], TILE):
-        add_terms(cand, own_docs, own_cw, out_ref, start, start)
+        add_terms(cand.at[new, :], own_docs, own_cw, out_ref.at[:, new], start, start)
     for copy in copies:
         copy.wait()
     for start in range(0, sib_docs.shape[0], TILE):
@@ -234,11 +236,13 @@
     column, first, last = ("z", "z"), ("x", "y"), ("y", "x")
     own = jnp.concatenate([own] + [along(own, column, -d) for d in (1, 2, 3)], axis=0)
     beside = [along(own, first, -d) for d in (1, 2, 3)]
+    own_docs = load(docs, own, "load_own")
+    own, own_docs, *beside = lax.optimization_barrier((own, own_docs, *beside))
     low = jnp.concatenate([own, beside[0]], axis=0)
     high = jnp.concatenate(beside[1:], axis=0)
     after_low, before_high = along(low, last, -1), along(high, last, -3)
-    own_docs = load(docs, low, "load_own")
-    low_again, high_again, own_docs = lax.optimization_barrier((low, high, own_docs))
+    g0 = gains_of([low, high], [(own_docs, 0, cw)], "gains_own")
+    low_again, high_again, g0 = lax.optimization_barrier((low, high, g0))
     after_high, before_low = along(high_again, last, -1), along(low_again, last, -3)
     far_low, far_high = along(after_low, last, -1), along(before_high, last, -3)
     g1, sib_docs = loading_gains(
@@ -249,8 +253,9 @@
     )
     parts = [(own_docs, 0, cw), (sib_docs, 0, sib_cw)]
     g2 = gains_of([after_high, before_low, far_low, far_high], parts, "gains_far")
-    g1, g2 = lax.optimization_barrier((g1, g2))
+    g0, g1, g2 = lax.optimization_barrier((g0, g1, g2))
     n = low.shape[0]
+    g1 = g1 + jnp.pad(g0, ((0, 0), (0, 2 * n)))
     g1, g2 = jnp.sum(g1, axis=0).reshape(4, n), jnp.sum(g2, axis=0).reshape(4, n)
     gains = jnp.stack([g1[0], g1[1], g1[2], g2[0], g2[2], g2[3], g2[1], g1[3]]).reshape(64, share_len)
 

time: 103 us -> 102 us (level)
  waiting for transfers between devices: 27.9 us -> 22.6 us
  Pallas kernels: 28.2 us -> 33.1 us
    ppermute x14, waiting for transfers between devices: 15.1 us -> 9.81 us  [send(): return lax.ppermute(value, AXES, moves(*steps))]
    pallas_call x1 -> x2, Pallas kernels: 8.98 us -> 13.7 us  [gains_of(): pl.pallas_call(functools.partial(gain_kernel, count, tuple((part[1] for p...]
  transfers between devices with their start and end apart: 16 -> 16, of which waited for: 8 -> 9; matrix products, arithmetic and copies ran while one was open for 3% -> 3% of each run, Pallas kernels for 19% -> 24%
where the time goes in v6:
time: 102 us
  Pallas kernels  33.1 us (32%)
  starting transfers between devices  25.8 us (25%)
  waiting for transfers between devices  22.6 us (22%)
  blocking collectives  14.2 us (14%)
  other arithmetic  3.88 us (4%)
  local copies, waits for them, and re-layouts  1.79 us (2%)
    ppermute x14, starting transfers between devices, send(): return lax.ppermute(value, AXES, moves(*steps))  14.3 us
    all_to_all x1, blocking collectives, body(): lax.all_to_all(terms, AXES, split_axis=0, concat_axis=0, tiled=True, axis...  14.2 us
    pallas_call x2, Pallas kernels, gains_of(): pl.pallas_call(functools.partial(gain_kernel, count, tuple((part[1] for p...  13.7 us
    pallas_call x1, Pallas kernels, loading_gains(): pl.pallas_call(functools.partial(loading_kernel, count), in_specs=[in_vme...  10.8 us
    ppermute x14, waiting for transfers between devices, send(): return lax.ppermute(value, AXES, moves(*steps))  9.81 us
    all_to_all x1, starting transfers between devices, body(): lax.all_to_all(named, 'slab', split_axis=0, concat_axis=0, tiled=True)  7.96 us
    all_to_all x1, waiting for transfers between devices, body(): lax.all_to_all(rows_out, 'slab', split_axis=0, concat_axis=0, tiled=True)  7.94 us
    pallas_call x2, Pallas kernels, load(): pl.pallas_call(load_kernel, in_specs=[pl.BlockSpec(memory_space=pltpu.HBM...  7.44 us
  transfers between devices with their start and end apart: 16, of which 9 were waited for; matrix products, arithmetic and copies ran while one was open for 3% of the time, Pallas kernels for 24%

profile of v6, /device:TPU:0, one launch (start us, length us, event | category | flops | bytes accessed | tf_op | source)
XLA Modules:
  0.0 101.5 jit_solution(16314811383597445143)
XLA Ops:
  1.4 8.0 %all-to-all-start = ((s32[16,8,128]{2,1,0:T(8,128)}), s32[16,8,128]{2,1,0:T(8,128)S(1)}, u32[]{:S(2)}, u32[]{:S(2)}) async-start(s32[16,8,128]{2,1,0:T(8,128)} %broadcast_in_dim.39), calls=%async_computation | async-start | bytes 131072 | tf_op jit(solution)/shard_map/all_to_all | solution.py:222
  10.6 1.5 %load_pool.1.pool = bf16[256,4096]{1,0:T(8,128)(2,1)S(1)} custom-call(bf16[256,4096]{1,0:T(8,128)(2,1)} %bitcast.33, f32[8,2048]{1,0:T(8,128)S(1)} %select_maximum_fusion.after.refs_3_.refs_6_), custom_call_target="tpu_custom_call" | custom-call | bytes 2097152 | tf_op jit(solution)/shard_map/load_pool/pallas_call | solution.py:77
  12.1 4.9 %all-to-all-done.asked = s32[16,8,128]{2,1,0:T(8,128)S(1)} async-done(((s32[16,8,128]{2,1,0:T(8,128)}), s32[16,8,128]{2,1,0:T(8,128)S(1)}, u32[]{:S(2)}, u32[]{:S(2)}) %all-to-all-start) | async-done | bytes 65568 | tf_op jit(solution)/shard_map/all_to_all | solution.py:222
  17.0 1.2 %answer.1 = bf16[16,2,4096]{2,1,0:T(2,128)(2,1)} custom-call(s32[1]{0:T(128)} %bitcast.me, s32[16,8,128]{2,1,0:T(8,128)S(1)} %all-to-all-done.asked, bf16[256,4096]{1,0:T(8,128)(2,1)S(1)} %load_pool.1.pool), custom_call_target="tpu_custom_call" | custom-call | tf_op jit(solution)/shard_map/answer/pallas_call | solution.py:193
  18.2 3.5 %all-to-all-start.1 = ((bf16[16,2,4096]{2,1,0:T(2,128)(2,1)}), bf16[16,2,4096]{2,1,0:T(2,128)(2,1)S(1)}, u32[]{:S(2)}, u32[]{:S(2)}) async-start(bf16[16,2,4096]{2,1,0:T(2,128)(2,1)} %answer.1), calls=%async_computation.1 | async-start | bytes 524288 | tf_op jit(solution)/shard_map/all_to_all | solution.py:225
  21.8 0.9 convert_reduce_fusion
  23.3 7.9 %all-to-all-done.1 = bf16[16,2,4096]{2,1,0:T(2,128)(2,1)S(1)} async-done(((bf16[16,2,4096]{2,1,0:T(2,128)(2,1)}), bf16[16,2,4096]{2,1,0:T(2,128)(2,1)S(1)}, u32[]{:S(2)}, u32[]{:S(2)}) %all-to-all-start.1) | async-done | bytes 262176 | tf_op jit(solution)/shard_map/all_to_all | solution.py:225
  32.0 0.9 collective-permute-start.1
  32.9 1.3 %collective-permute-start.2 = (bf16[8,4096]{1,0:T(8,128)(2,1)S(1)}, bf16[8,4096]{1,0:T(8,128)(2,1)S(1)}, u32[]{:S(2)}, u32[]{:S(2)}) collective-permute-start(bf16[8,4096]{1,0:T(8,128)(2,1)S(1)} %gather_fusion), channel_id=1, source_target_pairs={{0,64},{1,65},{2,66},{3,67},{4,68},{5,69},{6,70},{7,71},{8,72},{9,... | collective-permute-start | bytes 196616 | tf_op jit(solution)/shard_map/ppermute | solution.py:38
  34.4 2.5 %collective-permute-done.1 = bf16[8,4096]{1,0:T(8,128)(2,1)S(1)} collective-permute-done((bf16[8,4096]{1,0:T(8,128)(2,1)S(1)}, bf16[8,4096]{1,0:T(8,128)(2,1)S(1)}, u32[]{:S(2)}, u32[]{:S(2)}) %collective-permute-start.1) | collective-permute-done | bytes 65568 | tf_op jit(solution)/shard_map/ppermute | solution.py:38
  37.0 1.8 %collective-permute-done.2 = bf16[8,4096]{1,0:T(8,128)(2,1)S(1)} collective-permute-done((bf16[8,4096]{1,0:T(8,128)(2,1)S(1)}, bf16[8,4096]{1,0:T(8,128)(2,1)S(1)}, u32[]{:S(2)}, u32[]{:S(2)}) %collective-permute-start.2) | collective-permute-done | bytes 65568 | tf_op jit(solution)/shard_map/ppermute | solution.py:38
  38.7 1.3 %collective-permute-done.3 = bf16[8,4096]{1,0:T(8,128)(2,1)S(1)} collective-permute-done((bf16[8,4096]{1,0:T(8,128)(2,1)S(1)}, bf16[8,4096]{1,0:T(8,128)(2,1)S(1)}, u32[]{:S(2)}, u32[]{:S(2)}) %collective-permute-start.3) | collective-permute-done | bytes 65568 | tf_op jit(solution)/shard_map/ppermute | solution.py:38
  40.4 2.3 %collective-permute-start.5 = (bf16[32,4096]{1,0:T(8,128)(2,1)S(1)}, bf16[32,4096]{1,0:T(8,128)(2,1)S(1)}, u32[]{:S(2)}, u32[]{:S(2)}) collective-permute-start(bf16[32,4096]{1,0:T(8,128)(2,1)S(1)} %constant_dynamic-update-slice_fusion.after), channel_id=1, source_target_pairs={{0,16},{1,17},{2,18},{3,19},{4,20},{5,21},{6,22},{7,23},{8,12},{9,... | collective-permute-start | bytes 786440 | tf_op jit(solution)/shard_map/ppermute | solution.py:38
  42.7 5.9 %load_own.1.refs_2_.refs_4_ = bf16[2048,4096]{1,0:T(8,128)(2,1)S(1)} custom-call(bf16[2048,4096]{1,0:T(8,128)(2,1)} %bitcast.32, bf16[32,4096]{1,0:T(8,128)(2,1)S(1)} %constant_dynamic-update-slice_fusion.after), custom_call_target="tpu_custom_call" | custom-call | bytes 16777216 | tf_op jit(solution)/shard_map/load_own/pallas_call | solution.py:77
  48.6 2.5 %collective-permute-done.6 = bf16[32,4096]{1,0:T(8,128)(2,1)S(1)} collective-permute-done((bf16[32,4096]{1,0:T(8,128)(2,1)S(1)}, bf16[32,4096]{1,0:T(8,128)(2,1)S(1)}, u32[]{:S(2)}, u32[]{:S(2)}) %collective-permute-start.6) | collective-permute-done | bytes 262176 | tf_op jit(solution)/shard_map/ppermute | solution.py:38
  51.2 1.6 %collective-permute-start.11 = (bf16[64,4096]{1,0:T(8,128)(2,1)S(1)}, bf16[64,4096]{1,0:T(8,128)(2,1)S(1)}, u32[]{:S(2)}, u32[]{:S(2)}) collective-permute-start(bf16[64,4096]{1,0:T(8,128)(2,1)S(1)} %constant_dynamic-update-slice_fusion.6.refs_1_), channel_id=1, source_target_pairs={{0,2},{1,3},{2,4},{3,5},{4,6},{5,7},{6,0},{7,1},{8,9},{9,24},{10,1... | collective-permute-start | bytes 1572872 | tf_op jit(solution)/shard_map/ppermute | solution.py:38
  52.8 1.7 %collective-permute-start.9 = (bf16[64,4096]{1,0:T(8,128)(2,1)S(1)}, bf16[64,4096]{1,0:T(8,128)(2,1)S(1)}, u32[]{:S(2)}, u32[]{:S(2)}) collective-permute-start(bf16[64,4096]{1,0:T(8,128)(2,1)S(1)} %constant_dynamic-update-slice_fusion.4.refs_0_), channel_id=1, source_target_pairs={{0,6},{1,7},{2,0},{3,1},{4,2},{5,3},{6,4},{7,5},{8,25},{9,8},{10,2... | collective-permute-start | bytes 1572872 | tf_op jit(solution)/shard_map/ppermute | solution.py:38
  54.7 4.6 %gains_own.1 = f32[8,128]{1,0:T(8,128)S(1)} custom-call(bf16[64,4096]{1,0:T(8,128)(2,1)S(1)} %constant_dynamic-update-slice_fusion.4.refs_0_, bf16[64,4096]{1,0:T(8,128)(2,1)S(1)} %constant_dynamic-update-slice_fusion.6.refs_1_, bf16[2048,4096]{1,0:T(8,128)(2,1)S(1)} %load_own.1.refs_2_.refs_4_, f32[8,2048]{1,0:T(8,128)S(1)} %select_maximum_fusion.after.refs_3_.refs_6_), custom_call_target="tpu_custom_call" | custom-call | flops 5368709120 | tf_op jit(solution)/shard_map/gains_own/pallas_call | solution.py:157
  59.3 1.9 %collective-permute-start.7 = (bf16[64,4096]{1,0:T(8,128)(2,1)S(1)}, bf16[64,4096]{1,0:T(8,128)(2,1)S(1)}, u32[]{:S(2)}, u32[]{:S(2)}) collective-permute-start(bf16[64,4096]{1,0:T(8,128)(2,1)S(1)} %constant_dynamic-update-slice_fusion.6.refs_1_), channel_id=1, source_target_pairs={{0,6},{1,7},{2,0},{3,1},{4,2},{5,3},{6,4},{7,5},{8,25},{9,8},{10,2... | collective-permute-start | bytes 1572872 | tf_op jit(solution)/shard_map/ppermute | solution.py:38
  62.1 2.9 %collective-permute-start.10 = (bf16[64,4096]{1,0:T(8,128)(2,1)S(1)}, bf16[64,4096]{1,0:T(8,128)(2,1)S(1)}, u32[]{:S(2)}, u32[]{:S(2)}) collective-permute-start(bf16[64,4096]{1,0:T(8,128)(2,1)S(1)} %collective-permute-done.9.refs_2_), channel_id=1, source_target_pairs={{0,6},{1,7},{2,0},{3,1},{4,2},{5,3},{6,4},{7,5},{8,25},{9,8},{10,2... | collective-permute-start | bytes 1572872 | tf_op jit(solution)/shard_map/ppermute | solution.py:38
  65.0 10.8 %gains_near.1 = (f32[8,256]{1,0:T(8,128)S(1)}, bf16[2048,4096]{1,0:T(8,128)(2,1)S(1)}) custom-call(bf16[64,4096]{1,0:T(8,128)(2,1)S(1)} %constant_dynamic-update-slice_fusion.4.refs_0_, bf16[64,4096]{1,0:T(8,128)(2,1)S(1)} %constant_dynamic-update-slice_fusion.6.refs_1_, bf16[64,4096]{1,0:T(8,128)(2,1)S(1)} %collective-permute-done.9.refs_2_, ...), custom_call_target="tpu_custom_call" | custom-call | flops 10737418240 | tf_op jit(solution)/shard_map/gains_near/pallas_call | solution.py:117
  75.8 1.4 %collective-permute-done.12.refs_3_ = bf16[64,4096]{1,0:T(8,128)(2,1)S(1)} collective-permute-done((bf16[64,4096]{1,0:T(8,128)(2,1)S(1)}, bf16[64,4096]{1,0:T(8,128)(2,1)S(1)}, u32[]{:S(2)}, u32[]{:S(2)}) %collective-permute-start.12) | collective-permute-done | bytes 524320 | tf_op jit(solution)/shard_map/ppermute | solution.py:38
  77.2 9.1 %gains_far.1 = f32[8,256]{1,0:T(8,128)S(1)} custom-call(bf16[64,4096]{1,0:T(8,128)(2,1)S(1)} %collective-permute-done.7.refs_0_, bf16[64,4096]{1,0:T(8,128)(2,1)S(1)} %collective-permute-done.8.refs_1_, bf16[64,4096]{1,0:T(8,128)(2,1)S(1)} %collective-permute-done.10.refs_2_, bf16[64,4096]{1,0:T(8,128)(2,1)S(1)} %collective-permute-done.12.refs_3_, ...), custom_call_target="tpu_custom_call" | custom-call | flops 21474836480 | tf_op jit(solution)/shard_map/gains_far/pallas_call | solution.py:157
  86.8 14.2 %all_to_all.19 = f32[64,1,8]{2,1,0:T(1,128)S(1)} all-to-all(f32[64,1,8]{2,1,0:T(1,128)S(1)} %bitcast.34), channel_id=1, replica_groups={{0,1,2,3,4,5,6,7,16,17,18,19,20,21,22,23,32,33,34,35,36,37,38,39,48,49,..., dimensions={0} | all-to-all | bytes 4096 | tf_op jit(solution)/shard_map/all_to_all | solution.py:270
  (44 shorter events, 6.8 us)
Async XLA Ops:
  1.4 15.6 %all-to-all-start = ((s32[16,8,128]{2,1,0:T(8,128)}), s32[16,8,128]{2,1,0:T(8,128)S(1)}, u32[]{:S(2)}, u32[]{:S(2)}) async-start(s32[16,8,128]{2,1,0:T(8,128)} %broadcast_in_dim.39), calls=%async_computation | async-start | bytes 131072 | tf_op jit(solution)/shard_map/all_to_all | solution.py:222
  10.1 13.2 %collective-permute-start = (f32[8,2048]{1,0:T(8,128)S(1)}, f32[8,2048]{1,0:T(8,128)S(1)}, u32[]{:S(2)}, u32[]{:S(2)}) collective-permute-start(f32[8,2048]{1,0:T(8,128)S(1)} %select_maximum_fusion.after.refs_3_.refs_6_), channel_id=1, source_target_pairs={{0,8},{1,9},{2,10},{3,11},{4,12},{5,13},{6,14},{7,15},{8,0},{9,1},... | collective-permute-start | bytes 196616 | tf_op jit(solution)/shard_map/ppermute | solution.py:38
  18.2 13.1 %all-to-all-start.1 = ((bf16[16,2,4096]{2,1,0:T(2,128)(2,1)}), bf16[16,2,4096]{2,1,0:T(2,128)(2,1)S(1)}, u32[]{:S(2)}, u32[]{:S(2)}) async-start(bf16[16,2,4096]{2,1,0:T(2,128)(2,1)} %answer.1), calls=%async_computation.1 | async-start | bytes 524288 | tf_op jit(solution)/shard_map/all_to_all | solution.py:225
  31.3 33.7 %collective-permute-start.13 = (bf16[2048,4096]{1,0:T(8,128)(2,1)}, bf16[2048,4096]{1,0:T(8,128)(2,1)}, u32[]{:S(2)}, u32[]{:S(2)}) collective-permute-start(bf16[2048,4096]{1,0:T(8,128)(2,1)} %bitcast.31), channel_id=1, source_target_pairs={{0,8},{1,9},{2,10},{3,11},{4,12},{5,13},{6,14},{7,15},{8,0},{9,1},... | collective-permute-start | bytes 50331656 | tf_op jit(solution)/shard_map/ppermute | solution.py:38
  32.0 5.0 %collective-permute-start.1 = (bf16[8,4096]{1,0:T(8,128)(2,1)S(1)}, bf16[8,4096]{1,0:T(8,128)(2,1)S(1)}, u32[]{:S(2)}, u32[]{:S(2)}) collective-permute-start(bf16[8,4096]{1,0:T(8,128)(2,1)S(1)} %gather_fusion), channel_id=1, source_target_pairs={{0,96},{1,97},{2,98},{3,99},{4,100},{5,101},{6,102},{7,103},{8,104... | collective-permute-start | bytes 196616 | tf_op jit(solution)/shard_map/ppermute | solution.py:38
  32.9 5.8 %collective-permute-start.2 = (bf16[8,4096]{1,0:T(8,128)(2,1)S(1)}, bf16[8,4096]{1,0:T(8,128)(2,1)S(1)}, u32[]{:S(2)}, u32[]{:S(2)}) collective-permute-start(bf16[8,4096]{1,0:T(8,128)(2,1)S(1)} %gather_fusion), channel_id=1, source_target_pairs={{0,64},{1,65},{2,66},{3,67},{4,68},{5,69},{6,70},{7,71},{8,72},{9,... | collective-permute-start | bytes 196616 | tf_op jit(solution)/shard_map/ppermute | solution.py:38
  34.2 5.8 %collective-permute-start.3 = (bf16[8,4096]{1,0:T(8,128)(2,1)S(1)}, bf16[8,4096]{1,0:T(8,128)(2,1)S(1)}, u32[]{:S(2)}, u32[]{:S(2)}) collective-permute-start(bf16[8,4096]{1,0:T(8,128)(2,1)S(1)} %gather_fusion), channel_id=1, source_target_pairs={{0,32},{1,33},{2,34},{3,35},{4,36},{5,37},{6,38},{7,39},{8,40},{9,... | collective-permute-start | bytes 196616 | tf_op jit(solution)/shard_map/ppermute | solution.py:38
  40.0 8.6 %collective-permute-start.4 = (bf16[32,4096]{1,0:T(8,128)(2,1)S(1)}, bf16[32,4096]{1,0:T(8,128)(2,1)S(1)}, u32[]{:S(2)}, u32[]{:S(2)}) collective-permute-start(bf16[32,4096]{1,0:T(8,128)(2,1)S(1)} %constant_dynamic-update-slice_fusion.after), channel_id=1, source_target_pairs={{0,17},{1,0},{2,19},{3,2},{4,21},{5,4},{6,23},{7,6},{8,14},{9,15},... | collective-permute-start | bytes 786440 | tf_op jit(solution)/shard_map/ppermute | solution.py:38
  40.4 8.2 %collective-permute-start.5 = (bf16[32,4096]{1,0:T(8,128)(2,1)S(1)}, bf16[32,4096]{1,0:T(8,128)(2,1)S(1)}, u32[]{:S(2)}, u32[]{:S(2)}) collective-permute-start(bf16[32,4096]{1,0:T(8,128)(2,1)S(1)} %constant_dynamic-update-slice_fusion.after), channel_id=1, source_target_pairs={{0,16},{1,17},{2,18},{3,19},{4,20},{5,21},{6,22},{7,23},{8,12},{9,... | collective-permute-start | bytes 786440 | tf_op jit(solution)/shard_map/ppermute | solution.py:38
  42.7 8.4 %collective-permute-start.6 = (bf16[32,4096]{1,0:T(8,128)(2,1)S(1)}, bf16[32,4096]{1,0:T(8,128)(2,1)S(1)}, u32[]{:S(2)}, u32[]{:S(2)}) collective-permute-start(bf16[32,4096]{1,0:T(8,128)(2,1)S(1)} %constant_dynamic-update-slice_fusion.after), channel_id=1, source_target_pairs={{0,1},{1,16},{2,3},{3,18},{4,5},{5,20},{6,7},{7,22},{8,10},{9,11},... | collective-permute-start | bytes 786440 | tf_op jit(solution)/shard_map/ppermute | solution.py:38
  51.2 10.5 %collective-permute-start.11 = (bf16[64,4096]{1,0:T(8,128)(2,1)S(1)}, bf16[64,4096]{1,0:T(8,128)(2,1)S(1)}, u32[]{:S(2)}, u32[]{:S(2)}) collective-permute-start(bf16[64,4096]{1,0:T(8,128)(2,1)S(1)} %constant_dynamic-update-slice_fusion.6.refs_1_), channel_id=1, source_target_pairs={{0,2},{1,3},{2,4},{3,5},{4,6},{5,7},{6,0},{7,1},{8,9},{9,24},{10,1... | collective-permute-start | bytes 1572872 | tf_op jit(solution)/shard_map/ppermute | solution.py:38
  52.8 9.2 %collective-permute-start.9 = (bf16[64,4096]{1,0:T(8,128)(2,1)S(1)}, bf16[64,4096]{1,0:T(8,128)(2,1)S(1)}, u32[]{:S(2)}, u32[]{:S(2)}) collective-permute-start(bf16[64,4096]{1,0:T(8,128)(2,1)S(1)} %constant_dynamic-update-slice_fusion.4.refs_0_), channel_id=1, source_target_pairs={{0,6},{1,7},{2,0},{3,1},{4,2},{5,3},{6,4},{7,5},{8,25},{9,8},{10,2... | collective-permute-start | bytes 1572872 | tf_op jit(solution)/shard_map/ppermute | solution.py:38
  59.3 16.5 %collective-permute-start.7 = (bf16[64,4096]{1,0:T(8,128)(2,1)S(1)}, bf16[64,4096]{1,0:T(8,128)(2,1)S(1)}, u32[]{:S(2)}, u32[]{:S(2)}) collective-permute-start(bf16[64,4096]{1,0:T(8,128)(2,1)S(1)} %constant_dynamic-update-slice_fusion.6.refs_1_), channel_id=1, source_target_pairs={{0,6},{1,7},{2,0},{3,1},{4,2},{5,3},{6,4},{7,5},{8,25},{9,8},{10,2... | collective-permute-start | bytes 1572872 | tf_op jit(solution)/shard_map/ppermute | solution.py:38
  61.1 14.6 %collective-permute-start.8 = (bf16[64,4096]{1,0:T(8,128)(2,1)S(1)}, bf16[64,4096]{1,0:T(8,128)(2,1)S(1)}, u32[]{:S(2)}, u32[]{:S(2)}) collective-permute-start(bf16[64,4096]{1,0:T(8,128)(2,1)S(1)} %constant_dynamic-update-slice_fusion.4.refs_0_), channel_id=1, source_target_pairs={{0,2},{1,3},{2,4},{3,5},{4,6},{5,7},{6,0},{7,1},{8,9},{9,24},{10,1... | collective-permute-start | bytes 1572872 | tf_op jit(solution)/shard_map/ppermute | solution.py:38
  61.6 15.5 %collective-permute-start.12 = (bf16[64,4096]{1,0:T(8,128)(2,1)S(1)}, bf16[64,4096]{1,0:T(8,128)(2,1)S(1)}, u32[]{:S(2)}, u32[]{:S(2)}) collective-permute-start(bf16[64,4096]{1,0:T(8,128)(2,1)S(1)} %collective-permute-done.11.refs_3_), channel_id=1, source_target_pairs={{0,2},{1,3},{2,4},{3,5},{4,6},{5,7},{6,0},{7,1},{8,9},{9,24},{10,1... | collective-permute-start | bytes 1572872 | tf_op jit(solution)/shard_map/ppermute | solution.py:38
  62.1 15.1 %collective-permute-start.10 = (bf16[64,4096]{1,0:T(8,128)(2,1)S(1)}, bf16[64,4096]{1,0:T(8,128)(2,1)S(1)}, u32[]{:S(2)}, u32[]{:S(2)}) collective-permute-start(bf16[64,4096]{1,0:T(8,128)(2,1)S(1)} %collective-permute-done.9.refs_2_), channel_id=1, source_target_pairs={{0,6},{1,7},{2,0},{3,1},{4,2},{5,3},{6,4},{7,5},{8,25},{9,8},{10,2... | collective-permute-start | bytes 1572872 | tf_op jit(solution)/shard_map/ppermute | solution.py:38
